TPU v7x, 32 devices: a whole 2x2x4 slice. The times are simulated.
32 devices in a mesh: seq: 8 (over y, x, core), mp: 4 (over z).
Axes of the slice: x: 2, y: 2, z: 4, core: 2. Of those that a mesh axis runs over, the one named last changes fastest.
Arguments:
- queries: bfloat16 [1024, 2048], P('seq', 'mp'), may hold values from -2 to 2
- keys: bfloat16 [1024, 2048], P('seq', 'mp'), may hold values from -2 to 2
- values: bfloat16 [1024, 2048], P('seq', 'mp'), may hold values from -6 to 6
- log_decay: float32 [16, 1024], P('mp', 'seq'), may hold values from -1.2 to 0
- residual: bfloat16 [1024, 6144], P(('seq', 'mp')), may hold values from -6 to 6
- out_weight: bfloat16 [2048, 6144], P('mp', 'seq'), may hold values from -0.125 to 0.125
- gate_weight: bfloat16 [8, 6144, 2304], P('seq', None, 'mp'), may hold values from -0.078125 to 0.078125
- up_weight: bfloat16 [8, 6144, 2304], P('seq', None, 'mp'), may hold values from -0.078125 to 0.078125
- down_weight: bfloat16 [8, 2304, 6144], P('seq', 'mp'), may hold values from -0.09375 to 0.09375
- expert_ids: int32 [1024, 2], P(('seq', 'mp')), may hold values from 0 to 3, all different within a row; in each aligned block of 32 rows (0 to 31, 32 to 63, ...) at most 24 rows name the same one
- route_weights: float32 [1024, 2], P(('seq', 'mp')), may hold values from 0.2 to 1
Outputs:
- output: bfloat16 [1024, 6144], P(('seq', 'mp'))
Inputs may be any that keep to these rules, and one draw needn't show every extreme that they name: `expert_ids`: the 2 experts of a token differ. Among the 32 tokens of one device (aligned blocks of rows in token order) no expert is named more than 24 times, a bound that some block reaches.
All inputs are finite; a program needn't handle non-finite values.
Results may differ from a plain program's by a relative error of at most 0.015.
Values may be sent and summed in bfloat16 or wider, within the bound.
No kernel may reach another device: no remote copies, remote signals or barrier semaphores. Data moves between devices by JAX's collectives and lax.ppermute only.
A program may use at most 128 MiB of HBM per device.

v0:
```python
import jax
import jax.numpy as jnp
from jax import lax
from jax.sharding import PartitionSpec as P

TOP = 2
PAIR = 2


def per_device(
    queries,
    keys,
    values,
    log_decay,
    residual,
    out_weight,
    gate_weight,
    up_weight,
    down_weight,
    expert_ids,
    route_weights,
):
    seq_count = lax.axis_size("seq")
    span_len = queries.shape[0]
    head_count = log_decay.shape[0]
    head_size = queries.shape[1] // head_count
    query_heads = queries.reshape(span_len, head_count, head_size)
    key_heads = keys.reshape(span_len, head_count, head_size)
    value_heads = values.reshape(span_len, head_count, head_size)
    cumulative = jnp.cumsum(log_decay, axis=1)
    positions = jnp.arange(span_len)
    causal = (positions[:, None] >= positions[None, :])[None]
    spread_log = cumulative[:, :, None] - cumulative[:, None, :]
    weight = jnp.where(causal, jnp.exp(jnp.where(causal, spread_log, 0.0)), 0.0)
    raw_scores = jnp.einsum(
        "thd,shd->hts", query_heads, key_heads, preferred_element_type=jnp.float32
    )
    local_scores = (raw_scores * weight).astype(jnp.bfloat16)
    local_part = jnp.einsum(
        "hts,shd->thd", local_scores, value_heads, preferred_element_type=jnp.float32
    )
    span_total = cumulative[:, -1]
    key_scale = jnp.exp(span_total[:, None] - cumulative)
    weighted_keys = (key_scale.T[:, :, None] * key_heads.astype(jnp.float32)).astype(jnp.bfloat16)
    span_state = jnp.einsum(
        "thd,the->hde", weighted_keys, value_heads, preferred_element_type=jnp.float32
    ).astype(jnp.bfloat16)
    decays = lax.all_gather(span_total[None, :], "seq", axis=0, tiled=True)
    running = jnp.cumsum(decays, axis=0)
    my_index = lax.axis_index("seq")
    before = lax.dynamic_index_in_dim(running, jnp.maximum(my_index - 1, 0), 0, keepdims=False)
    shard_piece = lax.all_gather(span_state[None], "seq", axis=0, tiled=True)
    row_count = shard_piece.shape[0]
    source = jnp.arange(row_count)
    earlier_mask = (source < my_index)[:, None]
    factor = jnp.where(
        earlier_mask, jnp.exp(jnp.where(earlier_mask, before[None, :] - running, 0.0)), 0.0
    )
    prefix = jnp.einsum(
        "nh,nhde->hde", factor, shard_piece.astype(jnp.float32), precision=lax.Precision.HIGHEST
    )
    prefix_low = prefix.astype(jnp.bfloat16)
    weighted_queries = (jnp.exp(cumulative).T[:, :, None] * query_heads.astype(jnp.float32)).astype(
        jnp.bfloat16
    )
    carried_part = jnp.einsum(
        "thd,hde->the", weighted_queries, prefix_low, preferred_element_type=jnp.float32
    )
    mixed_heads = local_part + carried_part
    normed = (
        mixed_heads * lax.rsqrt(jnp.mean(mixed_heads * mixed_heads, axis=-1, keepdims=True) + 1e-06)
    ).astype(jnp.bfloat16)
    normed = normed.reshape(span_len, head_count * head_size)
    partial_out = jnp.dot(
        normed,
        lax.all_gather(out_weight, "seq", axis=1, tiled=True),
        preferred_element_type=jnp.float32,
    )
    attn_out = lax.psum_scatter(
        partial_out.astype(jnp.bfloat16), "mp", scatter_dimension=0, tiled=True
    ).astype(jnp.float32)
    hidden_state = (residual.astype(jnp.float32) + attn_out).astype(jnp.bfloat16)
    hidden_wide = hidden_state.astype(jnp.float32)
    moe_input = (
        hidden_wide * lax.rsqrt(jnp.mean(hidden_wide * hidden_wide, axis=-1, keepdims=True) + 1e-06)
    ).astype(jnp.bfloat16)
    model_width = residual.shape[1]
    experts = seq_count // PAIR
    tok_rows = residual.shape[0]
    capacity = max(2, tok_rows * TOP * 3 // (2 * experts))
    assign_count = tok_rows * TOP
    flat_ids = expert_ids.reshape(-1)
    expert_hot = (flat_ids[:, None] == jnp.arange(experts)[None, :]).astype(jnp.int32)
    slot_rank = jnp.sum((jnp.cumsum(expert_hot, axis=0) - expert_hot) * expert_hot, axis=1)
    target = flat_ids * capacity + slot_rank
    slot_hot = (target[:, None] == jnp.arange(experts * capacity)[None, :]).astype(jnp.float32)
    owner_hot = (
        (jnp.arange(assign_count) // TOP)[:, None] == jnp.arange(tok_rows)[None, :]
    ).astype(jnp.float32)
    dispatch_map = jnp.einsum("as,at->st", slot_hot, owner_hot).astype(jnp.bfloat16)
    packed = jnp.dot(dispatch_map, moe_input, preferred_element_type=jnp.float32).astype(
        jnp.bfloat16
    )
    outgoing = jnp.broadcast_to(
        packed.reshape(experts, 1, capacity, model_width), (experts, PAIR, capacity, model_width)
    )
    outgoing = outgoing.reshape(seq_count, capacity, model_width)
    incoming = lax.all_to_all(outgoing, "seq", split_axis=0, concat_axis=0, tiled=True)
    expert_rows = incoming.reshape(seq_count * capacity, model_width)
    gate_matrix = gate_weight[0]
    up_matrix = up_weight[0]
    down_matrix = down_weight[0]
    shard_piece = lax.all_gather(expert_rows, "mp", axis=0, tiled=True)
    gate_value = jnp.dot(shard_piece, gate_matrix, preferred_element_type=jnp.float32)
    lifted = jnp.dot(shard_piece, up_matrix, preferred_element_type=jnp.float32)
    hidden_rows = (jax.nn.silu(gate_value) * lifted).astype(jnp.bfloat16)
    half_out = lax.psum_scatter(
        jnp.dot(hidden_rows, down_matrix, preferred_element_type=jnp.float32).astype(jnp.bfloat16),
        "mp",
        scatter_dimension=0,
        tiled=True,
    )
    returned = lax.all_to_all(
        half_out.reshape(seq_count, capacity, model_width),
        "seq",
        split_axis=0,
        concat_axis=0,
        tiled=True,
    )
    expert_out = jnp.sum(
        returned.reshape(experts, PAIR, capacity, model_width).astype(jnp.float32), axis=1
    )
    expert_out = expert_out.reshape(experts * capacity, model_width)
    weighted = route_weights.reshape(-1)[:, None] * slot_hot
    combine_map = jnp.einsum("at,as->ts", owner_hot, weighted, precision=lax.Precision.HIGHEST)
    expert_mix = jnp.dot(combine_map, expert_out, precision=lax.Precision.HIGHEST)
    return (hidden_wide + expert_mix).astype(jnp.bfloat16)


def solution(mesh):
    placed = (
        P("seq", "mp"),
        P("seq", "mp"),
        P("seq", "mp"),
        P("mp", "seq"),
        P(("seq", "mp"), None),
        P("mp", "seq"),
        P("seq", None, "mp"),
        P("seq", None, "mp"),
        P("seq", "mp", None),
        P(("seq", "mp"), None),
        P(("seq", "mp"), None),
    )
    return jax.shard_map(
        per_device, mesh=mesh, in_specs=placed, out_specs=P(("seq", "mp"), None), check_vma=False
    )
```

profile of v0, /device:TPU:0, one launch (start us, length us, event | category | flops | bytes accessed | tf_op | source)
XLA Modules:
  0.0 556.1 jit_solution(4670933938253191104)
XLA Ops:
  6.5 1.0 reduce_window_sum.33
  7.6 0.2 slice_reduce_fusion
  7.8 1.0 copy.40
  8.9 1.7 convolution_convert_fusion.3
  10.7 0.7 all-gather.6.cloned.1.call-update
  11.4 1.3 dynamic-slice
  13.5 0.2 dynamic-update-slice
  13.7 15.1 %all-reduce = f32[32]{0:T(128)S(1)} all-reduce(f32[32]{0:T(128)S(1)} %dynamic-update-slice), channel_id=2, replica_groups=mesh['seq'=8,'mp'=4] {'seq'}, use_global_device_ids=true, to_apply=%add | all-reduce | flops 32 | bytes 256
  29.0 1.3 convolution_bitcast_fusion.1
  30.3 6.7 %all-gather.10.cloned.1.call-done = bf16[32,128,128]{2,1,0:T(8,128)(2,1)} async-done(((bf16[4,128,128]{2,1,0:T(8,128)(2,1)}), bf16[32,128,128]{2,1,0:T(8,128)(2,1)}) %all-gather.10.cloned.1.call-update) | async-done | bytes 1048592 | tf_op jit(solution)/shard_map/all_gather | solution.py:52
  37.0 1.5 multiply_reduce_fusion
  38.6 0.1 copy.38
  38.7 0.3 multiply_reduce_fusion.1
  39.0 45.3 %all-gather.6.cloned.1.call-done = bf16[512,6144]{1,0:T(8,128)(2,1)} async-done(((bf16[512,768]{1,0:T(8,128)(2,1)}), bf16[512,6144]{1,0:T(8,128)(2,1)}) %all-gather.6.cloned.1.call-update) | async-done | bytes 6291472 | tf_op jit(solution)/shard_map/all_gather | solution.py:76
  84.3 5.0 convolution_convert_fusion.1
  89.5 0.1 reshape.95
  89.8 0.2 select_reduce_fusion
  90.0 34.8 %reduce-scatter.3.cloned.1.call-done = bf16[32,6144]{1,0:T(8,128)(2,1)} async-done(((bf16[128,6144]{1,0:T(8,128)(2,1)}), bf16[32,6144]{1,0:T(8,128)(2,1)}) %reduce-scatter.3.cloned.1.call-update) | async-done | bytes 393232 | tf_op jit(solution)/shard_map/reduce_scatter | solution.py:79
  124.8 1.2 fusion.10
  126.0 1.8 convolution_convert_fusion.2
  127.8 0.2 broadcast_in_dim.66
  128.1 33.0 %all_to_all.10 = bf16[8,24,6144]{2,1,0:T(8,128)(2,1)} all-to-all(bf16[8,24,6144]{2,1,0:T(8,128)(2,1)S(1)} %bitcast.80), channel_id=1, replica_groups=mesh['seq'=8,'mp'=4] {'seq'}, dimensions={0} | all-to-all | bytes 4718592 | tf_op jit(solution)/shard_map/all_to_all | solution.py:108
  161.1 164.0 %all-gather.8.cloned.1.call-done = bf16[768,6144]{1,0:T(8,128)(2,1)} async-done(((bf16[192,6144]{1,0:T(8,128)(2,1)}), bf16[768,6144]{1,0:T(8,128)(2,1)}) %all-gather.8.cloned.1.call-update) | async-done | bytes 9437200 | tf_op jit(solution)/shard_map/all_gather | solution.py:113
  325.2 11.0 %fusion.1 = f32[768,576]{0,1:T(8,128)S(1)} fusion(bf16[768,6144]{1,0:T(8,128)(2,1)} %all-gather.8.cloned.1.call-done, bf16[1,6144,576]{1,2,0:T(8,128)(2,1)} %param.18), kind=kOutput, calls=%fused_computation.3 | convolution fusion | flops 5435817984 | bytes 18284544 | tf_op jit(solution)/shard_map/dot_general | solution.py:115
  336.2 8.4 %multiply_convert_fusion = bf16[768,576]{0,1:T(8,128)(2,1)S(1)} fusion(f32[768,576]{0,1:T(8,128)S(1)} %fusion.1, bf16[768,6144]{1,0:T(8,128)(2,1)S(1)} %copy-done.6, bf16[1,6144,576]{1,2,0:T(8,128)(2,1)} %param.17), kind=kOutput, calls=%fused_computation.12 | convolution fusion | flops 5438472192 | bytes 19169280 | tf_op jit(solution)/shard_map/dot_general | solution.py:114
  344.6 9.7 %convolution_convert_fusion = bf16[768,6144]{1,0:T(8,128)(2,1)} fusion(bf16[768,576]{0,1:T(8,128)(2,1)S(1)} %multiply_convert_fusion, bf16[1,576,6144]{2,1,0:T(8,128)(2,1)S(1)} %bitcast.88), kind=kOutput, calls=%fused_computation | convolution fusion | flops 5440536576 | bytes 17399808 | tf_op jit(solution)/shard_map/dot_general | solution.py:118
  354.3 159.6 %reduce-scatter.5.cloned.1.call-done = bf16[192,6144]{1,0:T(8,128)(2,1)} async-done(((bf16[768,6144]{1,0:T(8,128)(2,1)}), bf16[192,6144]{1,0:T(8,128)(2,1)}) %reduce-scatter.5.cloned.1.call-update) | async-done | bytes 2359312 | tf_op jit(solution)/shard_map/reduce_scatter | solution.py:117
  514.0 3.8 all-to-all-start.1
  517.9 0.3 fusion.35
  518.2 29.0 %all-to-all-done.1 = bf16[8,24,6144]{2,1,0:T(8,128)(2,1)S(1)} async-done(((bf16[8,24,6144]{2,1,0:T(8,128)(2,1)}), bf16[8,24,6144]{2,1,0:T(8,128)(2,1)S(1)}, u32[]{:S(2)}, u32[]{:S(2)}) %all-to-all-start.1) | async-done | bytes 2359328 | tf_op jit(solution)/shard_map/all_to_all | solution.py:123
  547.2 0.4 convert_reduce_fusion
  547.6 2.0 fusion.5
  (45 shorter events, 1.1 us)
Async XLA Ops:
  6.5 22.5 %copy-start = (bf16[128,512]{1,0:T(8,128)(2,1)S(1)}, bf16[128,512]{1,0:T(8,128)(2,1)}, u32[]{:S(2)}) copy-start(bf16[128,512]{1,0:T(8,128)(2,1)} %param.11) | copy-start | bytes 393220
  6.5 30.5 %all-gather.10.cloned.1.call-start = ((), (), s32[]{:S(2)}) async-start(), calls=%async_computation.8 | async-start | bytes 1179648 | tf_op jit(solution)/shard_map/all_gather | solution.py:52
  10.6 73.7 %all-gather.6.cloned.1.call-start = ((), (), s32[]{:S(2)}) async-start(), calls=%async_computation.4 | async-start | bytes 7077888 | tf_op jit(solution)/shard_map/all_gather | solution.py:76
  11.4 113.4 %reduce-scatter.3.cloned.1.call-start = ((), (), s32[]{:S(2)}) async-start(), calls=%async_computation.5 | async-start | bytes 1966080 | tf_op jit(solution)/shard_map/reduce_scatter | solution.py:79
  84.3 5.1 copy-start.4
  84.3 40.5 %copy-start.2 = (bf16[32,6144]{1,0:T(8,128)(2,1)S(1)}, bf16[32,6144]{1,0:T(8,128)(2,1)}, u32[]{:S(2)}) copy-start(bf16[32,6144]{1,0:T(8,128)(2,1)} %param.15) | copy-start | bytes 1179652
  89.4 235.8 %all-gather.8.cloned.1.call-start = ((), (), s32[]{:S(2)}) async-start(), calls=%async_computation.6 | async-start | bytes 11796480 | tf_op jit(solution)/shard_map/all_gather | solution.py:113
  161.1 352.9 %reduce-scatter.5.cloned.1.call-start = ((), (), s32[]{:S(2)}) async-start(), calls=%async_computation.7 | async-start | bytes 11796480 | tf_op jit(solution)/shard_map/reduce_scatter | solution.py:117
  325.2 11.0 %copy-start.6 = (bf16[768,6144]{1,0:T(8,128)(2,1)S(1)}, bf16[768,6144]{1,0:T(8,128)(2,1)}, u32[]{:S(2)}) copy-start(bf16[768,6144]{1,0:T(8,128)(2,1)} %all-gather.8.cloned.1.call-done) | copy-start | bytes 28311556
  325.2 19.4 %slice-start = ((s8[7077888]{0:T(1024)(128)(4,1)}), s8[4194304]{0:T(1024)(128)(4,1)S(1)}, s32[]{:S(2)}) async-start(s8[7077888]{0:T(1024)(128)(4,1)} %bitcast.87), calls=%async_computation.9 | async-start | bytes 8388608
  336.2 8.4 %slice-start.1 = ((s8[7077888]{0:T(1024)(128)(4,1)}), s8[2883584]{0:T(1024)(128)(4,1)S(1)}, s32[]{:S(2)}) async-start(s8[7077888]{0:T(1024)(128)(4,1)} %bitcast.87), calls=%async_computation.10 | async-start | bytes 5767168
  514.0 3.8 copy-start.5
  514.0 33.2 %all-to-all-start.1 = ((bf16[8,24,6144]{2,1,0:T(8,128)(2,1)}), bf16[8,24,6144]{2,1,0:T(8,128)(2,1)S(1)}, u32[]{:S(2)}, u32[]{:S(2)}) async-start(bf16[8,24,6144]{2,1,0:T(8,128)(2,1)} %bitcast.82), calls=%async_computation.3 | async-start | bytes 4718592 | tf_op jit(solution)/shard_map/all_to_all | solution.py:123
  518.2 29.4 %copy-start.3 = (bf16[32,6144]{1,0:T(8,128)(2,1)S(1)}, bf16[32,6144]{1,0:T(8,128)(2,1)}, u32[]{:S(2)}) copy-start(bf16[32,6144]{1,0:T(8,128)(2,1)} %reduce-scatter.3.cloned.1.call-done) | copy-start | bytes 1179652
  547.2 2.4 copy-start.1
Sparse Core Ops, SparseCore 0:
  10.7 26.2 all-gather.9
  38.9 45.3 all-gather.5
  89.5 35.2 reduce-scatter.2
  161.2 163.9 all-gather.7
  354.4 159.4 reduce-scatter.4
where the time goes:
time: 557 us; the launch traced here: 556 us
  waiting for transfers between devices  440 us (79%)
  blocking collectives  48.1 us (9%)
  matrix products  41.4 us (7%)
  between operations  14 us (3%)
    all_gather x1, waiting for transfers between devices, per_device(): shard_piece = lax.all_gather(expert_rows, 'mp', axis=0, tiled=True)  164 us
    reduce_scatter x1, waiting for transfers between devices, per_device(): lax.psum_scatter(jnp.dot(hidden_rows, down_matrix, preferred_element_type...  160 us
    all_gather x1, waiting for transfers between devices, per_device(): lax.all_gather(out_weight, 'seq', axis=1, tiled=True)  45.3 us
    reduce_scatter x1, waiting for transfers between devices, per_device(): lax.psum_scatter(partial_out.astype(jnp.bfloat16), 'mp', scatter_dimensio...  34.8 us
    all_to_all x1, blocking collectives, per_device(): lax.all_to_all(outgoing, 'seq', split_axis=0, concat_axis=0, tiled=True)  33 us
    all_to_all x1, waiting for transfers between devices, per_device(): lax.all_to_all(half_out.reshape(seq_count, capacity, model_width), 'seq',...  29 us
    unnamed x1, blocking collectives  15.1 us
  transfers between devices with their start and end apart: 6, of which 6 were waited for; matrix products, arithmetic and copies ran while one was open for 1% of the time, Pallas kernels for 0%

commit v1 on v0

--- a/solution.py
+++ b/solution.py
@@ -1,13 +1,469 @@
+import functools
+
 import jax
 import jax.numpy as jnp
 from jax import lax
+from jax.experimental import pallas as pl
+from jax.experimental.pallas import tpu as pltpu
 from jax.sharding import PartitionSpec as P
 
 TOP = 2
 PAIR = 2
-
-
-def per_device(
+VMEM_LIMIT = 44 * 1024 * 1024
+DECAY_ROWS = 16
+HIGH = lax.Precision.HIGHEST
+F32 = jnp.float32
+BF16 = jnp.bfloat16
+
+
+def params():
+    return pltpu.CompilerParams(vmem_limit_bytes=VMEM_LIMIT)
+
+
+def cost(flops, moved):
+    return pl.CostEstimate(flops=int(flops), bytes_accessed=int(moved), transcendentals=0)
+
+
+def after(array, *earlier):
+    return lax.optimization_barrier((array,) + earlier)[0]
+
+
+def swap_columns(array, distance):
+    count = lax.axis_size("seq")
+    return lax.ppermute(array, "seq", [(i, i ^ (PAIR * distance)) for i in range(count)])
+
+
+def swap_cores(array):
+    count = lax.axis_size("seq")
+    return lax.ppermute(array, "seq", [(i, i ^ 1) for i in range(count)])
+
+
+def swap_layers(array, distance):
+    count = lax.axis_size("mp")
+    return lax.ppermute(array, "mp", [(i, i ^ distance) for i in range(count)])
+
+
+def local_kernel(q_ref, k_ref, v_ref, decay_ref, state_ref, local_ref, weighted_ref):
+    span = q_ref.shape[0]
+    heads = decay_ref.shape[0]
+    size = q_ref.shape[1] // heads
+    row = lax.broadcasted_iota(jnp.int32, (span, span), 0)
+    col = lax.broadcasted_iota(jnp.int32, (span, span), 1)
+    causal = row >= col
+    decay = decay_ref[...]
+    along = jnp.dot(decay, (row <= col).astype(F32), precision=HIGH, preferred_element_type=F32)
+    down = lax.dot_general(
+        causal.astype(F32), decay, (((1,), (1,)), ((), ())), precision=HIGH, preferred_element_type=F32
+    )
+    extra = lax.broadcasted_iota(jnp.int32, (DECAY_ROWS, size), 0)
+    for h in range(heads):
+        cols = slice(h * size, (h + 1) * size)
+        q, k, v = q_ref[:, cols], k_ref[:, cols], v_ref[:, cols]
+        here = down[:, h : h + 1]
+        spread = here - along[h : h + 1, :]
+        weight = jnp.where(causal, jnp.exp(jnp.where(causal, spread, 0.0)), 0.0)
+        raw = lax.dot_general(q, k, (((1,), (1,)), ((), ())), preferred_element_type=F32)
+        local_ref[:, cols] = jnp.dot((raw * weight).astype(BF16), v, preferred_element_type=F32)
+        total = along[h : h + 1, span - 1 : span]
+        scaled = (jnp.exp(total - here) * k.astype(F32)).astype(BF16)
+        state_ref[h, :size, :] = lax.dot_general(
+            scaled, v, (((0,), (0,)), ((), ())), preferred_element_type=F32
+        ).astype(BF16)
+        first = total.astype(BF16).astype(F32)
+        second = (total - first).astype(BF16).astype(F32)
+        third = total - first - second
+        pieces = jnp.where(extra == 0, first, jnp.where(extra == 1, second, jnp.where(extra == 2, third, 0.0)))
+        state_ref[h, size:, :] = pieces.astype(BF16)
+        weighted_ref[:, cols] = (jnp.exp(here) * q.astype(F32)).astype(BF16)
+
+
+def prefix_kernel(count, layers, *refs):
+    row_ref, between_ref, earlier_ref, local_ref, weighted_ref = refs[:5]
+    state_refs = refs[5 : 5 + count]
+    out_ref, totals, held = refs[5 + count :]
+    heads, tall, size = state_refs[0].shape
+    span = local_ref.shape[0]
+    for p in range(count):
+        for h in range(heads):
+            totals[p : p + 1, h * size : (h + 1) * size] = jnp.sum(
+                state_refs[p][h, size:, :].astype(F32), axis=0, keepdims=True
+            )
+    gap = jnp.dot(between_ref[...], totals[...], precision=HIGH, preferred_element_type=F32)
+    totals[...] = jnp.exp(gap) * earlier_ref[...]
+    for h in range(heads):
+        cols = slice(h * size, (h + 1) * size)
+        prefix = jnp.zeros((size, size), F32)
+        for p in range(count):
+            prefix += totals[p : p + 1, cols] * state_refs[p][h, :size, :].astype(F32)
+        mixed = local_ref[:, cols] + jnp.dot(
+            weighted_ref[:, cols], prefix.astype(BF16), preferred_element_type=F32
+        )
+        mean = jnp.mean(mixed * mixed, axis=-1, keepdims=True)
+        held[:, cols] = (mixed * lax.rsqrt(mean + 1e-06)).astype(BF16)
+    rows = span // layers
+    for r in range(layers):
+        start = pl.multiple_of(row_ref[r] * rows, rows)
+        out_ref[r * rows : (r + 1) * rows, :] = held[pl.ds(start, rows), :]
+
+
+def project_kernel(count, *refs):
+    place_ref, rows_ref = refs[:2]
+    weight_refs = refs[2 : 2 + count]
+    keep_ref, send_ref = refs[2 + count :]
+    half = keep_ref.shape[0]
+    width = weight_refs[0].shape[1]
+    rows = rows_ref[...]
+    for p in range(count):
+        part = jnp.dot(rows, weight_refs[p][...], preferred_element_type=F32).astype(BF16)
+        start = pl.multiple_of(place_ref[p] * width, width)
+        keep_ref[:, pl.ds(start, width)] = part[:half]
+        send_ref[:, pl.ds(start, width)] = part[half:]
+
+
+def pack_kernel(count, map_ref, near_ref, far_ref, *out_refs):
+    rows = out_refs[0].shape[0]
+    tokens = jnp.concatenate([near_ref[...], far_ref[...]], axis=0)
+    packed = jnp.dot(map_ref[...], tokens, preferred_element_type=F32).astype(BF16)
+    for d in range(count):
+        out_refs[d][...] = packed[d * rows : (d + 1) * rows]
+
+
+def expert_kernel(pieces, blocks, first, last, features, *refs):
+    x_refs = refs[:pieces]
+    gate_refs, up_refs = refs[pieces : pieces + blocks], refs[pieces + blocks : pieces + 2 * blocks]
+    rest = refs[pieces + 2 * blocks :]
+    if not first:
+        sum_in, square_in = rest[:2]
+        rest = rest[2:]
+    if last:
+        out_ref, sum_ref, square_ref = rest
+    else:
+        sum_ref, square_ref = rest
+    size = gate_refs[0].shape[0]
+    even = size // 128 * 128
+    step = pl.program_id(0)
+    x = jnp.concatenate([ref[...] for ref in x_refs], axis=0)
+    gate = jnp.concatenate([ref[...] for ref in gate_refs], axis=1)
+    up = jnp.concatenate([ref[...] for ref in up_refs], axis=1)
+    both = jnp.concatenate([gate[:even], up[:even], gate[even:], up[even:]], axis=0)
+    sums = lax.dot_general(x, both, (((1,), (1,)), ((), ())), preferred_element_type=F32)
+    wide = x.astype(F32)
+    lanes = square_ref.shape[1]
+    squares = wide[:, :lanes] * wide[:, :lanes]
+    for i in range(1, x.shape[1] // lanes):
+        part = wide[:, i * lanes : (i + 1) * lanes]
+        squares += part * part
+
+    @pl.when(step == 0)
+    def _():
+        sum_ref[...] = sums if first else sum_in[...] + sums
+        square_ref[...] = squares if first else square_in[...] + squares
+
+    @pl.when(step > 0)
+    def _():
+        sum_ref[...] += sums
+        square_ref[...] += squares
+
+    if last:
+
+        @pl.when(step == pl.num_programs(0) - 1)
+        def _():
+            mean = jnp.sum(square_ref[...], axis=1, keepdims=True) / features
+            scale = lax.rsqrt(mean + 1e-06)
+
+            def activate(gate, up):
+                gate = gate * scale
+                return (gate / (1.0 + jnp.exp(-gate)) * (up * scale)).astype(BF16)
+
+            out_ref[:, :even] = activate(sum_ref[:, :even], sum_ref[:, even : 2 * even])
+            if even < size:
+                tail = sum_ref[:, 2 * even :]
+                out_ref[:, even:] = activate(tail[:, : size - even], tail[:, size - even :])
+
+
+def down_kernel(hidden_ref, weight_ref, own_ref, other_ref):
+    half = own_ref.shape[0]
+    out = jnp.dot(hidden_ref[...], weight_ref[...], preferred_element_type=F32).astype(BF16)
+    own_ref[...] = out[:half]
+    other_ref[...] = out[half:]
+
+
+def combine_kernel(count, high_ref, low_ref, *refs):
+    x_refs = refs[:count]
+    keep_ref, send_ref = refs[count:]
+    half = keep_ref.shape[0]
+    x = jnp.concatenate([ref[...] for ref in x_refs], axis=0)
+    out = jnp.dot(high_ref[...], x, preferred_element_type=F32)
+    out += jnp.dot(low_ref[...], x, preferred_element_type=F32)
+    keep_ref[...] = out[:half]
+    send_ref[...] = out[half:].astype(BF16)
+
+
+def whole_block(array):
+    return pl.BlockSpec(array.shape, lambda *_: (0,) * array.ndim)
+
+
+def tiled(
+    queries, keys, values, log_decay, residual, out_weight, gate_weight, up_weight, down_weight, expert_ids,
+    route_weights, chunks, returns,
+):
+    seq_count, layers = lax.axis_size("seq"), lax.axis_size("mp")
+    me, layer = lax.axis_index("seq"), lax.axis_index("mp")
+    columns = seq_count // PAIR
+    column = me // PAIR
+    span, heads = queries.shape[0], log_decay.shape[0]
+    size = queries.shape[1] // heads
+    features = residual.shape[1]
+    hidden_size = gate_weight.shape[2]
+    tok = residual.shape[0]
+    half = span // 2
+    block = out_weight.shape[1]
+    width = block // chunks
+    chunk_width = seq_count * width
+    capacity = max(2, tok * TOP * 3 // (2 * columns))
+    slots = -(-layers * capacity // 16) * 16
+    distances = [1 << i for i in range((layers - 1).bit_length())]
+    order = [0]
+    for d in reversed(distances):
+        order = order + [b ^ d for b in order]
+
+    away = [PAIR * (p % columns) + p // columns for p in range(seq_count)]
+    blocks_at = jnp.stack([me ^ a for a in away]).astype(jnp.int32)
+    rows_at = jnp.stack([layer ^ r for r in order]).astype(jnp.int32)
+
+    def spread(array):
+        own = [array] + [swap_columns(array, d) for d in range(1, columns)]
+        return own + [swap_cores(a) for a in own]
+
+    smem = pl.BlockSpec(memory_space=pltpu.SMEM)
+    vmem = pl.BlockSpec(memory_space=pltpu.VMEM)
+
+    def across(array):
+        return [array] + [swap_columns(array, d) for d in range(1, columns)]
+
+    def both_cores(arrays):
+        return arrays + [swap_cores(a) for a in arrays]
+
+    slices = [out_weight[:, i * width : (i + 1) * width] for i in range(chunks)]
+    weights = [None] * chunks
+    weights[0] = across(slices[0])
+    state, local_part, weighted_queries = pl.pallas_call(
+        local_kernel,
+        out_shape=(
+            jax.ShapeDtypeStruct((heads, size + DECAY_ROWS, size), BF16),
+            jax.ShapeDtypeStruct((span, heads * size), F32),
+            jax.ShapeDtypeStruct((span, heads * size), BF16),
+        ),
+        in_specs=[vmem] * 4,
+        out_specs=(vmem,) * 3,
+        compiler_params=params(),
+        cost_estimate=cost(8 * heads * span * span * size, 1 << 20),
+        name="local_attention",
+    )(queries, keys, values, log_decay)
+    states = across(state)
+
+    flat = expert_ids.reshape(-1)
+    count = flat.shape[0]
+    before = jnp.arange(count)[:, None] > jnp.arange(count)[None, :]
+    rank = jnp.sum((before & (flat[:, None] == flat[None, :])).astype(jnp.int32), axis=1).reshape(tok, TOP)
+    route = jnp.concatenate(
+        [expert_ids.astype(F32), rank.astype(F32), route_weights, jnp.zeros((tok, 2), F32)], axis=1
+    )
+    route = after(route, state)
+    for d in reversed(distances):
+        route = jnp.concatenate([route, swap_layers(route, d)], axis=0)
+    ids, ranks = route[:, :TOP].astype(jnp.int32), route[:, TOP : 2 * TOP].astype(jnp.int32)
+    gains = route[:, 2 * TOP : 3 * TOP]
+    slot = (jnp.arange(span) // tok * capacity)[:, None] + ranks
+    place = jnp.arange(columns * slots)
+    target = jnp.where(ids[:, :, None] == (column ^ (place // slots))[None, None, :], slot[:, :, None], -1)
+    hit = target == (place % slots)[None, None, :]
+    pack_map = jnp.any(hit, axis=1).T.astype(BF16)
+    mix = jnp.sum(jnp.where(hit, gains[:, :, None], 0.0), axis=1)
+    mix_high = lax.reduce_precision(mix, 8, 7)
+    mix_low = (mix - mix_high).astype(BF16)
+    mix_high = mix_high.astype(BF16)
+
+    near = after(residual, route)
+    for d in reversed(distances[1:]):
+        near = jnp.concatenate([near, swap_layers(near, d)], axis=0)
+
+    weights[0] = both_cores(weights[0])
+    weights[1] = across(after(slices[1], *states))
+    states = both_cores(states)
+    between = ((blocks_at[:, None] < blocks_at[None, :]) & (blocks_at[None, :] < me)).astype(F32)
+    earlier = jnp.broadcast_to((blocks_at < me).astype(F32)[:, None], (seq_count, heads * size))
+    normed = pl.pallas_call(
+        functools.partial(prefix_kernel, seq_count, layers),
+        out_shape=jax.ShapeDtypeStruct((span, heads * size), BF16),
+        in_specs=[smem] + [vmem] * (4 + seq_count),
+        out_specs=vmem,
+        scratch_shapes=[pltpu.VMEM((seq_count, heads * size), F32), pltpu.VMEM((span, heads * size), BF16)],
+        compiler_params=params(),
+        cost_estimate=cost(2 * heads * span * size * size, 3 << 20),
+        name="prefix_attention",
+    )(rows_at, between, earlier, local_part, weighted_queries, *states)
+
+    rows = 2 * columns * slots
+    gate_view, up_view = gate_weight[0].T, up_weight[0].T
+
+    def project(i, *earlier):
+        keep, send = pl.pallas_call(
+            functools.partial(project_kernel, seq_count),
+            out_shape=(jax.ShapeDtypeStruct((half, chunk_width), BF16),) * 2,
+            in_specs=[smem] + [vmem] * (1 + seq_count),
+            out_specs=(vmem,) * 2,
+            compiler_params=params(),
+            cost_estimate=cost(2 * span * heads * size * chunk_width, 2 * heads * size * chunk_width),
+            name="project",
+        )(blocks_at, after(normed, *earlier), *weights[i])
+        return keep, swap_layers(send, distances[0])
+
+    def sum_layers(keep, arrived):
+        part = (keep.astype(F32) + arrived.astype(F32)).astype(BF16)
+        for d in distances[1:-1]:
+            kept = part.shape[0] // 2
+            part = (part[:kept].astype(F32) + swap_layers(part[kept:], d).astype(F32)).astype(BF16)
+        return part, swap_layers(part, distances[-1])
+
+    def add_residual(i, part, other):
+        base = jnp.concatenate(
+            [near[: 2 * tok, s * block + i * width : s * block + (i + 1) * width] for s in range(seq_count)], axis=1
+        )
+        other = jnp.concatenate([other[tok:], other[:tok]], axis=0)
+        token = (base.astype(F32) + (part.astype(F32) + other.astype(F32))).astype(BF16)
+        mine = token[:tok]
+        for d in reversed(distances[1:-1]):
+            token = jnp.concatenate([token, swap_layers(token, d)], axis=0)
+        return mine, token, swap_layers(token, distances[0])
+
+    def dispatch(token, far):
+        tile = chunk_width // 4
+        packed = pl.pallas_call(
+            functools.partial(pack_kernel, columns),
+            grid=(chunk_width // tile,),
+            out_shape=(jax.ShapeDtypeStruct((slots, chunk_width), BF16),) * columns,
+            in_specs=[
+                whole_block(pack_map),
+                pl.BlockSpec((half, tile), lambda n: (0, n)),
+                pl.BlockSpec((half, tile), lambda n: (0, n)),
+            ],
+            out_specs=(pl.BlockSpec((slots, tile), lambda n: (0, n)),) * columns,
+            compiler_params=params(),
+            cost_estimate=cost(2 * columns * slots * span * chunk_width, 2 * columns * slots * chunk_width),
+            name="pack",
+        )(pack_map, token, far)
+        return [packed[0]] + [swap_columns(packed[d], d) for d in range(1, columns)]
+
+    steps = 2
+    blocks = seq_count // steps
+    sum_shapes = ((rows, 2 * hidden_size), (rows, 128))
+
+    def gate_up(i, arrived, held):
+        first, last = i == 0, i == chunks - 1
+
+        def weight_block(b):
+            return pl.BlockSpec((hidden_size, width), lambda s: (0, (s * blocks + b) * chunks + i))
+
+        return pl.pallas_call(
+            functools.partial(expert_kernel, seq_count, blocks, first, last, features),
+            grid=(steps,),
+            out_shape=jax.ShapeDtypeStruct((rows, hidden_size), BF16)
+            if last
+            else tuple(jax.ShapeDtypeStruct(s, F32) for s in sum_shapes),
+            in_specs=[pl.BlockSpec((slots, blocks * width), lambda s: (0, s))] * seq_count
+            + [weight_block(b) for b in range(blocks)] * 2
+            + [whole_block(a) for a in held],
+            out_specs=pl.BlockSpec((rows, hidden_size), lambda s: (0, 0))
+            if last
+            else tuple(pl.BlockSpec(s, lambda n: (0, 0)) for s in sum_shapes),
+            scratch_shapes=[pltpu.VMEM(s, F32) for s in sum_shapes] if last else [],
+            compiler_params=params(),
+            cost_estimate=cost(4 * rows * hidden_size * chunk_width, 4 * hidden_size * chunk_width),
+            name="gate_up",
+        )(*arrived, *[gate_view] * blocks, *[up_view] * blocks, *held)
+
+    projected, parts, tokens, arrived, sums = [None] * chunks, [None] * chunks, [None] * chunks, [None] * chunks, []
+    projected[0] = project(0)
+    for i in range(chunks):
+        if i + 2 < chunks:
+            weights[i + 2] = across(after(slices[i + 2], *weights[i + 1]))
+        parts[i] = sum_layers(*projected[i])
+        if i + 1 < chunks:
+            weights[i + 1] = both_cores(weights[i + 1])
+            projected[i + 1] = project(i + 1, projected[i][1])
+        tokens[i] = add_residual(i, *parts[i])
+        arrived[i] = dispatch(*tokens[i][1:])
+    for i in range(chunks):
+        sums = gate_up(i, both_cores(arrived[i]), sums)
+    expert_hidden = sums
+
+    own_hidden = jnp.concatenate(
+        [tokens[i][0][:, s * width : (s + 1) * width] for s in range(seq_count) for i in range(chunks)], axis=1
+    )
+    out_width = features // returns
+    tile = out_width // 4
+    downs, backs, outputs = [None] * returns, [None] * returns, []
+
+    def down(i):
+        own, other = pl.pallas_call(
+            down_kernel,
+            grid=(out_width // tile,),
+            out_shape=(jax.ShapeDtypeStruct((rows // 2, out_width), BF16),) * 2,
+            in_specs=[
+                whole_block(expert_hidden),
+                pl.BlockSpec((hidden_size, tile), lambda n: (0, i * (out_width // tile) + n)),
+            ],
+            out_specs=(pl.BlockSpec((rows // 2, tile), lambda n: (0, n)),) * 2,
+            compiler_params=params(),
+            cost_estimate=cost(2 * rows * hidden_size * out_width, 4 * rows * out_width),
+            name="down",
+        )(expert_hidden, down_weight[0])
+        return own, swap_cores(other)
+
+    def send_back(own, other, *earlier):
+        other = after(other, *earlier)
+        summed = [
+            (own[d * slots : (d + 1) * slots].astype(F32) + other[d * slots : (d + 1) * slots].astype(F32)).astype(BF16)
+            for d in range(columns)
+        ]
+        return [summed[0]] + [swap_columns(summed[d], d) for d in range(1, columns)]
+
+    def combine(back):
+        keep, send = pl.pallas_call(
+            functools.partial(combine_kernel, columns),
+            grid=(out_width // tile,),
+            out_shape=(
+                jax.ShapeDtypeStruct((half, out_width), F32),
+                jax.ShapeDtypeStruct((half, out_width), BF16),
+            ),
+            in_specs=[whole_block(mix_high), whole_block(mix_low)]
+            + [pl.BlockSpec((slots, tile), lambda n: (0, n))] * columns,
+            out_specs=(pl.BlockSpec((half, tile), lambda n: (0, n)),) * 2,
+            compiler_params=params(),
+            cost_estimate=cost(4 * span * columns * slots * out_width, 2 * columns * slots * out_width),
+            name="combine",
+        )(mix_high, mix_low, *back)
+        return keep, swap_layers(send, distances[0])
+
+    def finish(i, keep, arrived):
+        part = keep + arrived.astype(F32)
+        for d in distances[1:]:
+            kept = part.shape[0] // 2
+            part = part[:kept] + swap_layers(part[kept:].astype(BF16), d).astype(F32)
+        mine = own_hidden[:, i * out_width : (i + 1) * out_width].astype(F32)
+        return (mine + part).astype(BF16)
+
+    downs = [down(i) for i in range(returns)]
+    sent = []
+    for i in range(returns):
+        sent.append(send_back(*downs[i], *(sent[i - 1][1:3] if i else [])))
+    for i in range(returns):
+        outputs.append(finish(i, *combine(sent[i])))
+    return jnp.concatenate(outputs, axis=1)
+
+
+def general(
     queries,
     keys,
     values,
@@ -137,6 +593,13 @@
     return (hidden_wide + expert_mix).astype(jnp.bfloat16)
 
 
+def fits(mesh, tok, features, block, chunks, returns):
+    layers, seq_count = mesh.shape["mp"], mesh.shape["seq"]
+    powers = all(n & (n - 1) == 0 for n in (layers, seq_count)) and layers > 1 and seq_count > PAIR
+    whole = block % (128 * chunks) == 0 and features % (512 * returns) == 0
+    return powers and whole and tok % 16 == 0
+
+
 def solution(mesh):
     placed = (
         P("seq", "mp"),
@@ -151,6 +614,14 @@
         P(("seq", "mp"), None),
         P(("seq", "mp"), None),
     )
+    chunks, returns = 3, 3
+
+    def per_device(*args):
+        residual, out_weight = args[4], args[5]
+        if fits(mesh, residual.shape[0], residual.shape[1], out_weight.shape[1], chunks, returns):
+            return tiled(*args, chunks=chunks, returns=returns)
+        return general(*args)
+
     return jax.shard_map(
         per_device, mesh=mesh, in_specs=placed, out_specs=P(("seq", "mp"), None), check_vma=False
     )

time: 557 us -> 300 us (0.54)
  waiting for transfers between devices: 440 us -> 158 us
  starting transfers between devices: 3.95 us -> 67.5 us
  Pallas kernels: 0 us -> 50.7 us
  blocking collectives: 48.1 us -> 0 us
  matrix products: 41.4 us -> 0 us
  between operations: 14 us -> 0.66 us
  local copies, waits for them, and re-layouts: 3.68 us -> 12.4 us
    all_gather x3 -> x0, waiting for transfers between devices: 216 us -> none  [the longest x1 164 us: per_device(): shard_piece = lax.all_gather(expert_rows, 'mp', axis=0, tiled=True)]
    reduce_scatter x2 -> x0, waiting for transfers between devices: 194 us -> none  [the longest x1 160 us: per_device(): lax.psum_scatter(jnp.dot(hidden_rows, down_matrix, preferred_element_type...]
    ppermute x0 -> x79, waiting for transfers between devices: none -> 158 us  [the longest x30 94.5 us: swap_columns(): lax.ppermute(array, 'seq', [(i, i ^ PAIR * distance) for i in range(count)])]
    ppermute x0 -> x79, starting transfers between devices: none -> 67.5 us  [the longest x30 37.2 us: swap_columns(): lax.ppermute(array, 'seq', [(i, i ^ PAIR * distance) for i in range(count)])]
    pallas_call x0 -> x17, Pallas kernels: none -> 50.7 us  [the longest x3 23.3 us: gate_up(): pl.pallas_call(functools.partial(expert_kernel, seq_count, blocks, first,...]
    dot_general x10 -> x0, matrix products: 41.4 us -> none  [the longest x1 11 us: per_device(): lifted = jnp.dot(shard_piece, up_matrix, preferred_element_type=jnp.float32)]
    all_to_all x1 -> x0, blocking collectives: 33 us -> none  [per_device(): lax.all_to_all(outgoing, 'seq', split_axis=0, concat_axis=0, tiled=True)]
    all_to_all x1 -> x0, waiting for transfers between devices: 29 us -> none  [per_device(): lax.all_to_all(half_out.reshape(seq_count, capacity, model_width), 'seq',...]
  transfers between devices with their start and end apart: 6 -> 79, of which waited for: 6 -> 30; matrix products, arithmetic and copies ran while one was open for 1% -> 5% of each run, Pallas kernels for 0% -> 12%
where the time goes in v1:
time: 300 us; the launch traced here: 299 us
  waiting for transfers between devices  158 us (53%)
  starting transfers between devices  67.5 us (22%)
  Pallas kernels  50.7 us (17%)
  local copies, waits for them, and re-layouts  12.4 us (4%)
  other arithmetic  9.87 us (3%)
    ppermute x30, waiting for transfers between devices, swap_columns(): lax.ppermute(array, 'seq', [(i, i ^ PAIR * distance) for i in range(count)])  94.5 us
    ppermute x18, waiting for transfers between devices, swap_layers(): return lax.ppermute(array, 'mp', [(i, i ^ distance) for i in range(count)])  62.7 us
    ppermute x30, starting transfers between devices, swap_columns(): lax.ppermute(array, 'seq', [(i, i ^ PAIR * distance) for i in range(count)])  37.2 us
    ppermute x18, starting transfers between devices, swap_layers(): return lax.ppermute(array, 'mp', [(i, i ^ distance) for i in range(count)])  25.3 us
    pallas_call x3, Pallas kernels, gate_up(): pl.pallas_call(functools.partial(expert_kernel, seq_count, blocks, first,...  23.3 us
    pallas_call x3, Pallas kernels, down(): pl.pallas_call(down_kernel, grid=(out_width // tile,), out_shape=(jax.Sha...  14.2 us
    unnamed x45, local copies, waits for them, and re-layouts  7.44 us
  transfers between devices with their start and end apart: 79, of which 30 were waited for; matrix products, arithmetic and copies ran while one was open for 5% of the time, Pallas kernels for 12%

profile of v1, /device:TPU:0, one launch (start us, length us, event | category | flops | bytes accessed | tf_op | source)
XLA Modules:
  0.0 299.4 jit_solution(11336860021605624327)
XLA Ops:
  4.3 3.0 %collective-permute-start.3 = (bf16[4,144,128]{2,1,0:T(8,128)(2,1)S(1)}, bf16[4,144,128]{2,1,0:T(8,128)(2,1)S(1)}, u32[]{:S(2)}, u32[]{:S(2)}) collective-permute-start(bf16[4,144,128]{2,1,0:T(8,128)(2,1)S(1)} %get-tuple-element.50.refs_5_), channel_id=1, source_target_pairs={{0,8},{4,12},{8,0},{12,4},{16,24},{20,28},{24,16},{28,20},{1,9},{5... | collective-permute-start | bytes 442376 | tf_op jit(solution)/shard_map/ppermute | solution.py:33
  11.6 3.0 %collective-permute-start = (f32[32,8]{0,1:T(8,128)S(1)}, f32[32,8]{0,1:T(8,128)S(1)}, u32[]{:S(2)}, u32[]{:S(2)}) collective-permute-start(f32[32,8]{0,1:T(8,128)S(1)} %maximum_maximum_fusion), channel_id=1, source_target_pairs={{0,2},{1,3},{2,0},{3,1},{4,6},{5,7},{6,4},{7,5},{8,10},{9,11},{10,... | collective-permute-start | bytes 3080 | tf_op jit(solution)/shard_map/ppermute | solution.py:43
  36.5 2.8 collective-permute-done.11.refs_4_
  50.0 7.3 %collective-permute-done.20.refs_4_ = bf16[512,256]{1,0:T(8,128)(2,1)S(1)} collective-permute-done((bf16[512,256]{1,0:T(8,128)(2,1)S(1)}, bf16[512,256]{1,0:T(8,128)(2,1)S(1)}, u32[]{:S(2)}, u32[]{:S(2)}) %collective-permute-start.20) | collective-permute-done | bytes 262176 | tf_op jit(solution)/shard_map/ppermute | solution.py:33
  62.4 4.0 %collective-permute-done.28.refs_3_ = bf16[512,256]{1,0:T(8,128)(2,1)S(1)} collective-permute-done((bf16[512,256]{1,0:T(8,128)(2,1)S(1)}, bf16[512,256]{1,0:T(8,128)(2,1)S(1)}, u32[]{:S(2)}, u32[]{:S(2)}) %collective-permute-start.28) | collective-permute-done | bytes 262176 | tf_op jit(solution)/shard_map/ppermute | solution.py:33
  66.5 5.6 %collective-permute-done.29.refs_4_ = bf16[512,256]{1,0:T(8,128)(2,1)S(1)} collective-permute-done((bf16[512,256]{1,0:T(8,128)(2,1)S(1)}, bf16[512,256]{1,0:T(8,128)(2,1)S(1)}, u32[]{:S(2)}, u32[]{:S(2)}) %collective-permute-start.29) | collective-permute-done | bytes 262176 | tf_op jit(solution)/shard_map/ppermute | solution.py:33
  73.7 8.1 %collective-permute-done.26 = bf16[64,2048]{1,0:T(8,128)(2,1)S(1)} collective-permute-done((bf16[64,2048]{1,0:T(8,128)(2,1)S(1)}, bf16[64,2048]{1,0:T(8,128)(2,1)S(1)}, u32[]{:S(2)}, u32[]{:S(2)}) %collective-permute-start.26) | collective-permute-done | bytes 262176 | tf_op jit(solution)/shard_map/ppermute | solution.py:43
  82.1 13.6 %collective-permute-done.18 = bf16[64,2048]{1,0:T(8,128)(2,1)S(1)} collective-permute-done((bf16[64,2048]{1,0:T(8,128)(2,1)S(1)}, bf16[64,2048]{1,0:T(8,128)(2,1)S(1)}, u32[]{:S(2)}, u32[]{:S(2)}) %collective-permute-start.18) | collective-permute-done | bytes 262176 | tf_op jit(solution)/shard_map/ppermute | solution.py:43
  99.5 10.3 %collective-permute-done.27 = bf16[64,2048]{1,0:T(8,128)(2,1)S(1)} collective-permute-done((bf16[64,2048]{1,0:T(8,128)(2,1)S(1)}, bf16[64,2048]{1,0:T(8,128)(2,1)S(1)}, u32[]{:S(2)}, u32[]{:S(2)}) %collective-permute-start.27) | collective-permute-done | bytes 262176 | tf_op jit(solution)/shard_map/ppermute | solution.py:43
  110.0 6.7 %collective-permute-done.35 = bf16[64,2048]{1,0:T(8,128)(2,1)S(1)} collective-permute-done((bf16[64,2048]{1,0:T(8,128)(2,1)S(1)}, bf16[64,2048]{1,0:T(8,128)(2,1)S(1)}, u32[]{:S(2)}, u32[]{:S(2)}) %collective-permute-start.35) | collective-permute-done | bytes 262176 | tf_op jit(solution)/shard_map/ppermute | solution.py:43
  125.0 5.0 %collective-permute-done.36 = bf16[64,2048]{1,0:T(8,128)(2,1)S(1)} collective-permute-done((bf16[64,2048]{1,0:T(8,128)(2,1)S(1)}, bf16[64,2048]{1,0:T(8,128)(2,1)S(1)}, u32[]{:S(2)}, u32[]{:S(2)}) %collective-permute-start.36) | collective-permute-done | bytes 262176 | tf_op jit(solution)/shard_map/ppermute | solution.py:43
  132.0 3.7 %collective-permute-done.55.refs_2_ = bf16[96,2048]{1,0:T(8,128)(2,1)S(1)} collective-permute-done((bf16[96,2048]{1,0:T(8,128)(2,1)S(1)}, bf16[96,2048]{1,0:T(8,128)(2,1)S(1)}, u32[]{:S(2)}, u32[]{:S(2)}) %collective-permute-start.55) | collective-permute-done | bytes 393248 | tf_op jit(solution)/shard_map/ppermute | solution.py:33
  135.8 5.3 %collective-permute-start.37 = (bf16[64,2048]{1,0:T(8,128)(2,1)S(1)}, bf16[64,2048]{1,0:T(8,128)(2,1)S(1)}, u32[]{:S(2)}, u32[]{:S(2)}) collective-permute-start(bf16[64,2048]{1,0:T(8,128)(2,1)S(1)} %add_convert_fusion.12.near_ref), channel_id=1, source_target_pairs={{0,1},{1,0},{2,3},{3,2},{4,5},{5,4},{6,7},{7,6},{8,9},{9,8},{10,11... | collective-permute-start | bytes 786440 | tf_op jit(solution)/shard_map/ppermute | solution.py:43
  141.5 3.9 %collective-permute-done.37.far_ref = bf16[64,2048]{1,0:T(8,128)(2,1)S(1)} collective-permute-done((bf16[64,2048]{1,0:T(8,128)(2,1)S(1)}, bf16[64,2048]{1,0:T(8,128)(2,1)S(1)}, u32[]{:S(2)}, u32[]{:S(2)}) %collective-permute-start.37) | collective-permute-done | bytes 262176 | tf_op jit(solution)/shard_map/ppermute | solution.py:43
  147.4 6.9 %collective-permute-done.47.refs_2_ = bf16[96,2048]{1,0:T(8,128)(2,1)S(1)} collective-permute-done((bf16[96,2048]{1,0:T(8,128)(2,1)S(1)}, bf16[96,2048]{1,0:T(8,128)(2,1)S(1)}, u32[]{:S(2)}, u32[]{:S(2)}) %collective-permute-start.47) | collective-permute-done | bytes 393248 | tf_op jit(solution)/shard_map/ppermute | solution.py:33
  156.5 2.8 collective-permute-start.40
  159.9 7.8 %collective-permute-done.38.refs_1_ = bf16[96,2048]{1,0:T(8,128)(2,1)S(1)} collective-permute-done((bf16[96,2048]{1,0:T(8,128)(2,1)S(1)}, bf16[96,2048]{1,0:T(8,128)(2,1)S(1)}, u32[]{:S(2)}, u32[]{:S(2)}) %collective-permute-start.38) | collective-permute-done | bytes 393248 | tf_op jit(solution)/shard_map/ppermute | solution.py:33
  167.7 8.5 %collective-permute-done.39.refs_2_ = bf16[96,2048]{1,0:T(8,128)(2,1)S(1)} collective-permute-done((bf16[96,2048]{1,0:T(8,128)(2,1)S(1)}, bf16[96,2048]{1,0:T(8,128)(2,1)S(1)}, u32[]{:S(2)}, u32[]{:S(2)}) %collective-permute-start.39) | collective-permute-done | bytes 393248 | tf_op jit(solution)/shard_map/ppermute | solution.py:33
  177.2 7.0 %gate_up.3 = (f32[768,1152]{1,0:T(8,128)S(1)}, f32[768,128]{1,0:T(8,128)S(1)}) custom-call(bf16[96,2048]{1,0:T(8,128)(2,1)S(1)} %get-tuple-element.73.refs_0_, bf16[96,2048]{1,0:T(8,128)(2,1)S(1)} %collective-permute-done.54.refs_1_, bf16[96,2048]{1,0:T(8,128)(2,1)S(1)} %collective-permute-done.55.refs_2_, ...), custom_call_target="tpu_custom_call" | custom-call | flops 3623878656 | bytes 4718592 | tf_op jit(solution)/shard_map/gate_up/pallas_call | solution.py:368
  186.0 8.3 %gate_up.4 = (f32[768,1152]{1,0:T(8,128)S(1)}, f32[768,128]{1,0:T(8,128)S(1)}) custom-call(bf16[96,2048]{1,0:T(8,128)(2,1)S(1)} %get-tuple-element.69.refs_0_, bf16[96,2048]{1,0:T(8,128)(2,1)S(1)} %collective-permute-done.46.refs_1_, bf16[96,2048]{1,0:T(8,128)(2,1)S(1)} %collective-permute-done.47.refs_2_, ...), custom_call_target="tpu_custom_call" | custom-call | flops 3623878656 | bytes 4718592 | tf_op jit(solution)/shard_map/gate_up/pallas_call | solution.py:368
  194.4 7.9 %gate_up.5.hidden_ref = bf16[768,576]{1,0:T(8,128)(2,1)S(1)} custom-call(bf16[96,2048]{1,0:T(8,128)(2,1)S(1)} %get-tuple-element.65.refs_0_, bf16[96,2048]{1,0:T(8,128)(2,1)S(1)} %collective-permute-done.38.refs_1_, bf16[96,2048]{1,0:T(8,128)(2,1)S(1)} %collective-permute-done.39.refs_2_, bf16[96,2048]{1,0:T(8,128)(2,1)S(1)} %collective-permute-done.40.refs_3_, ...), custom_call_target="tpu_custom_call" | custom-call | flops 3623878656 | bytes 4718592 | tf_op jit(solution)/shard_map/gate_up/pallas_call | solution.py:368
  202.3 4.7 %down.3 = (bf16[384,2048]{1,0:T(8,128)(2,1)S(1)}, bf16[384,2048]{1,0:T(8,128)(2,1)S(1)}) custom-call(bf16[768,576]{1,0:T(8,128)(2,1)S(1)} %gate_up.5.hidden_ref, bf16[576,6144]{1,0:T(8,128)(2,1)} %bitcast.45), custom_call_target="tpu_custom_call" | custom-call | flops 1811939328 | bytes 6291456 | tf_op jit(solution)/shard_map/down/pallas_call | solution.py:409
  207.1 4.7 %down.4 = (bf16[384,2048]{1,0:T(8,128)(2,1)S(1)}, bf16[384,2048]{1,0:T(8,128)(2,1)S(1)}) custom-call(bf16[768,576]{1,0:T(8,128)(2,1)S(1)} %gate_up.5.hidden_ref, bf16[576,6144]{1,0:T(8,128)(2,1)} %bitcast.46), custom_call_target="tpu_custom_call" | custom-call | flops 1811939328 | bytes 6291456 | tf_op jit(solution)/shard_map/down/pallas_call | solution.py:409
  212.4 4.9 %down.5 = (bf16[384,2048]{1,0:T(8,128)(2,1)S(1)}, bf16[384,2048]{1,0:T(8,128)(2,1)S(1)}) custom-call(bf16[768,576]{1,0:T(8,128)(2,1)S(1)} %gate_up.5.hidden_ref, bf16[576,6144]{1,0:T(8,128)(2,1)} %bitcast.47), custom_call_target="tpu_custom_call" | custom-call | flops 1811939328 | bytes 6291456 | tf_op jit(solution)/shard_map/down/pallas_call | solution.py:409
  221.6 8.4 %collective-permute-done.62.refs_1_ = bf16[96,2048]{1,0:T(8,128)(2,1)S(1)} collective-permute-done((bf16[96,2048]{1,0:T(8,128)(2,1)S(1)}, bf16[96,2048]{1,0:T(8,128)(2,1)S(1)}, u32[]{:S(2)}, u32[]{:S(2)}) %collective-permute-start.62) | collective-permute-done | bytes 393248 | tf_op jit(solution)/shard_map/ppermute | solution.py:33
  230.0 9.1 %collective-permute-done.63.refs_2_ = bf16[96,2048]{1,0:T(8,128)(2,1)S(1)} collective-permute-done((bf16[96,2048]{1,0:T(8,128)(2,1)S(1)}, bf16[96,2048]{1,0:T(8,128)(2,1)S(1)}, u32[]{:S(2)}, u32[]{:S(2)}) %collective-permute-start.63) | collective-permute-done | bytes 393248 | tf_op jit(solution)/shard_map/ppermute | solution.py:33
  240.5 2.5 collective-permute-start.65
  250.8 5.0 %collective-permute-done.68.refs_1_ = bf16[96,2048]{1,0:T(8,128)(2,1)S(1)} collective-permute-done((bf16[96,2048]{1,0:T(8,128)(2,1)S(1)}, bf16[96,2048]{1,0:T(8,128)(2,1)S(1)}, u32[]{:S(2)}, u32[]{:S(2)}) %collective-permute-start.68) | collective-permute-done | bytes 393248 | tf_op jit(solution)/shard_map/ppermute | solution.py:33
  255.8 6.6 %collective-permute-done.69.refs_2_ = bf16[96,2048]{1,0:T(8,128)(2,1)S(1)} collective-permute-done((bf16[96,2048]{1,0:T(8,128)(2,1)S(1)}, bf16[96,2048]{1,0:T(8,128)(2,1)S(1)}, u32[]{:S(2)}, u32[]{:S(2)}) %collective-permute-start.69) | collective-permute-done | bytes 393248 | tf_op jit(solution)/shard_map/ppermute | solution.py:33
  268.5 8.5 %collective-permute-done.74.refs_1_ = bf16[96,2048]{1,0:T(8,128)(2,1)S(1)} collective-permute-done((bf16[96,2048]{1,0:T(8,128)(2,1)S(1)}, bf16[96,2048]{1,0:T(8,128)(2,1)S(1)}, u32[]{:S(2)}, u32[]{:S(2)}) %collective-permute-start.74) | collective-permute-done | bytes 393248 | tf_op jit(solution)/shard_map/ppermute | solution.py:33
  277.0 7.1 %collective-permute-done.75.refs_2_ = bf16[96,2048]{1,0:T(8,128)(2,1)S(1)} collective-permute-done((bf16[96,2048]{1,0:T(8,128)(2,1)S(1)}, bf16[96,2048]{1,0:T(8,128)(2,1)S(1)}, u32[]{:S(2)}, u32[]{:S(2)}) %collective-permute-start.75) | collective-permute-done | bytes 393248 | tf_op jit(solution)/shard_map/ppermute | solution.py:33
  287.5 4.8 %collective-permute-done.77 = bf16[64,2048]{1,0:T(8,128)(2,1)S(1)} collective-permute-done((bf16[64,2048]{1,0:T(8,128)(2,1)S(1)}, bf16[64,2048]{1,0:T(8,128)(2,1)S(1)}, u32[]{:S(2)}, u32[]{:S(2)}) %collective-permute-start.77) | collective-permute-done | bytes 262176 | tf_op jit(solution)/shard_map/ppermute | solution.py:43
  (240 shorter events, 100.9 us)
Async XLA Ops:
  4.3 19.4 %collective-permute-start.3 = (bf16[4,144,128]{2,1,0:T(8,128)(2,1)S(1)}, bf16[4,144,128]{2,1,0:T(8,128)(2,1)S(1)}, u32[]{:S(2)}, u32[]{:S(2)}) collective-permute-start(bf16[4,144,128]{2,1,0:T(8,128)(2,1)S(1)} %get-tuple-element.50.refs_5_), channel_id=1, source_target_pairs={{0,8},{4,12},{8,0},{12,4},{16,24},{20,28},{24,16},{28,20},{1,9},{5... | collective-permute-start | bytes 442376 | tf_op jit(solution)/shard_map/ppermute | solution.py:33
  8.9 17.4 %collective-permute-start.6 = (bf16[4,144,128]{2,1,0:T(8,128)(2,1)S(1)}, bf16[4,144,128]{2,1,0:T(8,128)(2,1)S(1)}, u32[]{:S(2)}, u32[]{:S(2)}) collective-permute-start(bf16[4,144,128]{2,1,0:T(8,128)(2,1)S(1)} %get-tuple-element.50.refs_5_), channel_id=1, source_target_pairs={{0,4},{4,0},{8,12},{12,8},{16,20},{20,16},{24,28},{28,24},{1,5},{5... | collective-permute-start | bytes 442376 | tf_op jit(solution)/shard_map/ppermute | solution.py:38
  22.2 19.5 %collective-permute-start.2 = (bf16[32,6144]{1,0:T(8,128)(2,1)S(1)}, bf16[32,6144]{1,0:T(8,128)(2,1)}, u32[]{:S(2)}, u32[]{:S(2)}) collective-permute-start(bf16[32,6144]{1,0:T(8,128)(2,1)S(1)} %copy-done.6), channel_id=1, source_target_pairs={{0,2},{1,3},{2,0},{3,1},{4,6},{5,7},{6,4},{7,5},{8,10},{9,11},{10,... | collective-permute-start | bytes 1179656 | tf_op jit(solution)/shard_map/ppermute | solution.py:43
  62.3 33.6 %collective-permute-start.31 = (bf16[512,256]{1,0:T(8,128)(2,1)S(1)}, bf16[512,256]{1,0:T(8,128)(2,1)S(1)}, u32[]{:S(2)}, u32[]{:S(2)}) collective-permute-start(bf16[512,256]{1,0:T(8,128)(2,1)S(1)} %get-tuple-element.62.refs_2_), channel_id=1, source_target_pairs={{0,4},{4,0},{8,12},{12,8},{16,20},{20,16},{24,28},{28,24},{1,5},{5... | collective-permute-start | bytes 786440 | tf_op jit(solution)/shard_map/ppermute | solution.py:38
  66.5 31.9 %collective-permute-start.32 = (bf16[512,256]{1,0:T(8,128)(2,1)S(1)}, bf16[512,256]{1,0:T(8,128)(2,1)S(1)}, u32[]{:S(2)}, u32[]{:S(2)}) collective-permute-start(bf16[512,256]{1,0:T(8,128)(2,1)S(1)} %collective-permute-done.28.refs_3_), channel_id=1, source_target_pairs={{0,4},{4,0},{8,12},{12,8},{16,20},{20,16},{24,28},{28,24},{1,5},{5... | collective-permute-start | bytes 786440 | tf_op jit(solution)/shard_map/ppermute | solution.py:38
  72.0 26.3 %collective-permute-start.33 = (bf16[512,256]{1,0:T(8,128)(2,1)S(1)}, bf16[512,256]{1,0:T(8,128)(2,1)S(1)}, u32[]{:S(2)}, u32[]{:S(2)}) collective-permute-start(bf16[512,256]{1,0:T(8,128)(2,1)S(1)} %collective-permute-done.29.refs_4_), channel_id=1, source_target_pairs={{0,4},{4,0},{8,12},{12,8},{16,20},{20,16},{24,28},{28,24},{1,5},{5... | collective-permute-start | bytes 786440 | tf_op jit(solution)/shard_map/ppermute | solution.py:38
  72.1 26.3 %collective-permute-start.34 = (bf16[512,256]{1,0:T(8,128)(2,1)S(1)}, bf16[512,256]{1,0:T(8,128)(2,1)S(1)}, u32[]{:S(2)}, u32[]{:S(2)}) collective-permute-start(bf16[512,256]{1,0:T(8,128)(2,1)S(1)} %collective-permute-done.30.refs_5_), channel_id=1, source_target_pairs={{0,4},{4,0},{8,12},{12,8},{16,20},{20,16},{24,28},{28,24},{1,5},{5... | collective-permute-start | bytes 786440 | tf_op jit(solution)/shard_map/ppermute | solution.py:38
  95.9 21.1 %collective-permute-start.53 = (bf16[64,2048]{1,0:T(8,128)(2,1)S(1)}, bf16[64,2048]{1,0:T(8,128)(2,1)S(1)}, u32[]{:S(2)}, u32[]{:S(2)}) collective-permute-start(bf16[64,2048]{1,0:T(8,128)(2,1)S(1)} %add_convert_fusion.16.near_ref), channel_id=1, source_target_pairs={{0,1},{1,0},{2,3},{3,2},{4,5},{5,4},{6,7},{7,6},{8,9},{9,8},{10,11... | collective-permute-start | bytes 786440 | tf_op jit(solution)/shard_map/ppermute | solution.py:43
  99.4 17.3 %collective-permute-start.35 = (bf16[64,2048]{1,0:T(8,128)(2,1)S(1)}, bf16[64,2048]{1,0:T(8,128)(2,1)S(1)}, u32[]{:S(2)}, u32[]{:S(2)}) collective-permute-start(bf16[64,2048]{1,0:T(8,128)(2,1)S(1)} %get-tuple-element.64), channel_id=1, source_target_pairs={{0,1},{1,0},{2,3},{3,2},{4,5},{5,4},{6,7},{7,6},{8,9},{9,8},{10,11... | collective-permute-start | bytes 786440 | tf_op jit(solution)/shard_map/ppermute | solution.py:43
  120.2 20.8 %collective-permute-start.56 = (bf16[96,2048]{1,0:T(8,128)(2,1)S(1)}, bf16[96,2048]{1,0:T(8,128)(2,1)S(1)}, u32[]{:S(2)}, u32[]{:S(2)}) collective-permute-start(bf16[96,2048]{1,0:T(8,128)(2,1)S(1)} %get-tuple-element.76), channel_id=1, source_target_pairs={{0,24},{4,28},{8,16},{12,20},{16,8},{20,12},{24,0},{28,4},{1,25},{... | collective-permute-start | bytes 1179656 | tf_op jit(solution)/shard_map/ppermute | solution.py:33
  123.8 17.7 %collective-permute-start.57 = (bf16[96,2048]{1,0:T(8,128)(2,1)S(1)}, bf16[96,2048]{1,0:T(8,128)(2,1)S(1)}, u32[]{:S(2)}, u32[]{:S(2)}) collective-permute-start(bf16[96,2048]{1,0:T(8,128)(2,1)S(1)} %get-tuple-element.73.refs_0_), channel_id=1, source_target_pairs={{0,4},{4,0},{8,12},{12,8},{16,20},{20,16},{24,28},{28,24},{1,5},{5... | collective-permute-start | bytes 1179656 | tf_op jit(solution)/shard_map/ppermute | solution.py:38
  130.0 17.4 %collective-permute-start.46 = (bf16[96,2048]{1,0:T(8,128)(2,1)S(1)}, bf16[96,2048]{1,0:T(8,128)(2,1)S(1)}, u32[]{:S(2)}, u32[]{:S(2)}) collective-permute-start(bf16[96,2048]{1,0:T(8,128)(2,1)S(1)} %get-tuple-element.70), channel_id=1, source_target_pairs={{0,8},{4,12},{8,0},{12,4},{16,24},{20,28},{24,16},{28,20},{1,9},{5... | collective-permute-start | bytes 1179656 | tf_op jit(solution)/shard_map/ppermute | solution.py:33
  131.4 22.9 %collective-permute-start.47 = (bf16[96,2048]{1,0:T(8,128)(2,1)S(1)}, bf16[96,2048]{1,0:T(8,128)(2,1)S(1)}, u32[]{:S(2)}, u32[]{:S(2)}) collective-permute-start(bf16[96,2048]{1,0:T(8,128)(2,1)S(1)} %get-tuple-element.71), channel_id=1, source_target_pairs={{0,16},{4,20},{8,24},{12,28},{16,0},{20,4},{24,8},{28,12},{1,17},{... | collective-permute-start | bytes 1179656 | tf_op jit(solution)/shard_map/ppermute | solution.py:33
  156.4 19.7 %collective-permute-start.39 = (bf16[96,2048]{1,0:T(8,128)(2,1)S(1)}, bf16[96,2048]{1,0:T(8,128)(2,1)S(1)}, u32[]{:S(2)}, u32[]{:S(2)}) collective-permute-start(bf16[96,2048]{1,0:T(8,128)(2,1)S(1)} %get-tuple-element.67), channel_id=1, source_target_pairs={{0,16},{4,20},{8,24},{12,28},{16,0},{20,4},{24,8},{28,12},{1,17},{... | collective-permute-start | bytes 1179656 | tf_op jit(solution)/shard_map/ppermute | solution.py:33
  156.5 19.6 %collective-permute-start.40 = (bf16[96,2048]{1,0:T(8,128)(2,1)S(1)}, bf16[96,2048]{1,0:T(8,128)(2,1)S(1)}, u32[]{:S(2)}, u32[]{:S(2)}) collective-permute-start(bf16[96,2048]{1,0:T(8,128)(2,1)S(1)} %get-tuple-element.68), channel_id=1, source_target_pairs={{0,24},{4,28},{8,16},{12,20},{16,8},{20,12},{24,0},{28,4},{1,25},{... | collective-permute-start | bytes 1179656 | tf_op jit(solution)/shard_map/ppermute | solution.py:33
  159.3 17.3 %collective-permute-start.50 = (bf16[96,2048]{1,0:T(8,128)(2,1)S(1)}, bf16[96,2048]{1,0:T(8,128)(2,1)S(1)}, u32[]{:S(2)}, u32[]{:S(2)}) collective-permute-start(bf16[96,2048]{1,0:T(8,128)(2,1)S(1)} %collective-permute-done.46.refs_1_), channel_id=1, source_target_pairs={{0,4},{4,0},{8,12},{12,8},{16,20},{20,16},{24,28},{28,24},{1,5},{5... | collective-permute-start | bytes 1179656 | tf_op jit(solution)/shard_map/ppermute | solution.py:38
  159.4 17.4 %collective-permute-start.51 = (bf16[96,2048]{1,0:T(8,128)(2,1)S(1)}, bf16[96,2048]{1,0:T(8,128)(2,1)S(1)}, u32[]{:S(2)}, u32[]{:S(2)}) collective-permute-start(bf16[96,2048]{1,0:T(8,128)(2,1)S(1)} %collective-permute-done.47.refs_2_), channel_id=1, source_target_pairs={{0,4},{4,0},{8,12},{12,8},{16,20},{20,16},{24,28},{28,24},{1,5},{5... | collective-permute-start | bytes 1179656 | tf_op jit(solution)/shard_map/ppermute | solution.py:38
  167.7 18.3 %collective-permute-start.52 = (bf16[96,2048]{1,0:T(8,128)(2,1)S(1)}, bf16[96,2048]{1,0:T(8,128)(2,1)S(1)}, u32[]{:S(2)}, u32[]{:S(2)}) collective-permute-start(bf16[96,2048]{1,0:T(8,128)(2,1)S(1)} %collective-permute-done.48.refs_3_), channel_id=1, source_target_pairs={{0,4},{4,0},{8,12},{12,8},{16,20},{20,16},{24,28},{28,24},{1,5},{5... | collective-permute-start | bytes 1179656 | tf_op jit(solution)/shard_map/ppermute | solution.py:38
  176.1 18.2 %collective-permute-start.41 = (bf16[96,2048]{1,0:T(8,128)(2,1)S(1)}, bf16[96,2048]{1,0:T(8,128)(2,1)S(1)}, u32[]{:S(2)}, u32[]{:S(2)}) collective-permute-start(bf16[96,2048]{1,0:T(8,128)(2,1)S(1)} %get-tuple-element.65.refs_0_), channel_id=1, source_target_pairs={{0,4},{4,0},{8,12},{12,8},{16,20},{20,16},{24,28},{28,24},{1,5},{5... | collective-permute-start | bytes 1179656 | tf_op jit(solution)/shard_map/ppermute | solution.py:38
  176.1 18.2 %collective-permute-start.42 = (bf16[96,2048]{1,0:T(8,128)(2,1)S(1)}, bf16[96,2048]{1,0:T(8,128)(2,1)S(1)}, u32[]{:S(2)}, u32[]{:S(2)}) collective-permute-start(bf16[96,2048]{1,0:T(8,128)(2,1)S(1)} %collective-permute-done.38.refs_1_), channel_id=1, source_target_pairs={{0,4},{4,0},{8,12},{12,8},{16,20},{20,16},{24,28},{28,24},{1,5},{5... | collective-permute-start | bytes 1179656 | tf_op jit(solution)/shard_map/ppermute | solution.py:38
  176.6 17.7 %collective-permute-start.43 = (bf16[96,2048]{1,0:T(8,128)(2,1)S(1)}, bf16[96,2048]{1,0:T(8,128)(2,1)S(1)}, u32[]{:S(2)}, u32[]{:S(2)}) collective-permute-start(bf16[96,2048]{1,0:T(8,128)(2,1)S(1)} %collective-permute-done.39.refs_2_), channel_id=1, source_target_pairs={{0,4},{4,0},{8,12},{12,8},{16,20},{20,16},{24,28},{28,24},{1,5},{5... | collective-permute-start | bytes 1179656 | tf_op jit(solution)/shard_map/ppermute | solution.py:38
  176.7 17.6 %collective-permute-start.44 = (bf16[96,2048]{1,0:T(8,128)(2,1)S(1)}, bf16[96,2048]{1,0:T(8,128)(2,1)S(1)}, u32[]{:S(2)}, u32[]{:S(2)}) collective-permute-start(bf16[96,2048]{1,0:T(8,128)(2,1)S(1)} %collective-permute-done.40.refs_3_), channel_id=1, source_target_pairs={{0,4},{4,0},{8,12},{12,8},{16,20},{20,16},{24,28},{28,24},{1,5},{5... | collective-permute-start | bytes 1179656 | tf_op jit(solution)/shard_map/ppermute | solution.py:38
  211.8 31.2 %collective-permute-start.67 = (bf16[384,2048]{1,0:T(8,128)(2,1)S(1)}, bf16[384,2048]{1,0:T(8,128)(2,1)S(1)}, u32[]{:S(2)}, u32[]{:S(2)}) collective-permute-start(bf16[384,2048]{1,0:T(8,128)(2,1)S(1)} %get-tuple-element.86), channel_id=1, source_target_pairs={{0,4},{4,0},{8,12},{12,8},{16,20},{20,16},{24,28},{28,24},{1,5},{5... | collective-permute-start | bytes 4718600 | tf_op jit(solution)/shard_map/ppermute | solution.py:38
  217.2 47.0 %collective-permute-start.73 = (bf16[384,2048]{1,0:T(8,128)(2,1)S(1)}, bf16[384,2048]{1,0:T(8,128)(2,1)S(1)}, u32[]{:S(2)}, u32[]{:S(2)}) collective-permute-start(bf16[384,2048]{1,0:T(8,128)(2,1)S(1)} %get-tuple-element.91), channel_id=1, source_target_pairs={{0,4},{4,0},{8,12},{12,8},{16,20},{20,16},{24,28},{28,24},{1,5},{5... | collective-permute-start | bytes 4718600 | tf_op jit(solution)/shard_map/ppermute | solution.py:38
  219.5 19.6 %collective-permute-start.63 = (bf16[96,2048]{1,0:T(8,128)(2,1)S(1)}, bf16[96,2048]{1,0:T(8,128)(2,1)S(1)}, u32[]{:S(2)}, u32[]{:S(2)}) collective-permute-start(bf16[96,2048]{1,0:T(8,128)(2,1)S(1)} %get-tuple-element.98), channel_id=1, source_target_pairs={{0,16},{4,20},{8,24},{12,28},{16,0},{20,4},{24,8},{28,12},{1,17},{... | collective-permute-start | bytes 1179656 | tf_op jit(solution)/shard_map/ppermute | solution.py:33
  219.7 19.4 %collective-permute-start.64 = (bf16[96,2048]{1,0:T(8,128)(2,1)S(1)}, bf16[96,2048]{1,0:T(8,128)(2,1)S(1)}, u32[]{:S(2)}, u32[]{:S(2)}) collective-permute-start(bf16[96,2048]{1,0:T(8,128)(2,1)S(1)} %get-tuple-element.97), channel_id=1, source_target_pairs={{0,24},{4,28},{8,16},{12,20},{16,8},{20,12},{24,0},{28,4},{1,25},{... | collective-permute-start | bytes 1179656 | tf_op jit(solution)/shard_map/ppermute | solution.py:33
  244.2 18.2 %collective-permute-start.69 = (bf16[96,2048]{1,0:T(8,128)(2,1)S(1)}, bf16[96,2048]{1,0:T(8,128)(2,1)S(1)}, u32[]{:S(2)}, u32[]{:S(2)}) collective-permute-start(bf16[96,2048]{1,0:T(8,128)(2,1)S(1)} %get-tuple-element.102), channel_id=1, source_target_pairs={{0,16},{4,20},{8,24},{12,28},{16,0},{20,4},{24,8},{28,12},{1,17},{... | collective-permute-start | bytes 1179656 | tf_op jit(solution)/shard_map/ppermute | solution.py:33
  245.5 16.9 %collective-permute-start.70 = (bf16[96,2048]{1,0:T(8,128)(2,1)S(1)}, bf16[96,2048]{1,0:T(8,128)(2,1)S(1)}, u32[]{:S(2)}, u32[]{:S(2)}) collective-permute-start(bf16[96,2048]{1,0:T(8,128)(2,1)S(1)} %get-tuple-element.101), channel_id=1, source_target_pairs={{0,24},{4,28},{8,16},{12,20},{16,8},{20,12},{24,0},{28,4},{1,25},{... | collective-permute-start | bytes 1179656 | tf_op jit(solution)/shard_map/ppermute | solution.py:33
  249.0 19.5 %collective-permute-start.66 = (bf16[32,2048]{1,0:T(8,128)(2,1)S(1)}, bf16[32,2048]{1,0:T(8,128)(2,1)S(1)}, u32[]{:S(2)}, u32[]{:S(2)}) collective-permute-start(bf16[32,2048]{1,0:T(8,128)(2,1)S(1)} %slice.552), channel_id=1, source_target_pairs={{0,2},{1,3},{2,0},{3,1},{4,6},{5,7},{6,4},{7,5},{8,10},{9,11},{10,... | collective-permute-start | bytes 393224 | tf_op jit(solution)/shard_map/ppermute | solution.py:43
  263.8 23.1 %collective-permute-start.71 = (bf16[64,2048]{1,0:T(8,128)(2,1)S(1)}, bf16[64,2048]{1,0:T(8,128)(2,1)S(1)}, u32[]{:S(2)}, u32[]{:S(2)}) collective-permute-start(bf16[64,2048]{1,0:T(8,128)(2,1)S(1)} %get-tuple-element.89), channel_id=1, source_target_pairs={{0,1},{1,0},{2,3},{3,2},{4,5},{5,4},{6,7},{7,6},{8,9},{9,8},{10,11... | collective-permute-start | bytes 786440 | tf_op jit(solution)/shard_map/ppermute | solution.py:43
  266.6 17.4 %collective-permute-start.75 = (bf16[96,2048]{1,0:T(8,128)(2,1)S(1)}, bf16[96,2048]{1,0:T(8,128)(2,1)S(1)}, u32[]{:S(2)}, u32[]{:S(2)}) collective-permute-start(bf16[96,2048]{1,0:T(8,128)(2,1)S(1)} %get-tuple-element.106), channel_id=1, source_target_pairs={{0,16},{4,20},{8,24},{12,28},{16,0},{20,4},{24,8},{28,12},{1,17},{... | collective-permute-start | bytes 1179656 | tf_op jit(solution)/shard_map/ppermute | solution.py:33
  267.0 17.0 %collective-permute-start.76 = (bf16[96,2048]{1,0:T(8,128)(2,1)S(1)}, bf16[96,2048]{1,0:T(8,128)(2,1)S(1)}, u32[]{:S(2)}, u32[]{:S(2)}) collective-permute-start(bf16[96,2048]{1,0:T(8,128)(2,1)S(1)} %get-tuple-element.105), channel_id=1, source_target_pairs={{0,24},{4,28},{8,16},{12,20},{16,8},{20,12},{24,0},{28,4},{1,25},{... | collective-permute-start | bytes 1179656 | tf_op jit(solution)/shard_map/ppermute | solution.py:33
  (61 other events, 697.6 us)

commit v2 on v0

--- a/solution.py
+++ b/solution.py
@@ -1,13 +1,556 @@
+import functools
+
 import jax
 import jax.numpy as jnp
 from jax import lax
+from jax.experimental import pallas as pl
+from jax.experimental.pallas import tpu as pltpu
 from jax.sharding import PartitionSpec as P
 
 TOP = 2
 PAIR = 2
-
-
-def per_device(
+VMEM_LIMIT = 44 * 1024 * 1024
+EXTRA_ROWS = 16
+ROUTE_ROWS = 10
+HIGH = lax.Precision.HIGHEST
+F32 = jnp.float32
+BF16 = jnp.bfloat16
+
+
+def params():
+    return pltpu.CompilerParams(vmem_limit_bytes=VMEM_LIMIT)
+
+
+def cost(microseconds):
+    return pl.CostEstimate(flops=0, bytes_accessed=int(microseconds * 3.69e6), transcendentals=0)
+
+
+def after(array, *earlier):
+    return lax.optimization_barrier((array,) + earlier)[0]
+
+
+def swap_columns(array, distance):
+    count = lax.axis_size("seq")
+    return lax.ppermute(array, "seq", [(i, i ^ (PAIR * distance)) for i in range(count)])
+
+
+def swap_cores(array):
+    count = lax.axis_size("seq")
+    return lax.ppermute(array, "seq", [(i, i ^ 1) for i in range(count)])
+
+
+def swap_layers(array, distance):
+    count = lax.axis_size("mp")
+    return lax.ppermute(array, "mp", [(i, i ^ distance) for i in range(count)])
+
+
+def local_kernel(column_ref, q_ref, k_ref, v_ref, decay_ref, residual_ref, local_ref, weighted_ref, *message_refs):
+    span = q_ref.shape[0]
+    heads = decay_ref.shape[0]
+    size = q_ref.shape[1] // heads
+    row = lax.broadcasted_iota(jnp.int32, (span, span), 0)
+    col = lax.broadcasted_iota(jnp.int32, (span, span), 1)
+    causal = row >= col
+    decay = decay_ref[...]
+    along = jnp.dot(decay, (row <= col).astype(F32), precision=HIGH, preferred_element_type=F32)
+    down = lax.dot_general(
+        causal.astype(F32), decay, (((1,), (1,)), ((), ())), precision=HIGH, preferred_element_type=F32
+    )
+    extra = lax.broadcasted_iota(jnp.int32, (EXTRA_ROWS, size), 0)
+    for h in range(heads):
+        cols = slice(h * size, (h + 1) * size)
+        q, k, v = q_ref[:, cols], k_ref[:, cols], v_ref[:, cols]
+        here = down[:, h : h + 1]
+        spread = here - along[h : h + 1, :]
+        weight = jnp.where(causal, jnp.exp(jnp.where(causal, spread, 0.0)), 0.0)
+        raw = lax.dot_general(q, k, (((1,), (1,)), ((), ())), preferred_element_type=F32)
+        local_ref[:, cols] = jnp.dot((raw * weight).astype(BF16), v, preferred_element_type=F32)
+        total = along[h : h + 1, span - 1 : span]
+        scaled = (jnp.exp(total - here) * k.astype(F32)).astype(BF16)
+        state = lax.dot_general(scaled, v, (((0,), (0,)), ((), ())), preferred_element_type=F32).astype(BF16)
+        first = total.astype(BF16).astype(F32)
+        second = (total - first).astype(BF16).astype(F32)
+        third = total - first - second
+        pieces = jnp.where(extra == 0, first, jnp.where(extra == 1, second, jnp.where(extra == 2, third, 0.0)))
+        at = h * (size + EXTRA_ROWS)
+        for message in message_refs:
+            message[at : at + size, :] = state
+            message[at + size : at + size + EXTRA_ROWS, :] = pieces.astype(BF16)
+        weighted_ref[:, cols] = (jnp.exp(here) * q.astype(F32)).astype(BF16)
+    tok = residual_ref.shape[0]
+    first = heads * (size + EXTRA_ROWS)
+    for d, message in enumerate(message_refs):
+        parts = (message.shape[0] - first) // tok
+        for b in range(parts):
+            at = pl.multiple_of((column_ref[d] * parts + b) * size, size)
+            message[first + b * tok : first + (b + 1) * tok, :] = residual_ref[:, pl.ds(at, size)]
+
+
+def prefix_kernel(count, heads, layers, *refs):
+    row_ref, between_ref, earlier_ref, local_ref, weighted_ref, route_ref = refs[:6]
+    message_refs = refs[6 : 6 + count]
+    out_ref, totals, held = refs[6 + count :]
+    span = local_ref.shape[0]
+    size = local_ref.shape[1] // heads
+    tall = size + EXTRA_ROWS
+    for p in range(count):
+        for h in range(heads):
+            extra = message_refs[p][h * tall + size : (h + 1) * tall, :].astype(F32)
+            totals[p : p + 1, h * size : (h + 1) * size] = jnp.sum(extra, axis=0, keepdims=True)
+    gap = jnp.dot(between_ref[...], totals[...], precision=HIGH, preferred_element_type=F32)
+    totals[...] = jnp.exp(gap) * earlier_ref[...]
+    for h in range(heads):
+        cols = slice(h * size, (h + 1) * size)
+        prefix = jnp.zeros((size, size), F32)
+        for p in range(count):
+            prefix += totals[p : p + 1, cols] * message_refs[p][h * tall : h * tall + size, :].astype(F32)
+        mixed = local_ref[:, cols] + jnp.dot(
+            weighted_ref[:, cols], prefix.astype(BF16), preferred_element_type=F32
+        )
+        mean = jnp.mean(mixed * mixed, axis=-1, keepdims=True)
+        held[:, cols] = (mixed * lax.rsqrt(mean + 1e-06)).astype(BF16)
+    rows = span // layers
+    for r in range(layers):
+        start = pl.multiple_of(row_ref[r] * rows, rows)
+        out_ref[r * rows : (r + 1) * rows, :] = held[pl.ds(start, rows), :]
+    out_ref[span:, :] = jnp.zeros((EXTRA_ROWS, heads * size), BF16)
+    out_ref[span:, :span] = route_ref[...]
+
+
+def map_kernel(count, columns, capacity, tok, column_ref, *refs):
+    row_refs, (pack_ref, high_ref, low_ref) = refs[:count], refs[count:]
+    slots, span = high_ref.shape[0] // columns, high_ref.shape[1]
+    row = lax.broadcasted_iota(jnp.int32, (slots, span), 0)
+    lane = lax.broadcasted_iota(jnp.int32, (1, span), 1)
+    base = (lane // tok) * capacity
+    for p in range(count):
+        route = row_refs[p][span : span + EXTRA_ROWS, :span].astype(F32)
+        for d in range(columns):
+            expert = column_ref[d]
+            hit, gain = None, None
+            for k in range(TOP):
+                named = route[k : k + 1].astype(jnp.int32) == expert
+                rank = route[TOP + k : TOP + k + 1].astype(jnp.int32)
+                at = 2 * TOP + 3 * k
+                value = route[at : at + 1] + route[at + 1 : at + 2] + route[at + 2 : at + 3]
+                here = jnp.where(named, base + rank, -1) == row
+                weight = jnp.where(here, value, 0.0)
+                hit = here if hit is None else hit | here
+                gain = weight if gain is None else gain + weight
+            pack_ref[p, d * slots : (d + 1) * slots, :] = jnp.where(hit, 1.0, 0.0).astype(BF16)
+            if p == 0:
+                high = gain.astype(BF16)
+                high_ref[d * slots : (d + 1) * slots, :] = high
+                low_ref[d * slots : (d + 1) * slots, :] = (gain - high.astype(F32)).astype(BF16)
+
+
+def project_kernel(count, layers, tok, chunk, core_ref, *refs):
+    row_refs, message_refs = refs[:count], refs[count : 2 * count]
+    weight_ref, keep_ref, send_ref = refs[2 * count :]
+    span = layers * tok
+    rows = jnp.concatenate([ref[:span] for ref in row_refs], axis=0)
+    part = jnp.dot(rows, weight_ref[...], preferred_element_type=F32).astype(BF16)
+    lanes = message_refs[0].shape[1]
+    pieces = weight_ref.shape[1] // lanes
+    for r in range(layers):
+        for p in range(count):
+            to = (r % (layers // 2)) * count * tok + p * tok
+            here = part[p * span + r * tok : p * span + (r + 1) * tok]
+            if r >= layers // 2:
+                send_ref[to : to + tok, :] = here
+            elif r > 0:
+                keep_ref[to : to + tok, :] = here.astype(F32)
+            else:
+                for b in range(pieces):
+                    at = pl.multiple_of(core_ref[0] + (chunk * pieces + b) * tok, tok)
+                    own = message_refs[p][pl.ds(at, tok), :].astype(F32)
+                    cols = slice(b * lanes, (b + 1) * lanes)
+                    keep_ref[to : to + tok, cols] = here[:, cols].astype(F32) + own
+
+
+def pack_kernel(count, layers, place_ref, map_ref, near_ref, far_ref, *out_refs):
+    slots = out_refs[0].shape[0] // count
+    tok = near_ref.shape[0] // (layers // 2) // count
+    for p in range(count):
+        pieces = [
+            ref[r * count * tok + p * tok : r * count * tok + (p + 1) * tok, :]
+            for ref in (near_ref, far_ref)
+            for r in range(layers // 2)
+        ]
+        tokens = jnp.concatenate(pieces, axis=0)
+        packed = jnp.dot(map_ref[p], tokens, preferred_element_type=F32).astype(BF16)
+        start = pl.multiple_of(place_ref[p] * slots, slots)
+        for d in range(len(out_refs)):
+            out_refs[d][pl.ds(start, slots), :] = packed[d * slots : (d + 1) * slots]
+
+
+def expert_kernel(pieces, blocks, first, last, features, place_ref, *refs):
+    x_refs = refs[:pieces]
+    gate_refs, up_refs = refs[pieces : pieces + blocks], refs[pieces + blocks : pieces + 2 * blocks]
+    rest = refs[pieces + 2 * blocks :]
+    if not first:
+        sum_in, square_in = rest[:2]
+        rest = rest[2:]
+    if last:
+        out_ref, sum_ref, square_ref = rest
+    else:
+        sum_ref, square_ref = rest
+    size = gate_refs[0].shape[0]
+    even = size // 128 * 128
+    lanes = square_ref.shape[1]
+    step = pl.program_id(0)
+
+    for s in range(pieces // blocks):
+
+        @pl.when(step == s)
+        def _(s=s):
+            x = jnp.concatenate([ref[...] for ref in x_refs[s * blocks : (s + 1) * blocks]], axis=1)
+            gate = jnp.concatenate([ref[...] for ref in gate_refs], axis=1)
+            up = jnp.concatenate([ref[...] for ref in up_refs], axis=1)
+            both = jnp.concatenate([gate[:even], up[:even], gate[even:], up[even:]], axis=0)
+            sums = lax.dot_general(x, both, (((1,), (1,)), ((), ())), preferred_element_type=F32)
+            wide = x.astype(F32)
+            squares = wide[:, :lanes] * wide[:, :lanes]
+            for i in range(1, x.shape[1] // lanes):
+                part = wide[:, i * lanes : (i + 1) * lanes]
+                squares += part * part
+            if s > 0:
+                sum_ref[...] += sums
+                square_ref[...] += squares
+            else:
+                sum_ref[...] = sums if first else sum_in[...] + sums
+                square_ref[...] = squares if first else square_in[...] + squares
+
+    if last:
+
+        @pl.when(step == pl.num_programs(0) - 1)
+        def _():
+            slots = out_ref.shape[0] // pieces
+
+            def activate(gate, up, scale):
+                gate = gate * scale
+                return (gate / (1.0 + jnp.exp(-gate)) * (up * scale)).astype(BF16)
+
+            for p in range(pieces):
+                rows = pl.ds(pl.multiple_of(place_ref[p] * slots, slots), slots)
+                to = slice(p * slots, (p + 1) * slots)
+                mean = jnp.sum(square_ref[rows, :], axis=1, keepdims=True) / features
+                scale = lax.rsqrt(mean + 1e-06)
+                out_ref[to, :even] = activate(sum_ref[rows, :even], sum_ref[rows, even : 2 * even], scale)
+                if even < size:
+                    tail = sum_ref[rows, 2 * even :]
+                    out_ref[to, even:] = activate(tail[:, : size - even], tail[:, size - even :], scale)
+
+
+def down_kernel(hidden_ref, weight_ref, own_ref, *other_refs):
+    half = own_ref.shape[0]
+    out = jnp.dot(hidden_ref[...], weight_ref[...], preferred_element_type=F32).astype(BF16)
+    own_ref[...] = out[:half]
+    rows = half // len(other_refs)
+    for d, ref in enumerate(other_refs):
+        ref[...] = out[half + d * rows : half + (d + 1) * rows]
+
+
+def combine_kernel(count, high_ref, low_ref, *refs):
+    x_refs = refs[:count]
+    keep_ref, send_ref = refs[count:]
+    half = keep_ref.shape[0]
+    x = jnp.concatenate([ref[...] for ref in x_refs], axis=0)
+    out = lax.dot_general(high_ref[...], x, (((0,), (0,)), ((), ())), preferred_element_type=F32)
+    out += lax.dot_general(low_ref[...], x, (((0,), (0,)), ((), ())), preferred_element_type=F32)
+    keep_ref[...] = out[:half]
+    send_ref[...] = out[half:].astype(BF16)
+
+
+def whole_block(array):
+    return pl.BlockSpec(array.shape, lambda *_: (0,) * array.ndim)
+
+
+def tiled(
+    queries, keys, values, log_decay, residual, out_weight, gate_weight, up_weight, down_weight, expert_ids,
+    route_weights, chunks, returns,
+):
+    seq_count, layers = lax.axis_size("seq"), lax.axis_size("mp")
+    me, layer = lax.axis_index("seq"), lax.axis_index("mp")
+    columns = seq_count // PAIR
+    column = me // PAIR
+    span, heads = queries.shape[0], log_decay.shape[0]
+    size = queries.shape[1] // heads
+    features = residual.shape[1]
+    hidden_size = gate_weight.shape[2]
+    tok = residual.shape[0]
+    half = span // 2
+    block = out_weight.shape[1]
+    width = block // chunks
+    capacity = max(2, tok * TOP * 3 // (2 * columns))
+    slots = layers * capacity
+    distances = [1 << i for i in range((layers - 1).bit_length())]
+    order = [0]
+    for d in reversed(distances):
+        order = order + [b ^ d for b in order]
+
+    away = [PAIR * (p % columns) + p // columns for p in range(seq_count)]
+    blocks_at = jnp.stack([me ^ a for a in away]).astype(jnp.int32)
+    rows_at = jnp.stack([layer ^ r for r in order]).astype(jnp.int32)
+    columns_at = jnp.stack([column ^ d for d in range(columns)]).astype(jnp.int32)
+
+    def across(array):
+        return [array] + [swap_columns(array, d) for d in range(1, columns)]
+
+    def both_cores(arrays):
+        arrays = list(arrays)
+        return arrays + [swap_cores(a) for a in arrays]
+
+    smem = pl.BlockSpec(memory_space=pltpu.SMEM)
+    vmem = pl.BlockSpec(memory_space=pltpu.VMEM)
+    residual_at = heads * (size + EXTRA_ROWS)
+    message = (residual_at + PAIR * block // size * tok, size)
+    local_part, weighted_queries, *messages = pl.pallas_call(
+        local_kernel,
+        out_shape=(
+            jax.ShapeDtypeStruct((span, heads * size), F32),
+            jax.ShapeDtypeStruct((span, heads * size), BF16),
+        )
+        + (jax.ShapeDtypeStruct(message, BF16),) * columns,
+        grid=(1,),
+        in_specs=[smem] + [whole_block(a) for a in (queries, keys, values, log_decay, residual)],
+        out_specs=(pl.BlockSpec((span, heads * size), lambda n: (0, 0)),) * 2
+        + (pl.BlockSpec(message, lambda n: (0, 0)),) * columns,
+        compiler_params=params(),
+        cost_estimate=cost(1.5),
+        name="local_attention",
+    )(columns_at, queries, keys, values, log_decay, residual)
+    messages = [messages[0]] + [swap_columns(messages[d], d) for d in range(1, columns)]
+
+    flat = after(expert_ids, local_part).reshape(-1)
+    count = flat.shape[0]
+    before = jnp.arange(count)[:, None] > jnp.arange(count)[None, :]
+    rank = jnp.sum((before & (flat[:, None] == flat[None, :])).astype(jnp.int32), axis=1).reshape(tok, TOP)
+    first = lax.reduce_precision(route_weights, 8, 7)
+    second = lax.reduce_precision(route_weights - first, 8, 7)
+    third = route_weights - first - second
+    parts = jnp.stack([first, second, third], axis=2).reshape(tok, 3 * TOP)
+    route = jnp.concatenate([expert_ids.astype(F32), rank.astype(F32), parts], axis=1).T.astype(BF16)
+    route = jnp.pad(route, ((0, EXTRA_ROWS - ROUTE_ROWS), (0, 0)))
+    for d in reversed(distances):
+        route = jnp.concatenate([route, swap_layers(route, d)], axis=1)
+
+    messages = both_cores([after(a, route) for a in messages])
+    between = ((blocks_at[:, None] < blocks_at[None, :]) & (blocks_at[None, :] < me)).astype(F32)
+    earlier = jnp.broadcast_to((blocks_at < me).astype(F32)[:, None], (seq_count, heads * size))
+    normed = pl.pallas_call(
+        functools.partial(prefix_kernel, seq_count, heads, layers),
+        out_shape=jax.ShapeDtypeStruct((span + EXTRA_ROWS, heads * size), BF16),
+        in_specs=[smem] + [vmem] * (5 + seq_count),
+        out_specs=vmem,
+        scratch_shapes=[pltpu.VMEM((seq_count, heads * size), F32), pltpu.VMEM((span, heads * size), BF16)],
+        compiler_params=params(),
+        cost_estimate=cost(1.2),
+        name="prefix_attention",
+    )(rows_at, between, earlier, local_part, weighted_queries, route, *messages)
+    normed = both_cores(across(normed))
+
+    core = me % PAIR
+    core_at = (residual_at + core * (block // size * tok)).reshape(1).astype(jnp.int32)
+
+    def slot_maps(*earlier):
+        return pl.pallas_call(
+            functools.partial(map_kernel, seq_count, columns, capacity, tok),
+            out_shape=(
+                jax.ShapeDtypeStruct((seq_count, columns * slots, span), BF16),
+                jax.ShapeDtypeStruct((columns * slots, span), BF16),
+                jax.ShapeDtypeStruct((columns * slots, span), BF16),
+            ),
+            in_specs=[smem] + [vmem] * seq_count,
+            out_specs=(vmem,) * 3,
+            compiler_params=params(),
+            cost_estimate=cost(1.3),
+            name="slot_maps",
+        )(columns_at, after(normed[0], *earlier), *normed[1:])
+
+    rows = seq_count * slots
+    summed_rows = seq_count * half
+    gate_view, up_view = gate_weight[0].T, up_weight[0].T
+
+    def project(i, *earlier):
+        keep, send = pl.pallas_call(
+            functools.partial(project_kernel, seq_count, layers, tok, i),
+            grid=(1,),
+            out_shape=(
+                jax.ShapeDtypeStruct((summed_rows, width), F32),
+                jax.ShapeDtypeStruct((summed_rows, width), BF16),
+            ),
+            in_specs=[smem] + [whole_block(a) for a in (*normed, *messages)]
+            + [pl.BlockSpec((heads * size, width), lambda n: (0, i))],
+            out_specs=(pl.BlockSpec((summed_rows, width), lambda n: (0, 0)),) * 2,
+            compiler_params=params(),
+            cost_estimate=cost(1),
+            name="project",
+        )(core_at, after(normed[0], *earlier), *normed[1:], *messages, out_weight)
+        return keep, swap_layers(send, distances[0])
+
+    def sum_layers(keep, arrived):
+        part = (keep + arrived.astype(F32)).astype(BF16)
+        return part, swap_layers(part, distances[-1])
+
+    def add_layers(part, other):
+        middle = other.shape[0] // 2
+        other = jnp.concatenate([other[middle:], other[:middle]], axis=0)
+        token = (part.astype(F32) + other.astype(F32)).astype(BF16)
+        return token, swap_layers(token, distances[0])
+
+    def dispatch(token, far):
+        packed = pl.pallas_call(
+            functools.partial(pack_kernel, seq_count, layers),
+            out_shape=(jax.ShapeDtypeStruct((rows, width), BF16),) * columns,
+            in_specs=[smem] + [vmem] * 3,
+            out_specs=(vmem,) * columns,
+            compiler_params=params(),
+            cost_estimate=cost(1),
+            name="pack",
+        )(blocks_at, pack_map, token, far)
+        return [packed[0]] + [swap_columns(packed[d], d) for d in range(1, columns)]
+
+    blocks = columns
+    sum_shapes = ((rows, 2 * hidden_size), (rows, 128))
+
+    def gate_up(i, arrived, held):
+        first, last = i == 0, i == chunks - 1
+
+        def weight_block(b):
+            return pl.BlockSpec((hidden_size, width), lambda s, at: (0, at[s * blocks + b] * chunks + i))
+
+        def constant(shape):
+            return pl.BlockSpec(shape, lambda s, at: (0, 0))
+
+        return pl.pallas_call(
+            functools.partial(expert_kernel, seq_count, blocks, first, last, features),
+            grid_spec=pltpu.PrefetchScalarGridSpec(
+                num_scalar_prefetch=1,
+                grid=(seq_count // blocks,),
+                in_specs=[constant((rows, width))] * seq_count
+                + [weight_block(b) for b in range(blocks)] * 2
+                + [vmem] * len(held),
+                out_specs=constant((rows, hidden_size)) if last else (vmem, vmem),
+                scratch_shapes=[pltpu.VMEM(s, F32) for s in sum_shapes] if last else [],
+            ),
+            out_shape=jax.ShapeDtypeStruct((rows, hidden_size), BF16)
+            if last
+            else tuple(jax.ShapeDtypeStruct(s, F32) for s in sum_shapes),
+            compiler_params=params(),
+            cost_estimate=cost(24 / chunks),
+            name="gate_up",
+        )(blocks_at, *arrived, *[gate_view] * blocks, *[up_view] * blocks, *held)
+
+    projected, sent, tokens, arrived, sums = [None] * chunks, [None] * chunks, [None] * chunks, [None] * chunks, []
+    projected[0] = project(0)
+    sent[0] = sum_layers(*projected[0])
+    pack_map, mix_high, mix_low = slot_maps(sent[0][0])
+    for i in range(chunks):
+        if i + 1 < chunks:
+            projected[i + 1] = project(i + 1, sent[i][0])
+        if i == chunks - 1:
+            both = both_cores(after(a, sent[i][0]) for a in arrived[0])
+            sums = gate_up(0, both, sums)
+            sent[i] = (after(sent[i][0], *sums), sent[i][1])
+        tokens[i] = add_layers(*sent[i])
+        if i + 1 < chunks:
+            sent[i + 1] = sum_layers(*projected[i + 1])
+        arrived[i] = dispatch(*tokens[i])
+    for i in range(1, chunks):
+        sums = gate_up(i, both_cores([after(a, *sums) for a in arrived[i]]), sums)
+
+    middle = summed_rows // 2
+    own = jnp.concatenate([token[:middle] for token, _ in tokens], axis=1)
+    other = swap_cores(own[middle // 2 :])
+    own = own[: middle // 2]
+    joined = jnp.where(core == 0, jnp.concatenate([own, other], axis=1), jnp.concatenate([other, own], axis=1))
+    expert_hidden = sums
+    tile = 512
+
+    def down(piece, *earlier):
+        offset, out_width = piece
+        own, *other = pl.pallas_call(
+            down_kernel,
+            grid=(out_width // tile,),
+            out_shape=(jax.ShapeDtypeStruct((rows // 2, out_width), BF16),)
+            + (jax.ShapeDtypeStruct((slots, out_width), BF16),) * columns,
+            in_specs=[
+                whole_block(expert_hidden),
+                pl.BlockSpec((hidden_size, tile), lambda n: (0, offset // tile + n)),
+            ],
+            out_specs=(pl.BlockSpec((rows // 2, tile), lambda n: (0, n)),)
+            + (pl.BlockSpec((slots, tile), lambda n: (0, n)),) * columns,
+            compiler_params=params(),
+            cost_estimate=cost(16 * out_width / features),
+            name="down",
+        )(after(expert_hidden, *earlier), down_weight[0])
+        return own, [swap_cores(a) for a in other]
+
+    def summed(own, other, *earlier):
+        own = after(own, *earlier)
+        return [
+            (own[d * slots : (d + 1) * slots].astype(F32) + other[d].astype(F32)).astype(BF16)
+            for d in range(columns)
+        ]
+
+    def combine(piece, back):
+        out_width = piece[1]
+        keep, send = pl.pallas_call(
+            functools.partial(combine_kernel, columns),
+            grid=(out_width // tile,),
+            out_shape=(
+                jax.ShapeDtypeStruct((half, out_width), F32),
+                jax.ShapeDtypeStruct((half, out_width), BF16),
+            ),
+            in_specs=[whole_block(mix_high), whole_block(mix_low)]
+            + [pl.BlockSpec((slots, tile), lambda n: (0, n))] * columns,
+            out_specs=(pl.BlockSpec((half, tile), lambda n: (0, n)),) * 2,
+            compiler_params=params(),
+            cost_estimate=cost(1),
+            name="combine",
+        )(mix_high, mix_low, *back)
+        return keep, swap_layers(send, distances[0])
+
+    def layer_sum(keep, arrived):
+        part = keep + arrived.astype(F32)
+        kept = part.shape[0] // 2
+        return part[:kept], swap_layers(part[kept:].astype(BF16), distances[-1])
+
+    def finish(piece, part, arrived):
+        mine = own_hidden[:, piece[0] : piece[0] + piece[1]].astype(F32)
+        return (mine + (part + arrived.astype(F32))).astype(BF16)
+
+    sent, mixed, last = [], [], []
+    ahead = down(returns[0])
+    joined = after(joined, ahead[0])
+    joined = [joined[d * tok : (d + 1) * tok] for d in range(columns)]
+    ahead = (after(ahead[0], *joined), ahead[1])
+    joined = [joined[0]] + [swap_columns(joined[d], d) for d in range(1, columns)]
+    for i, piece in enumerate(returns):
+        earlier = sent[i - 1] + (joined if i == 1 else []) if i else []
+        sums = summed(*ahead, *earlier)
+        if i + 1 < len(returns):
+            ahead = down(returns[i + 1], *sums)
+        if i:
+            mixed.append(combine(returns[i - 1], [after(a, *sums) for a in sent[i - 1]]))
+        sent.append([sums[0]] + [swap_columns(sums[d], d) for d in range(1, columns)])
+    earlier = []
+    for i in range(len(returns) - 1):
+        last.append(layer_sum(mixed[i][0], after(mixed[i][1], *earlier)))
+        earlier = [last[i][1]] if i + 2 < len(returns) else [last[i][0]]
+    mixed.append(combine(returns[-1], [after(a, *earlier) for a in sent[-1]]))
+    last.append(layer_sum(*mixed[-1]))
+
+    joined = jnp.concatenate(joined, axis=0)
+    own_hidden = jnp.concatenate(
+        [lax.dynamic_slice_in_dim(joined, columns_at[d] * tok, tok, 0) for d in range(columns)], axis=1
+    )
+    outputs = [finish(piece, *last[i]) for i, piece in enumerate(returns)]
+    return jnp.concatenate(outputs, axis=1)
+
+
+def general(
     queries,
     keys,
     values,
@@ -137,6 +680,16 @@
     return (hidden_wide + expert_mix).astype(jnp.bfloat16)
 
 
+def cuts(tile, parts):
+    return [(sum(parts[:i]) * tile, part * tile) for i, part in enumerate(parts)]
+
+
+def fits(mesh, tok, features, block, chunks):
+    layers, seq_count = mesh.shape["mp"], mesh.shape["seq"]
+    powers = seq_count & (seq_count - 1) == 0 and seq_count > PAIR
+    return powers and layers == 4 and tok % 16 == 0 and block % (128 * chunks) == 0 and features % (512 * 12) == 0
+
+
 def solution(mesh):
     placed = (
         P("seq", "mp"),
@@ -151,6 +704,15 @@
         P(("seq", "mp"), None),
         P(("seq", "mp"), None),
     )
+    chunks = 3
+
+    def per_device(*args):
+        residual, out_weight = args[4], args[5]
+        features, block = residual.shape[1], out_weight.shape[1]
+        if fits(mesh, residual.shape[0], features, block, chunks):
+            return tiled(*args, chunks=chunks, returns=cuts(features // 12, [2, 4, 4, 2]))
+        return general(*args)
+
     return jax.shard_map(
         per_device, mesh=mesh, in_specs=placed, out_specs=P(("seq", "mp"), None), check_vma=False
     )

time: 557 us -> 268 us (0.48)
  waiting for transfers between devices: 440 us -> 100 us
  starting transfers between devices: 3.95 us -> 84.9 us
  Pallas kernels: 0 us -> 55 us
  blocking collectives: 48.1 us -> 0 us
  matrix products: 41.4 us -> 0 us
  local copies, waits for them, and re-layouts: 3.68 us -> 17.4 us
  between operations: 14 us -> 0.77 us
    all_gather x3 -> x0, waiting for transfers between devices: 216 us -> none  [the longest x1 164 us: per_device(): shard_piece = lax.all_gather(expert_rows, 'mp', axis=0, tiled=True)]
    reduce_scatter x2 -> x0, waiting for transfers between devices: 194 us -> none  [the longest x1 160 us: per_device(): lax.psum_scatter(jnp.dot(hidden_rows, down_matrix, preferred_element_type...]
    ppermute x0 -> x86, waiting for transfers between devices: none -> 100 us  [the longest x19 51.3 us: swap_layers(): return lax.ppermute(array, 'mp', [(i, i ^ distance) for i in range(count)])]
    ppermute x0 -> x86, starting transfers between devices: none -> 84.9 us  [the longest x19 42.6 us: swap_layers(): return lax.ppermute(array, 'mp', [(i, i ^ distance) for i in range(count)])]
    pallas_call x0 -> x20, Pallas kernels: none -> 55 us  [the longest x3 25.8 us: gate_up(): pl.pallas_call(functools.partial(expert_kernel, seq_count, blocks, first,...]
    dot_general x10 -> x0, matrix products: 41.4 us -> none  [the longest x1 11 us: per_device(): lifted = jnp.dot(shard_piece, up_matrix, preferred_element_type=jnp.float32)]
    all_to_all x1 -> x0, blocking collectives: 33 us -> none  [per_device(): lax.all_to_all(outgoing, 'seq', split_axis=0, concat_axis=0, tiled=True)]
    all_to_all x1 -> x0, waiting for transfers between devices: 29 us -> none  [per_device(): lax.all_to_all(half_out.reshape(seq_count, capacity, model_width), 'seq',...]
  transfers between devices with their start and end apart: 6 -> 86, of which waited for: 6 -> 42; matrix products, arithmetic and copies ran while one was open for 1% -> 4% of each run, Pallas kernels for 0% -> 14%
where the time goes in v2:
time: 268 us; the launch traced here: 267 us
  waiting for transfers between devices  100 us (37%)
  starting transfers between devices  84.9 us (32%)
  Pallas kernels  55 us (21%)
  local copies, waits for them, and re-layouts  17.4 us (6%)
  other arithmetic  9.11 us (3%)
    ppermute x19, waiting for transfers between devices, swap_layers(): return lax.ppermute(array, 'mp', [(i, i ^ distance) for i in range(count)])  51.3 us
    ppermute x30, waiting for transfers between devices, swap_columns(): lax.ppermute(array, 'seq', [(i, i ^ PAIR * distance) for i in range(count)])  43.1 us
    ppermute x19, starting transfers between devices, swap_layers(): return lax.ppermute(array, 'mp', [(i, i ^ distance) for i in range(count)])  42.6 us
    ppermute x30, starting transfers between devices, swap_columns(): lax.ppermute(array, 'seq', [(i, i ^ PAIR * distance) for i in range(count)])  35.4 us
    pallas_call x3, Pallas kernels, gate_up(): pl.pallas_call(functools.partial(expert_kernel, seq_count, blocks, first,...  25.8 us
    unnamed x58, local copies, waits for them, and re-layouts  14 us
    pallas_call x4, Pallas kernels, down(): pl.pallas_call(down_kernel, grid=(out_width // tile,), out_shape=(jax.Sha...  12.9 us
    ppermute x37, starting transfers between devices, swap_cores(): return lax.ppermute(array, 'seq', [(i, i ^ 1) for i in range(count)])  6.93 us
  transfers between devices with their start and end apart: 86, of which 42 were waited for; matrix products, arithmetic and copies ran while one was open for 4% of the time, Pallas kernels for 14%

profile of v2, /device:TPU:0, one launch (start us, length us, event | category | flops | bytes accessed | tf_op | source)
XLA Modules:
  0.0 267.2 jit_solution(1611837032690545424)
XLA Ops:
  6.0 4.0 %collective-permute-start.4 = (bf16[960,128]{1,0:T(8,128)(2,1)S(1)}, bf16[960,128]{1,0:T(8,128)(2,1)S(1)}, u32[]{:S(2)}, u32[]{:S(2)}) collective-permute-start(bf16[960,128]{1,0:T(8,128)(2,1)S(1)} %get-tuple-element.119), channel_id=1, source_target_pairs={{0,24},{4,28},{8,16},{12,20},{16,8},{20,12},{24,0},{28,4},{1,25},{... | collective-permute-start | bytes 737288 | tf_op jit(solution)/shard_map/ppermute | solution.py:34
  12.7 2.7 collective-permute-start
  29.2 3.2 %collective-permute-done.9.refs_1_ = bf16[144,512]{1,0:T(8,128)(2,1)S(1)} collective-permute-done((bf16[144,512]{1,0:T(8,128)(2,1)S(1)}, bf16[144,512]{1,0:T(8,128)(2,1)S(1)}, u32[]{:S(2)}, u32[]{:S(2)}) %collective-permute-start.9) | collective-permute-done | bytes 147488 | tf_op jit(solution)/shard_map/ppermute | solution.py:34
  32.9 2.7 collective-permute-done.11.refs_3_
  40.2 6.8 %collective-permute-done.16 = bf16[512,256]{1,0:T(8,128)(2,1)S(1)} collective-permute-done((bf16[512,256]{1,0:T(8,128)(2,1)S(1)}, bf16[512,256]{1,0:T(8,128)(2,1)S(1)}, u32[]{:S(2)}, u32[]{:S(2)}) %collective-permute-start.16) | collective-permute-done | bytes 262176 | tf_op jit(solution)/shard_map/ppermute | solution.py:44
  47.1 2.3 collective-permute-start.17
  52.5 8.7 %collective-permute-done.17 = bf16[512,256]{1,0:T(8,128)(2,1)S(1)} collective-permute-done((bf16[512,256]{1,0:T(8,128)(2,1)S(1)}, bf16[512,256]{1,0:T(8,128)(2,1)S(1)}, u32[]{:S(2)}, u32[]{:S(2)}) %collective-permute-start.17) | collective-permute-done | bytes 262176 | tf_op jit(solution)/shard_map/ppermute | solution.py:44
  65.1 2.5 collective-permute-start.19
  68.9 7.4 %collective-permute-done.21.far_ref = bf16[512,256]{1,0:T(8,128)(2,1)S(1)} collective-permute-done((bf16[512,256]{1,0:T(8,128)(2,1)S(1)}, bf16[512,256]{1,0:T(8,128)(2,1)S(1)}, u32[]{:S(2)}, u32[]{:S(2)}) %collective-permute-start.21) | collective-permute-done | bytes 262176 | tf_op jit(solution)/shard_map/ppermute | solution.py:44
  77.4 2.4 collective-permute-start.24
  83.2 3.1 %collective-permute-done.24.refs_3_ = bf16[768,256]{1,0:T(8,128)(2,1)S(1)} collective-permute-done((bf16[768,256]{1,0:T(8,128)(2,1)S(1)}, bf16[768,256]{1,0:T(8,128)(2,1)S(1)}, u32[]{:S(2)}, u32[]{:S(2)}) %collective-permute-start.24) | collective-permute-done | bytes 393248 | tf_op jit(solution)/shard_map/ppermute | solution.py:34
  86.3 5.5 %collective-permute-start.29 = (bf16[512,256]{1,0:T(8,128)(2,1)S(1)}, bf16[512,256]{1,0:T(8,128)(2,1)S(1)}, u32[]{:S(2)}, u32[]{:S(2)}) collective-permute-start(bf16[512,256]{1,0:T(8,128)(2,1)S(1)} %add_convert_fusion.9), channel_id=1, source_target_pairs={{0,2},{1,3},{2,0},{3,1},{4,6},{5,7},{6,4},{7,5},{8,10},{9,11},{10,... | collective-permute-start | bytes 786440 | tf_op jit(solution)/shard_map/ppermute | solution.py:44
  93.9 6.1 %collective-permute-done.29 = bf16[512,256]{1,0:T(8,128)(2,1)S(1)} collective-permute-done((bf16[512,256]{1,0:T(8,128)(2,1)S(1)}, bf16[512,256]{1,0:T(8,128)(2,1)S(1)}, u32[]{:S(2)}, u32[]{:S(2)}) %collective-permute-start.29) | collective-permute-done | bytes 262176 | tf_op jit(solution)/shard_map/ppermute | solution.py:44
  103.6 7.2 %gate_up.3 = (f32[768,1152]{1,0:T(8,128)S(1)}, f32[768,128]{1,0:T(8,128)S(1)}) custom-call(s32[8]{0:T(128)S(1)} %stack.86.place_ref, bf16[768,256]{1,0:T(8,128)(2,1)S(1)} %get-tuple-element.131.refs_0_, bf16[768,256]{1,0:T(8,128)(2,1)S(1)} %collective-permute-done.22.refs_1_, bf16[768,256]{1,0:T(8,128)(2,1)S(1)} %collective-permute-done.23.refs_2_, ...), custom_call_target="tpu_custom_call" | custom-call | bytes 29520000 | tf_op jit(solution)/shard_map/gate_up/pallas_call | solution.py:426
  110.8 4.0 %collective-permute-done.34.refs_2_ = bf16[768,256]{1,0:T(8,128)(2,1)S(1)} collective-permute-done((bf16[768,256]{1,0:T(8,128)(2,1)S(1)}, bf16[768,256]{1,0:T(8,128)(2,1)S(1)}, u32[]{:S(2)}, u32[]{:S(2)}) %collective-permute-start.34) | collective-permute-done | bytes 393248 | tf_op jit(solution)/shard_map/ppermute | solution.py:34
  117.6 6.3 %collective-permute-done.31.far_ref = bf16[512,256]{1,0:T(8,128)(2,1)S(1)} collective-permute-done((bf16[512,256]{1,0:T(8,128)(2,1)S(1)}, bf16[512,256]{1,0:T(8,128)(2,1)S(1)}, u32[]{:S(2)}, u32[]{:S(2)}) %collective-permute-start.31) | collective-permute-done | bytes 262176 | tf_op jit(solution)/shard_map/ppermute | solution.py:44
  129.4 8.7 %gate_up.4 = (f32[768,1152]{1,0:T(8,128)S(1)}, f32[768,128]{1,0:T(8,128)S(1)}) custom-call(s32[8]{0:T(128)S(1)} %stack.86.place_ref, bf16[768,256]{1,0:T(8,128)(2,1)S(1)} %get-tuple-element.143.refs_0_, bf16[768,256]{1,0:T(8,128)(2,1)S(1)} %collective-permute-done.33.refs_1_, bf16[768,256]{1,0:T(8,128)(2,1)S(1)} %collective-permute-done.34.refs_2_, ...), custom_call_target="tpu_custom_call" | custom-call | bytes 29520000 | tf_op jit(solution)/shard_map/gate_up/pallas_call | solution.py:426
  141.2 4.3 %collective-permute-done.41.refs_2_ = bf16[768,256]{1,0:T(8,128)(2,1)} collective-permute-done((bf16[768,256]{1,0:T(8,128)(2,1)S(1)}, bf16[768,256]{1,0:T(8,128)(2,1)}, u32[]{:S(2)}, u32[]{:S(2)}) %collective-permute-start.41) | collective-permute-done | bytes 393248 | tf_op jit(solution)/shard_map/ppermute | solution.py:34
  151.4 9.9 %gate_up.5.hidden_ref = bf16[768,576]{1,0:T(8,128)(2,1)S(1)} custom-call(s32[8]{0:T(128)S(1)} %stack.86.place_ref, bf16[768,256]{1,0:T(8,128)(2,1)S(1)} %get-tuple-element.152.refs_0_, bf16[768,256]{1,0:T(8,128)(2,1)} %collective-permute-done.40.refs_1_, bf16[768,256]{1,0:T(8,128)(2,1)} %collective-permute-done.41.refs_2_, ...), custom_call_target="tpu_custom_call" | custom-call | bytes 29520000 | tf_op jit(solution)/shard_map/gate_up/pallas_call | solution.py:426
  171.1 4.7 %down.5 = (bf16[384,2048]{1,0:T(8,128)(2,1)S(1)}, bf16[96,2048]{1,0:T(8,128)(2,1)S(1)}, bf16[96,2048]{1,0:T(8,128)(2,1)S(1)}, bf16[96,2048]{1,0:T(8,128)(2,1)S(1)}, bf16[96,2048]{1,0:T(8,128)(2,1)S(1)}) custom-call(bf16[768,576]{1,0:T(8,128)(2,1)S(1)} %gate_up.5.hidden_ref, bf16[576,6144]{1,0:T(8,128)(2,1)} %bitcast.34), custom_call_target="tpu_custom_call" | custom-call | bytes 19680000 | tf_op jit(solution)/shard_map/down/pallas_call | solution.py:473
  180.0 5.8 %collective-permute-done.56.refs_3_ = bf16[96,1024]{1,0:T(8,128)(2,1)S(1)} collective-permute-done((bf16[96,1024]{1,0:T(8,128)(2,1)S(1)}, bf16[96,1024]{1,0:T(8,128)(2,1)S(1)}, u32[]{:S(2)}, u32[]{:S(2)}) %collective-permute-start.56) | collective-permute-done | bytes 196640 | tf_op jit(solution)/shard_map/ppermute | solution.py:34
  190.1 4.7 %down.6 = (bf16[384,2048]{1,0:T(8,128)(2,1)S(1)}, bf16[96,2048]{1,0:T(8,128)(2,1)S(1)}, bf16[96,2048]{1,0:T(8,128)(2,1)S(1)}, bf16[96,2048]{1,0:T(8,128)(2,1)S(1)}, bf16[96,2048]{1,0:T(8,128)(2,1)S(1)}) custom-call(bf16[768,576]{1,0:T(8,128)(2,1)S(1)} %gate_up.5.hidden_ref, bf16[576,6144]{1,0:T(8,128)(2,1)} %bitcast.35), custom_call_target="tpu_custom_call" | custom-call | bytes 19680000 | tf_op jit(solution)/shard_map/down/pallas_call | solution.py:473
  195.4 3.2 %collective-permute-done.63.refs_1_ = bf16[96,2048]{1,0:T(8,128)(2,1)S(1)} collective-permute-done((bf16[96,2048]{1,0:T(8,128)(2,1)S(1)}, bf16[96,2048]{1,0:T(8,128)(2,1)S(1)}, u32[]{:S(2)}, u32[]{:S(2)}) %collective-permute-start.63) | collective-permute-done | bytes 393248 | tf_op jit(solution)/shard_map/ppermute | solution.py:34
  198.6 5.5 %collective-permute-done.64.refs_2_ = bf16[96,2048]{1,0:T(8,128)(2,1)S(1)} collective-permute-done((bf16[96,2048]{1,0:T(8,128)(2,1)S(1)}, bf16[96,2048]{1,0:T(8,128)(2,1)S(1)}, u32[]{:S(2)}, u32[]{:S(2)}) %collective-permute-start.64) | collective-permute-done | bytes 393248 | tf_op jit(solution)/shard_map/ppermute | solution.py:34
  205.1 3.0 %collective-permute-start.61 = (bf16[64,1024]{1,0:T(8,128)(2,1)S(1)}, bf16[64,1024]{1,0:T(8,128)(2,1)S(1)}, u32[]{:S(2)}, u32[]{:S(2)}) collective-permute-start(bf16[64,1024]{1,0:T(8,128)(2,1)S(1)} %get-tuple-element.180), channel_id=1, source_target_pairs={{0,1},{1,0},{2,3},{3,2},{4,5},{5,4},{6,7},{7,6},{8,9},{9,8},{10,11... | collective-permute-start | bytes 393224 | tf_op jit(solution)/shard_map/ppermute | solution.py:44
  217.0 6.8 %collective-permute-start.62 = (bf16[32,1024]{1,0:T(8,128)(2,1)}, bf16[32,1024]{1,0:T(8,128)(2,1)}, u32[]{:S(2)}, u32[]{:S(2)}) collective-permute-start(bf16[32,1024]{1,0:T(8,128)(2,1)} %slice.240), channel_id=1, source_target_pairs={{0,2},{1,3},{2,0},{3,1},{4,6},{5,7},{6,4},{7,5},{8,10},{9,11},{10,... | collective-permute-start | bytes 196616 | tf_op jit(solution)/shard_map/ppermute | solution.py:44
  223.8 3.0 %copy-done = bf16[1,576,6144]{2,1,0:T(8,128)(2,1)S(1)} copy-done((bf16[1,576,6144]{2,1,0:T(8,128)(2,1)S(1)}, bf16[1,576,6144]{2,1,0:T(8,128)(2,1)}, u32[]{:S(2)}) %copy-start) | copy-done | bytes 7077912
  235.3 4.7 %collective-permute-start.71 = (bf16[32,2048]{1,0:T(8,128)(2,1)S(1)}, bf16[32,2048]{1,0:T(8,128)(2,1)S(1)}, u32[]{:S(2)}, u32[]{:S(2)}) collective-permute-start(bf16[32,2048]{1,0:T(8,128)(2,1)S(1)} %slice.238), channel_id=1, source_target_pairs={{0,2},{1,3},{2,0},{3,1},{4,6},{5,7},{6,4},{7,5},{8,10},{9,11},{10,... | collective-permute-start | bytes 393224 | tf_op jit(solution)/shard_map/ppermute | solution.py:44
  244.4 4.6 %collective-permute-done.83.refs_3_ = bf16[96,1024]{1,0:T(8,128)(2,1)S(1)} collective-permute-done((bf16[96,1024]{1,0:T(8,128)(2,1)S(1)}, bf16[96,1024]{1,0:T(8,128)(2,1)S(1)}, u32[]{:S(2)}, u32[]{:S(2)}) %collective-permute-start.83) | collective-permute-done | bytes 196640 | tf_op jit(solution)/shard_map/ppermute | solution.py:34
  248.9 2.7 %collective-permute-done.82.refs_2_ = bf16[96,1024]{1,0:T(8,128)(2,1)S(1)} collective-permute-done((bf16[96,1024]{1,0:T(8,128)(2,1)S(1)}, bf16[96,1024]{1,0:T(8,128)(2,1)S(1)}, u32[]{:S(2)}, u32[]{:S(2)}) %collective-permute-start.82) | collective-permute-done | bytes 196640 | tf_op jit(solution)/shard_map/ppermute | solution.py:34
  254.5 4.0 %collective-permute-done.84 = bf16[64,1024]{1,0:T(8,128)(2,1)S(1)} collective-permute-done((bf16[64,1024]{1,0:T(8,128)(2,1)S(1)}, bf16[64,1024]{1,0:T(8,128)(2,1)S(1)}, u32[]{:S(2)}, u32[]{:S(2)}) %collective-permute-start.84) | collective-permute-done | bytes 131104 | tf_op jit(solution)/shard_map/ppermute | solution.py:44
  260.2 4.0 %collective-permute-done.80 = bf16[32,2048]{1,0:T(8,128)(2,1)S(1)} collective-permute-done((bf16[32,2048]{1,0:T(8,128)(2,1)S(1)}, bf16[32,2048]{1,0:T(8,128)(2,1)S(1)}, u32[]{:S(2)}, u32[]{:S(2)}) %collective-permute-start.80) | collective-permute-done | bytes 131104 | tf_op jit(solution)/shard_map/ppermute | solution.py:44
  (274 shorter events, 112.1 us)
Async XLA Ops:
  6.0 15.0 %collective-permute-start.4 = (bf16[960,128]{1,0:T(8,128)(2,1)S(1)}, bf16[960,128]{1,0:T(8,128)(2,1)S(1)}, u32[]{:S(2)}, u32[]{:S(2)}) collective-permute-start(bf16[960,128]{1,0:T(8,128)(2,1)S(1)} %get-tuple-element.119), channel_id=1, source_target_pairs={{0,24},{4,28},{8,16},{12,20},{16,8},{20,12},{24,0},{28,4},{1,25},{... | collective-permute-start | bytes 737288 | tf_op jit(solution)/shard_map/ppermute | solution.py:34
  47.1 14.2 %collective-permute-start.17 = (bf16[512,256]{1,0:T(8,128)(2,1)S(1)}, bf16[512,256]{1,0:T(8,128)(2,1)S(1)}, u32[]{:S(2)}, u32[]{:S(2)}) collective-permute-start(bf16[512,256]{1,0:T(8,128)(2,1)S(1)} %add_convert_fusion.13), channel_id=1, source_target_pairs={{0,2},{1,3},{2,0},{3,1},{4,6},{5,7},{6,4},{7,5},{8,10},{9,11},{10,... | collective-permute-start | bytes 786440 | tf_op jit(solution)/shard_map/ppermute | solution.py:44
  50.9 12.0 %collective-permute-start.18 = (bf16[512,256]{1,0:T(8,128)(2,1)S(1)}, bf16[512,256]{1,0:T(8,128)(2,1)S(1)}, u32[]{:S(2)}, u32[]{:S(2)}) collective-permute-start(bf16[512,256]{1,0:T(8,128)(2,1)S(1)} %get-tuple-element.125), channel_id=1, source_target_pairs={{0,1},{1,0},{2,3},{3,2},{4,5},{5,4},{6,7},{7,6},{8,9},{9,8},{10,11... | collective-permute-start | bytes 786440 | tf_op jit(solution)/shard_map/ppermute | solution.py:44
  61.4 14.9 %collective-permute-start.21 = (bf16[512,256]{1,0:T(8,128)(2,1)S(1)}, bf16[512,256]{1,0:T(8,128)(2,1)S(1)}, u32[]{:S(2)}, u32[]{:S(2)}) collective-permute-start(bf16[512,256]{1,0:T(8,128)(2,1)S(1)} %add_convert_fusion.12.near_ref), channel_id=1, source_target_pairs={{0,1},{1,0},{2,3},{3,2},{4,5},{5,4},{6,7},{7,6},{8,9},{9,8},{10,11... | collective-permute-start | bytes 786440 | tf_op jit(solution)/shard_map/ppermute | solution.py:44
  64.4 16.5 %collective-permute-start.20 = (bf16[512,256]{1,0:T(8,128)(2,1)S(1)}, bf16[512,256]{1,0:T(8,128)(2,1)S(1)}, u32[]{:S(2)}, u32[]{:S(2)}) collective-permute-start(bf16[512,256]{1,0:T(8,128)(2,1)S(1)} %get-tuple-element.128), channel_id=1, source_target_pairs={{0,1},{1,0},{2,3},{3,2},{4,5},{5,4},{6,7},{7,6},{8,9},{9,8},{10,11... | collective-permute-start | bytes 786440 | tf_op jit(solution)/shard_map/ppermute | solution.py:44
  65.1 16.0 %collective-permute-start.19 = (bf16[512,256]{1,0:T(8,128)(2,1)S(1)}, bf16[512,256]{1,0:T(8,128)(2,1)S(1)}, u32[]{:S(2)}, u32[]{:S(2)}) collective-permute-start(bf16[512,256]{1,0:T(8,128)(2,1)S(1)} %add_convert_fusion.11), channel_id=1, source_target_pairs={{0,2},{1,3},{2,0},{3,1},{4,6},{5,7},{6,4},{7,5},{8,10},{9,11},{10,... | collective-permute-start | bytes 786440 | tf_op jit(solution)/shard_map/ppermute | solution.py:44
  79.8 12.0 %collective-permute-start.23 = (bf16[768,256]{1,0:T(8,128)(2,1)S(1)}, bf16[768,256]{1,0:T(8,128)(2,1)S(1)}, u32[]{:S(2)}, u32[]{:S(2)}) collective-permute-start(bf16[768,256]{1,0:T(8,128)(2,1)S(1)} %get-tuple-element.134), channel_id=1, source_target_pairs={{0,16},{4,20},{8,24},{12,28},{16,0},{20,4},{24,8},{28,12},{1,17},{... | collective-permute-start | bytes 1179656 | tf_op jit(solution)/shard_map/ppermute | solution.py:34
  81.0 20.4 %collective-permute-start.25 = (bf16[768,256]{1,0:T(8,128)(2,1)S(1)}, bf16[768,256]{1,0:T(8,128)(2,1)S(1)}, u32[]{:S(2)}, u32[]{:S(2)}) collective-permute-start(bf16[768,256]{1,0:T(8,128)(2,1)S(1)} %get-tuple-element.131.refs_0_), channel_id=1, source_target_pairs={{0,4},{4,0},{8,12},{12,8},{16,20},{20,16},{24,28},{28,24},{1,5},{5... | collective-permute-start | bytes 1179656 | tf_op jit(solution)/shard_map/ppermute | solution.py:39
  81.2 11.6 %collective-permute-start.32 = (bf16[512,256]{1,0:T(8,128)(2,1)S(1)}, bf16[512,256]{1,0:T(8,128)(2,1)S(1)}, u32[]{:S(2)}, u32[]{:S(2)}) collective-permute-start(bf16[512,256]{1,0:T(8,128)(2,1)S(1)} %add_convert_fusion.10.near_ref), channel_id=1, source_target_pairs={{0,1},{1,0},{2,3},{3,2},{4,5},{5,4},{6,7},{7,6},{8,9},{9,8},{10,11... | collective-permute-start | bytes 786440 | tf_op jit(solution)/shard_map/ppermute | solution.py:44
  86.3 13.7 %collective-permute-start.29 = (bf16[512,256]{1,0:T(8,128)(2,1)S(1)}, bf16[512,256]{1,0:T(8,128)(2,1)S(1)}, u32[]{:S(2)}, u32[]{:S(2)}) collective-permute-start(bf16[512,256]{1,0:T(8,128)(2,1)S(1)} %add_convert_fusion.9), channel_id=1, source_target_pairs={{0,2},{1,3},{2,0},{3,1},{4,6},{5,7},{6,4},{7,5},{8,10},{9,11},{10,... | collective-permute-start | bytes 786440 | tf_op jit(solution)/shard_map/ppermute | solution.py:44
  91.8 11.7 %collective-permute-start.27 = (bf16[768,256]{1,0:T(8,128)(2,1)S(1)}, bf16[768,256]{1,0:T(8,128)(2,1)S(1)}, u32[]{:S(2)}, u32[]{:S(2)}) collective-permute-start(bf16[768,256]{1,0:T(8,128)(2,1)S(1)} %collective-permute-done.23.refs_2_), channel_id=1, source_target_pairs={{0,4},{4,0},{8,12},{12,8},{16,20},{20,16},{24,28},{28,24},{1,5},{5... | collective-permute-start | bytes 1179656 | tf_op jit(solution)/shard_map/ppermute | solution.py:39
  101.4 13.4 %collective-permute-start.34 = (bf16[768,256]{1,0:T(8,128)(2,1)S(1)}, bf16[768,256]{1,0:T(8,128)(2,1)S(1)}, u32[]{:S(2)}, u32[]{:S(2)}) collective-permute-start(bf16[768,256]{1,0:T(8,128)(2,1)S(1)} %get-tuple-element.146), channel_id=1, source_target_pairs={{0,16},{4,20},{8,24},{12,28},{16,0},{20,4},{24,8},{28,12},{1,17},{... | collective-permute-start | bytes 1179656 | tf_op jit(solution)/shard_map/ppermute | solution.py:34
  102.1 14.8 %collective-permute-start.33 = (bf16[768,256]{1,0:T(8,128)(2,1)S(1)}, bf16[768,256]{1,0:T(8,128)(2,1)S(1)}, u32[]{:S(2)}, u32[]{:S(2)}) collective-permute-start(bf16[768,256]{1,0:T(8,128)(2,1)S(1)} %get-tuple-element.144), channel_id=1, source_target_pairs={{0,8},{4,12},{8,0},{12,4},{16,24},{20,28},{24,16},{28,20},{1,9},{5... | collective-permute-start | bytes 1179656 | tf_op jit(solution)/shard_map/ppermute | solution.py:34
  110.8 15.8 %collective-permute-start.39 = (bf16[768,256]{1,0:T(8,128)(2,1)S(1)}, bf16[768,256]{1,0:T(8,128)(2,1)S(1)}, u32[]{:S(2)}, u32[]{:S(2)}) collective-permute-start(bf16[768,256]{1,0:T(8,128)(2,1)S(1)} %collective-permute-done.35.refs_3_), channel_id=1, source_target_pairs={{0,4},{4,0},{8,12},{12,8},{16,20},{20,16},{24,28},{28,24},{1,5},{5... | collective-permute-start | bytes 1179656 | tf_op jit(solution)/shard_map/ppermute | solution.py:39
  114.8 13.0 %collective-permute-start.38 = (bf16[768,256]{1,0:T(8,128)(2,1)S(1)}, bf16[768,256]{1,0:T(8,128)(2,1)S(1)}, u32[]{:S(2)}, u32[]{:S(2)}) collective-permute-start(bf16[768,256]{1,0:T(8,128)(2,1)S(1)} %collective-permute-done.34.refs_2_), channel_id=1, source_target_pairs={{0,4},{4,0},{8,12},{12,8},{16,20},{20,16},{24,28},{28,24},{1,5},{5... | collective-permute-start | bytes 1179656 | tf_op jit(solution)/shard_map/ppermute | solution.py:39
  117.0 12.4 %collective-permute-start.37 = (bf16[768,256]{1,0:T(8,128)(2,1)S(1)}, bf16[768,256]{1,0:T(8,128)(2,1)S(1)}, u32[]{:S(2)}, u32[]{:S(2)}) collective-permute-start(bf16[768,256]{1,0:T(8,128)(2,1)S(1)} %collective-permute-done.33.refs_1_), channel_id=1, source_target_pairs={{0,4},{4,0},{8,12},{12,8},{16,20},{20,16},{24,28},{28,24},{1,5},{5... | collective-permute-start | bytes 1179656 | tf_op jit(solution)/shard_map/ppermute | solution.py:39
  117.2 12.1 %collective-permute-start.36 = (bf16[768,256]{1,0:T(8,128)(2,1)S(1)}, bf16[768,256]{1,0:T(8,128)(2,1)S(1)}, u32[]{:S(2)}, u32[]{:S(2)}) collective-permute-start(bf16[768,256]{1,0:T(8,128)(2,1)S(1)} %get-tuple-element.143.refs_0_), channel_id=1, source_target_pairs={{0,4},{4,0},{8,12},{12,8},{16,20},{20,16},{24,28},{28,24},{1,5},{5... | collective-permute-start | bytes 1179656 | tf_op jit(solution)/shard_map/ppermute | solution.py:39
  125.0 16.1 %collective-permute-start.42 = (bf16[768,256]{1,0:T(8,128)(2,1)S(1)}, bf16[768,256]{1,0:T(8,128)(2,1)}, u32[]{:S(2)}, u32[]{:S(2)}) collective-permute-start(bf16[768,256]{1,0:T(8,128)(2,1)S(1)} %get-tuple-element.157), channel_id=1, source_target_pairs={{0,24},{4,28},{8,16},{12,20},{16,8},{20,12},{24,0},{28,4},{1,25},{... | collective-permute-start | bytes 1179656 | tf_op jit(solution)/shard_map/ppermute | solution.py:34
  126.6 18.9 %collective-permute-start.41 = (bf16[768,256]{1,0:T(8,128)(2,1)S(1)}, bf16[768,256]{1,0:T(8,128)(2,1)}, u32[]{:S(2)}, u32[]{:S(2)}) collective-permute-start(bf16[768,256]{1,0:T(8,128)(2,1)S(1)} %get-tuple-element.155), channel_id=1, source_target_pairs={{0,16},{4,20},{8,24},{12,28},{16,0},{20,4},{24,8},{28,12},{1,17},{... | collective-permute-start | bytes 1179656 | tf_op jit(solution)/shard_map/ppermute | solution.py:34
  127.8 17.7 %collective-permute-start.40 = (bf16[768,256]{1,0:T(8,128)(2,1)S(1)}, bf16[768,256]{1,0:T(8,128)(2,1)}, u32[]{:S(2)}, u32[]{:S(2)}) collective-permute-start(bf16[768,256]{1,0:T(8,128)(2,1)S(1)} %get-tuple-element.153), channel_id=1, source_target_pairs={{0,8},{4,12},{8,0},{12,4},{16,24},{20,28},{24,16},{28,20},{1,9},{5... | collective-permute-start | bytes 1179656 | tf_op jit(solution)/shard_map/ppermute | solution.py:34
  129.3 16.7 %collective-permute-start.30 = (bf16[128,768]{1,0:T(8,128)(2,1)}, bf16[128,768]{1,0:T(8,128)(2,1)}, u32[]{:S(2)}, u32[]{:S(2)}) collective-permute-start(bf16[128,768]{1,0:T(8,128)(2,1)} %get-tuple-element.246), channel_id=1, source_target_pairs={{0,4},{4,0},{8,12},{12,8},{16,20},{20,16},{24,28},{28,24},{1,5},{5... | collective-permute-start | bytes 589832 | tf_op jit(solution)/shard_map/ppermute | solution.py:39
  165.7 11.8 %collective-permute-start.54 = (bf16[96,1024]{1,0:T(8,128)(2,1)S(1)}, bf16[96,1024]{1,0:T(8,128)(2,1)S(1)}, u32[]{:S(2)}, u32[]{:S(2)}) collective-permute-start(bf16[96,1024]{1,0:T(8,128)(2,1)S(1)} %get-tuple-element.231), channel_id=1, source_target_pairs={{0,8},{4,12},{8,0},{12,4},{16,24},{20,28},{24,16},{28,20},{1,9},{5... | collective-permute-start | bytes 589832 | tf_op jit(solution)/shard_map/ppermute | solution.py:34
  186.5 12.1 %collective-permute-start.63 = (bf16[96,2048]{1,0:T(8,128)(2,1)S(1)}, bf16[96,2048]{1,0:T(8,128)(2,1)S(1)}, u32[]{:S(2)}, u32[]{:S(2)}) collective-permute-start(bf16[96,2048]{1,0:T(8,128)(2,1)S(1)} %get-tuple-element.223), channel_id=1, source_target_pairs={{0,8},{4,12},{8,0},{12,4},{16,24},{20,28},{24,16},{28,20},{1,9},{5... | collective-permute-start | bytes 1179656 | tf_op jit(solution)/shard_map/ppermute | solution.py:34
  187.5 16.6 %collective-permute-start.64 = (bf16[96,2048]{1,0:T(8,128)(2,1)S(1)}, bf16[96,2048]{1,0:T(8,128)(2,1)S(1)}, u32[]{:S(2)}, u32[]{:S(2)}) collective-permute-start(bf16[96,2048]{1,0:T(8,128)(2,1)S(1)} %get-tuple-element.222), channel_id=1, source_target_pairs={{0,16},{4,20},{8,24},{12,28},{16,0},{20,4},{24,8},{28,12},{1,17},{... | collective-permute-start | bytes 1179656 | tf_op jit(solution)/shard_map/ppermute | solution.py:34
  188.7 16.4 %collective-permute-start.65 = (bf16[96,2048]{1,0:T(8,128)(2,1)S(1)}, bf16[96,2048]{1,0:T(8,128)(2,1)S(1)}, u32[]{:S(2)}, u32[]{:S(2)}) collective-permute-start(bf16[96,2048]{1,0:T(8,128)(2,1)S(1)} %get-tuple-element.221), channel_id=1, source_target_pairs={{0,24},{4,28},{8,16},{12,20},{16,8},{20,12},{24,0},{28,4},{1,25},{... | collective-permute-start | bytes 1179656 | tf_op jit(solution)/shard_map/ppermute | solution.py:34
  194.8 13.3 %collective-permute-start.66 = (bf16[96,2048]{1,0:T(8,128)(2,1)S(1)}, bf16[96,2048]{1,0:T(8,128)(2,1)S(1)}, u32[]{:S(2)}, u32[]{:S(2)}) collective-permute-start(bf16[96,2048]{1,0:T(8,128)(2,1)S(1)} %get-tuple-element.184), channel_id=1, source_target_pairs={{0,4},{4,0},{8,12},{12,8},{16,20},{20,16},{24,28},{28,24},{1,5},{5... | collective-permute-start | bytes 1179656 | tf_op jit(solution)/shard_map/ppermute | solution.py:39
  194.9 13.3 %collective-permute-start.67 = (bf16[96,2048]{1,0:T(8,128)(2,1)S(1)}, bf16[96,2048]{1,0:T(8,128)(2,1)S(1)}, u32[]{:S(2)}, u32[]{:S(2)}) collective-permute-start(bf16[96,2048]{1,0:T(8,128)(2,1)S(1)} %get-tuple-element.185), channel_id=1, source_target_pairs={{0,4},{4,0},{8,12},{12,8},{16,20},{20,16},{24,28},{28,24},{1,5},{5... | collective-permute-start | bytes 1179656 | tf_op jit(solution)/shard_map/ppermute | solution.py:39
  209.6 19.6 %collective-permute-start.72 = (bf16[96,2048]{1,0:T(8,128)(2,1)}, bf16[96,2048]{1,0:T(8,128)(2,1)S(1)}, u32[]{:S(2)}, u32[]{:S(2)}) collective-permute-start(bf16[96,2048]{1,0:T(8,128)(2,1)} %get-tuple-element.219), channel_id=1, source_target_pairs={{0,8},{4,12},{8,0},{12,4},{16,24},{20,28},{24,16},{28,20},{1,9},{5... | collective-permute-start | bytes 1179656 | tf_op jit(solution)/shard_map/ppermute | solution.py:34
  210.2 19.6 %collective-permute-start.73 = (bf16[96,2048]{1,0:T(8,128)(2,1)}, bf16[96,2048]{1,0:T(8,128)(2,1)S(1)}, u32[]{:S(2)}, u32[]{:S(2)}) collective-permute-start(bf16[96,2048]{1,0:T(8,128)(2,1)} %get-tuple-element.218), channel_id=1, source_target_pairs={{0,16},{4,20},{8,24},{12,28},{16,0},{20,4},{24,8},{28,12},{1,17},{... | collective-permute-start | bytes 1179656 | tf_op jit(solution)/shard_map/ppermute | solution.py:34
  212.3 17.6 %collective-permute-start.74 = (bf16[96,2048]{1,0:T(8,128)(2,1)}, bf16[96,2048]{1,0:T(8,128)(2,1)S(1)}, u32[]{:S(2)}, u32[]{:S(2)}) collective-permute-start(bf16[96,2048]{1,0:T(8,128)(2,1)} %get-tuple-element.217), channel_id=1, source_target_pairs={{0,24},{4,28},{8,16},{12,20},{16,8},{20,12},{24,0},{28,4},{1,25},{... | collective-permute-start | bytes 1179656 | tf_op jit(solution)/shard_map/ppermute | solution.py:34
  215.1 13.5 %collective-permute-start.70 = (bf16[64,2048]{1,0:T(8,128)(2,1)S(1)}, bf16[64,2048]{1,0:T(8,128)(2,1)}, u32[]{:S(2)}, u32[]{:S(2)}) collective-permute-start(bf16[64,2048]{1,0:T(8,128)(2,1)S(1)} %get-tuple-element.193), channel_id=1, source_target_pairs={{0,1},{1,0},{2,3},{3,2},{4,5},{5,4},{6,7},{7,6},{8,9},{9,8},{10,11... | collective-permute-start | bytes 786440 | tf_op jit(solution)/shard_map/ppermute | solution.py:44
  217.0 11.6 %collective-permute-start.62 = (bf16[32,1024]{1,0:T(8,128)(2,1)}, bf16[32,1024]{1,0:T(8,128)(2,1)}, u32[]{:S(2)}, u32[]{:S(2)}) collective-permute-start(bf16[32,1024]{1,0:T(8,128)(2,1)} %slice.240), channel_id=1, source_target_pairs={{0,2},{1,3},{2,0},{3,1},{4,6},{5,7},{6,4},{7,5},{8,10},{9,11},{10,... | collective-permute-start | bytes 196616 | tf_op jit(solution)/shard_map/ppermute | solution.py:44
  (83 other events, 690.0 us)

commit v3 on v2

--- a/solution.py
+++ b/solution.py
@@ -430,8 +430,8 @@
                 grid=(seq_count // blocks,),
                 in_specs=[constant((rows, width))] * seq_count
                 + [weight_block(b) for b in range(blocks)] * 2
-                + [vmem] * len(held),
-                out_specs=constant((rows, hidden_size)) if last else (vmem, vmem),
+                + [constant(a.shape) for a in held],
+                out_specs=constant((rows, hidden_size)) if last else tuple(constant(s) for s in sum_shapes),
                 scratch_shapes=[pltpu.VMEM(s, F32) for s in sum_shapes] if last else [],
             ),
             out_shape=jax.ShapeDtypeStruct((rows, hidden_size), BF16)
@@ -457,15 +457,20 @@
         if i + 1 < chunks:
             sent[i + 1] = sum_layers(*projected[i + 1])
         arrived[i] = dispatch(*tokens[i])
-    for i in range(1, chunks):
-        sums = gate_up(i, both_cores([after(a, *sums) for a in arrived[i]]), sums)
-
     middle = summed_rows // 2
     own = jnp.concatenate([token[:middle] for token, _ in tokens], axis=1)
     other = swap_cores(own[middle // 2 :])
     own = own[: middle // 2]
     joined = jnp.where(core == 0, jnp.concatenate([own, other], axis=1), jnp.concatenate([other, own], axis=1))
-    expert_hidden = sums
+    joined = [joined[d * tok : (d + 1) * tok] for d in range(columns)]
+    for i in range(1, chunks):
+        both = both_cores([after(a, *sums) for a in arrived[i]])
+        if i == chunks - 1:
+            joined = [after(a, *arrived[i]) for a in joined]
+            both[0] = after(both[0], *joined)
+            joined = [joined[0]] + [swap_columns(joined[d], d) for d in range(1, columns)]
+        sums = gate_up(i, both, sums)
+    expert_hidden = after(sums, *joined)
     tile = 512
 
     def down(piece, *earlier):
@@ -523,18 +528,14 @@
 
     sent, mixed, last = [], [], []
     ahead = down(returns[0])
-    joined = after(joined, ahead[0])
-    joined = [joined[d * tok : (d + 1) * tok] for d in range(columns)]
-    ahead = (after(ahead[0], *joined), ahead[1])
-    joined = [joined[0]] + [swap_columns(joined[d], d) for d in range(1, columns)]
     for i, piece in enumerate(returns):
-        earlier = sent[i - 1] + (joined if i == 1 else []) if i else []
-        sums = summed(*ahead, *earlier)
+        sums = summed(*ahead, *(sent[i - 1] if i else []))
+        sent.append([sums[0]] + [swap_columns(sums[d], d) for d in range(1, columns)])
         if i + 1 < len(returns):
             ahead = down(returns[i + 1], *sums)
         if i:
-            mixed.append(combine(returns[i - 1], [after(a, *sums) for a in sent[i - 1]]))
-        sent.append([sums[0]] + [swap_columns(sums[d], d) for d in range(1, columns)])
+            gate = ahead[1] if i + 1 < len(returns) else sums
+            mixed.append(combine(returns[i - 1], [after(a, *gate) for a in sent[i - 1]]))
     earlier = []
     for i in range(len(returns) - 1):
         last.append(layer_sum(mixed[i][0], after(mixed[i][1], *earlier)))

time: 268 us -> 252 us (0.940)
  starting transfers between devices: 84.9 us -> 72.3 us
    ppermute x19, starting transfers between devices: 42.6 us -> 27.7 us  [swap_layers(): return lax.ppermute(array, 'mp', [(i, i ^ distance) for i in range(count)])]
    ppermute x19, waiting for transfers between devices: 51.3 us -> 42.1 us  [swap_layers(): return lax.ppermute(array, 'mp', [(i, i ^ distance) for i in range(count)])]
    ppermute x30, waiting for transfers between devices: 43.1 us -> 52.3 us  [swap_columns(): lax.ppermute(array, 'seq', [(i, i ^ PAIR * distance) for i in range(count)])]
    unnamed x58 -> x59, local copies, waits for them, and re-layouts: 14 us -> 12 us
  transfers between devices with their start and end apart: 86 -> 86, of which waited for: 42 -> 42; matrix products, arithmetic and copies ran while one was open for 4% -> 3% of each run, Pallas kernels for 14% -> 19%
where the time goes in v3:
time: 252 us; the launch traced here: 251 us
  waiting for transfers between devices  100 us (40%)
  starting transfers between devices  72.3 us (29%)
  Pallas kernels  55.6 us (22%)
  local copies, waits for them, and re-layouts  14.8 us (6%)
  other arithmetic  7.49 us (3%)
    ppermute x30, waiting for transfers between devices, swap_columns(): lax.ppermute(array, 'seq', [(i, i ^ PAIR * distance) for i in range(count)])  52.3 us
    ppermute x19, waiting for transfers between devices, swap_layers(): return lax.ppermute(array, 'mp', [(i, i ^ distance) for i in range(count)])  42.1 us
    ppermute x30, starting transfers between devices, swap_columns(): lax.ppermute(array, 'seq', [(i, i ^ PAIR * distance) for i in range(count)])  37.2 us
    ppermute x19, starting transfers between devices, swap_layers(): return lax.ppermute(array, 'mp', [(i, i ^ distance) for i in range(count)])  27.7 us
    pallas_call x3, Pallas kernels, gate_up(): pl.pallas_call(functools.partial(expert_kernel, seq_count, blocks, first,...  24.6 us
    pallas_call x4, Pallas kernels, down(): pl.pallas_call(down_kernel, grid=(out_width // tile,), out_shape=(jax.Sha...  13.5 us
    unnamed x59, local copies, waits for them, and re-layouts  12 us
    ppermute x37, starting transfers between devices, swap_cores(): return lax.ppermute(array, 'seq', [(i, i ^ 1) for i in range(count)])  7.47 us
  transfers between devices with their start and end apart: 86, of which 42 were waited for; matrix products, arithmetic and copies ran while one was open for 3% of the time, Pallas kernels for 19%

profile of v3, /device:TPU:0, one launch (start us, length us, event | category | flops | bytes accessed | tf_op | source)
XLA Modules:
  0.0 251.3 jit_solution(10028209181194364938)
XLA Ops:
  6.0 4.0 %collective-permute-start.4 = (bf16[960,128]{1,0:T(8,128)(2,1)S(1)}, bf16[960,128]{1,0:T(8,128)(2,1)S(1)}, u32[]{:S(2)}, u32[]{:S(2)}) collective-permute-start(bf16[960,128]{1,0:T(8,128)(2,1)S(1)} %get-tuple-element.123), channel_id=1, source_target_pairs={{0,24},{4,28},{8,16},{12,20},{16,8},{20,12},{24,0},{28,4},{1,25},{... | collective-permute-start | bytes 737288 | tf_op jit(solution)/shard_map/ppermute | solution.py:34
  12.7 2.7 %collective-permute-start = (bf16[16,32]{1,0:T(8,128)(2,1)S(1)}, bf16[16,32]{1,0:T(8,128)(2,1)S(1)}, u32[]{:S(2)}, u32[]{:S(2)}) collective-permute-start(bf16[16,32]{1,0:T(8,128)(2,1)S(1)} %pad.4), channel_id=1, source_target_pairs={{0,2},{1,3},{2,0},{3,1},{4,6},{5,7},{6,4},{7,5},{8,10},{9,11},{10,... | collective-permute-start | bytes 3080 | tf_op jit(solution)/shard_map/ppermute | solution.py:44
  29.2 3.2 %collective-permute-done.9.refs_1_ = bf16[144,512]{1,0:T(8,128)(2,1)S(1)} collective-permute-done((bf16[144,512]{1,0:T(8,128)(2,1)S(1)}, bf16[144,512]{1,0:T(8,128)(2,1)S(1)}, u32[]{:S(2)}, u32[]{:S(2)}) %collective-permute-start.9) | collective-permute-done | bytes 147488 | tf_op jit(solution)/shard_map/ppermute | solution.py:34
  32.9 2.7 %collective-permute-done.11.refs_3_ = bf16[144,512]{1,0:T(8,128)(2,1)S(1)} collective-permute-done((bf16[144,512]{1,0:T(8,128)(2,1)S(1)}, bf16[144,512]{1,0:T(8,128)(2,1)S(1)}, u32[]{:S(2)}, u32[]{:S(2)}) %collective-permute-start.11) | collective-permute-done | bytes 147488 | tf_op jit(solution)/shard_map/ppermute | solution.py:34
  40.2 6.8 %collective-permute-done.16 = bf16[512,256]{1,0:T(8,128)(2,1)S(1)} collective-permute-done((bf16[512,256]{1,0:T(8,128)(2,1)S(1)}, bf16[512,256]{1,0:T(8,128)(2,1)S(1)}, u32[]{:S(2)}, u32[]{:S(2)}) %collective-permute-start.16) | collective-permute-done | bytes 262176 | tf_op jit(solution)/shard_map/ppermute | solution.py:44
  47.1 2.3 collective-permute-start.17
  52.5 8.7 %collective-permute-done.17 = bf16[512,256]{1,0:T(8,128)(2,1)S(1)} collective-permute-done((bf16[512,256]{1,0:T(8,128)(2,1)S(1)}, bf16[512,256]{1,0:T(8,128)(2,1)S(1)}, u32[]{:S(2)}, u32[]{:S(2)}) %collective-permute-start.17) | collective-permute-done | bytes 262176 | tf_op jit(solution)/shard_map/ppermute | solution.py:44
  63.0 2.5 %collective-permute-start.19 = (bf16[512,256]{1,0:T(8,128)(2,1)S(1)}, bf16[512,256]{1,0:T(8,128)(2,1)S(1)}, u32[]{:S(2)}, u32[]{:S(2)}) collective-permute-start(bf16[512,256]{1,0:T(8,128)(2,1)S(1)} %add_convert_fusion.11), channel_id=1, source_target_pairs={{0,2},{1,3},{2,0},{3,1},{4,6},{5,7},{6,4},{7,5},{8,10},{9,11},{10,... | collective-permute-start | bytes 786440 | tf_op jit(solution)/shard_map/ppermute | solution.py:44
  69.1 6.9 %collective-permute-done.21.far_ref = bf16[512,256]{1,0:T(8,128)(2,1)S(1)} collective-permute-done((bf16[512,256]{1,0:T(8,128)(2,1)S(1)}, bf16[512,256]{1,0:T(8,128)(2,1)S(1)}, u32[]{:S(2)}, u32[]{:S(2)}) %collective-permute-start.21) | collective-permute-done | bytes 262176 | tf_op jit(solution)/shard_map/ppermute | solution.py:44
  77.1 2.7 %collective-permute-start.24 = (bf16[768,256]{1,0:T(8,128)(2,1)S(1)}, bf16[768,256]{1,0:T(8,128)(2,1)S(1)}, u32[]{:S(2)}, u32[]{:S(2)}) collective-permute-start(bf16[768,256]{1,0:T(8,128)(2,1)S(1)} %get-tuple-element.140), channel_id=1, source_target_pairs={{0,24},{4,28},{8,16},{12,20},{16,8},{20,12},{24,0},{28,4},{1,25},{... | collective-permute-start | bytes 1179656 | tf_op jit(solution)/shard_map/ppermute | solution.py:34
  81.7 7.4 %collective-permute-done.24.refs_3_ = bf16[768,256]{1,0:T(8,128)(2,1)S(1)} collective-permute-done((bf16[768,256]{1,0:T(8,128)(2,1)S(1)}, bf16[768,256]{1,0:T(8,128)(2,1)S(1)}, u32[]{:S(2)}, u32[]{:S(2)}) %collective-permute-start.24) | collective-permute-done | bytes 393248 | tf_op jit(solution)/shard_map/ppermute | solution.py:34
  90.1 2.8 %collective-permute-done.23.refs_2_ = bf16[768,256]{1,0:T(8,128)(2,1)S(1)} collective-permute-done((bf16[768,256]{1,0:T(8,128)(2,1)S(1)}, bf16[768,256]{1,0:T(8,128)(2,1)S(1)}, u32[]{:S(2)}, u32[]{:S(2)}) %collective-permute-start.23) | collective-permute-done | bytes 393248 | tf_op jit(solution)/shard_map/ppermute | solution.py:34
  94.9 4.3 %collective-permute-done.29 = bf16[512,256]{1,0:T(8,128)(2,1)S(1)} collective-permute-done((bf16[512,256]{1,0:T(8,128)(2,1)S(1)}, bf16[512,256]{1,0:T(8,128)(2,1)S(1)}, u32[]{:S(2)}, u32[]{:S(2)}) %collective-permute-start.29) | collective-permute-done | bytes 262176 | tf_op jit(solution)/shard_map/ppermute | solution.py:44
  99.2 2.4 collective-permute-start.41
  102.8 7.2 %gate_up.3 = (f32[768,1152]{1,0:T(8,128)S(1)}, f32[768,128]{1,0:T(8,128)S(1)}) custom-call(s32[8]{0:T(128)S(1)} %stack.86.place_ref, bf16[768,256]{1,0:T(8,128)(2,1)S(1)} %get-tuple-element.135.refs_0_, bf16[768,256]{1,0:T(8,128)(2,1)S(1)} %collective-permute-done.22.refs_1_, bf16[768,256]{1,0:T(8,128)(2,1)S(1)} %collective-permute-done.23.refs_2_, ...), custom_call_target="tpu_custom_call" | custom-call | bytes 29520000 | tf_op jit(solution)/shard_map/gate_up/pallas_call | solution.py:426
  111.4 4.1 %collective-permute-done.40.refs_2_ = bf16[768,256]{1,0:T(8,128)(2,1)S(1)} collective-permute-done((bf16[768,256]{1,0:T(8,128)(2,1)S(1)}, bf16[768,256]{1,0:T(8,128)(2,1)S(1)}, u32[]{:S(2)}, u32[]{:S(2)}) %collective-permute-start.40) | collective-permute-done | bytes 393248 | tf_op jit(solution)/shard_map/ppermute | solution.py:34
  117.3 2.0 pack.4
  127.7 8.6 %gate_up.4 = (f32[768,1152]{1,0:T(8,128)S(1)}, f32[768,128]{1,0:T(8,128)S(1)}) custom-call(s32[8]{0:T(128)S(1)} %stack.86.place_ref, bf16[768,256]{1,0:T(8,128)(2,1)S(1)} %get-tuple-element.156.refs_0_, bf16[768,256]{1,0:T(8,128)(2,1)S(1)} %collective-permute-done.39.refs_1_, bf16[768,256]{1,0:T(8,128)(2,1)S(1)} %collective-permute-done.40.refs_2_, ...), custom_call_target="tpu_custom_call" | custom-call | bytes 29520000 | tf_op jit(solution)/shard_map/gate_up/pallas_call | solution.py:426
  144.7 2.1 copy-done.3
  146.8 8.9 %gate_up.5.hidden_ref = bf16[768,576]{1,0:T(8,128)(2,1)S(1)} custom-call(s32[8]{0:T(128)S(1)} %stack.86.place_ref, bf16[768,256]{1,0:T(8,128)(2,1)S(1)} %get-tuple-element.166.refs_0_, bf16[768,256]{1,0:T(8,128)(2,1)S(1)} %collective-permute-done.32.refs_1_, bf16[768,256]{1,0:T(8,128)(2,1)S(1)} %collective-permute-done.33.refs_2_, ...), custom_call_target="tpu_custom_call" | custom-call | bytes 29520000 | tf_op jit(solution)/shard_map/gate_up/pallas_call | solution.py:426
  162.9 4.7 %down.5 = (bf16[384,2048]{1,0:T(8,128)(2,1)S(1)}, bf16[96,2048]{1,0:T(8,128)(2,1)S(1)}, bf16[96,2048]{1,0:T(8,128)(2,1)S(1)}, bf16[96,2048]{1,0:T(8,128)(2,1)S(1)}, bf16[96,2048]{1,0:T(8,128)(2,1)S(1)}) custom-call(bf16[768,576]{1,0:T(8,128)(2,1)S(1)} %gate_up.5.hidden_ref, bf16[576,6144]{1,0:T(8,128)(2,1)} %bitcast.34), custom_call_target="tpu_custom_call" | custom-call | bytes 19680000 | tf_op jit(solution)/shard_map/down/pallas_call | solution.py:478
  170.1 6.3 %collective-permute-done.56.refs_3_ = bf16[96,1024]{1,0:T(8,128)(2,1)S(1)} collective-permute-done((bf16[96,1024]{1,0:T(8,128)(2,1)S(1)}, bf16[96,1024]{1,0:T(8,128)(2,1)S(1)}, u32[]{:S(2)}, u32[]{:S(2)}) %collective-permute-start.56) | collective-permute-done | bytes 196640 | tf_op jit(solution)/shard_map/ppermute | solution.py:34
  181.6 5.3 %down.6 = (bf16[384,2048]{1,0:T(8,128)(2,1)S(1)}, bf16[96,2048]{1,0:T(8,128)(2,1)S(1)}, bf16[96,2048]{1,0:T(8,128)(2,1)S(1)}, bf16[96,2048]{1,0:T(8,128)(2,1)S(1)}, bf16[96,2048]{1,0:T(8,128)(2,1)S(1)}) custom-call(bf16[768,576]{1,0:T(8,128)(2,1)S(1)} %gate_up.5.hidden_ref, bf16[576,6144]{1,0:T(8,128)(2,1)} %bitcast.35), custom_call_target="tpu_custom_call" | custom-call | bytes 19680000 | tf_op jit(solution)/shard_map/down/pallas_call | solution.py:478
  187.5 2.7 %collective-permute-done.67.refs_1_ = bf16[96,2048]{1,0:T(8,128)(2,1)S(1)} collective-permute-done((bf16[96,2048]{1,0:T(8,128)(2,1)}, bf16[96,2048]{1,0:T(8,128)(2,1)S(1)}, u32[]{:S(2)}, u32[]{:S(2)}) %collective-permute-start.67) | collective-permute-done | bytes 393248 | tf_op jit(solution)/shard_map/ppermute | solution.py:34
  191.0 6.6 %collective-permute-done.69.refs_3_ = bf16[96,2048]{1,0:T(8,128)(2,1)S(1)} collective-permute-done((bf16[96,2048]{1,0:T(8,128)(2,1)S(1)}, bf16[96,2048]{1,0:T(8,128)(2,1)S(1)}, u32[]{:S(2)}, u32[]{:S(2)}) %collective-permute-start.69) | collective-permute-done | bytes 393248 | tf_op jit(solution)/shard_map/ppermute | solution.py:34
  209.1 4.3 %collective-permute-start.66 = (bf16[32,1024]{1,0:T(8,128)(2,1)S(1)}, bf16[32,1024]{1,0:T(8,128)(2,1)S(1)}, u32[]{:S(2)}, u32[]{:S(2)}) collective-permute-start(bf16[32,1024]{1,0:T(8,128)(2,1)S(1)} %slice.244), channel_id=1, source_target_pairs={{0,2},{1,3},{2,0},{3,1},{4,6},{5,7},{6,4},{7,5},{8,10},{9,11},{10,... | collective-permute-start | bytes 196616 | tf_op jit(solution)/shard_map/ppermute | solution.py:44
  215.0 6.0 %collective-permute-done.77.refs_2_ = bf16[96,2048]{1,0:T(8,128)(2,1)S(1)} collective-permute-done((bf16[96,2048]{1,0:T(8,128)(2,1)S(1)}, bf16[96,2048]{1,0:T(8,128)(2,1)S(1)}, u32[]{:S(2)}, u32[]{:S(2)}) %collective-permute-start.77) | collective-permute-done | bytes 393248 | tf_op jit(solution)/shard_map/ppermute | solution.py:34
  224.7 2.9 %collective-permute-start.75 = (bf16[32,2048]{1,0:T(8,128)(2,1)S(1)}, bf16[32,2048]{1,0:T(8,128)(2,1)S(1)}, u32[]{:S(2)}, u32[]{:S(2)}) collective-permute-start(bf16[32,2048]{1,0:T(8,128)(2,1)S(1)} %slice.242), channel_id=1, source_target_pairs={{0,2},{1,3},{2,0},{3,1},{4,6},{5,7},{6,4},{7,5},{8,10},{9,11},{10,... | collective-permute-start | bytes 393224 | tf_op jit(solution)/shard_map/ppermute | solution.py:44
  232.9 3.2 %collective-permute-done.83.refs_3_ = bf16[96,1024]{1,0:T(8,128)(2,1)S(1)} collective-permute-done((bf16[96,1024]{1,0:T(8,128)(2,1)S(1)}, bf16[96,1024]{1,0:T(8,128)(2,1)S(1)}, u32[]{:S(2)}, u32[]{:S(2)}) %collective-permute-start.83) | collective-permute-done | bytes 196640 | tf_op jit(solution)/shard_map/ppermute | solution.py:34
  236.1 2.0 collective-permute-done.82.refs_2_
  240.8 4.1 %collective-permute-done.84 = bf16[64,1024]{1,0:T(8,128)(2,1)S(1)} collective-permute-done((bf16[64,1024]{1,0:T(8,128)(2,1)S(1)}, bf16[64,1024]{1,0:T(8,128)(2,1)S(1)}, u32[]{:S(2)}, u32[]{:S(2)}) %collective-permute-start.84) | collective-permute-done | bytes 131104 | tf_op jit(solution)/shard_map/ppermute | solution.py:44
  245.2 4.6 %collective-permute-done.80 = bf16[32,2048]{1,0:T(8,128)(2,1)S(1)} collective-permute-done((bf16[32,2048]{1,0:T(8,128)(2,1)S(1)}, bf16[32,2048]{1,0:T(8,128)(2,1)S(1)}, u32[]{:S(2)}, u32[]{:S(2)}) %collective-permute-start.80) | collective-permute-done | bytes 131104 | tf_op jit(solution)/shard_map/ppermute | solution.py:44
  (276 shorter events, 105.6 us)
Async XLA Ops:
  6.0 15.0 %collective-permute-start.4 = (bf16[960,128]{1,0:T(8,128)(2,1)S(1)}, bf16[960,128]{1,0:T(8,128)(2,1)S(1)}, u32[]{:S(2)}, u32[]{:S(2)}) collective-permute-start(bf16[960,128]{1,0:T(8,128)(2,1)S(1)} %get-tuple-element.123), channel_id=1, source_target_pairs={{0,24},{4,28},{8,16},{12,20},{16,8},{20,12},{24,0},{28,4},{1,25},{... | collective-permute-start | bytes 737288 | tf_op jit(solution)/shard_map/ppermute | solution.py:34
  47.1 14.2 %collective-permute-start.17 = (bf16[512,256]{1,0:T(8,128)(2,1)S(1)}, bf16[512,256]{1,0:T(8,128)(2,1)S(1)}, u32[]{:S(2)}, u32[]{:S(2)}) collective-permute-start(bf16[512,256]{1,0:T(8,128)(2,1)S(1)} %add_convert_fusion.13), channel_id=1, source_target_pairs={{0,2},{1,3},{2,0},{3,1},{4,6},{5,7},{6,4},{7,5},{8,10},{9,11},{10,... | collective-permute-start | bytes 786440 | tf_op jit(solution)/shard_map/ppermute | solution.py:44
  50.9 12.0 %collective-permute-start.18 = (bf16[512,256]{1,0:T(8,128)(2,1)S(1)}, bf16[512,256]{1,0:T(8,128)(2,1)S(1)}, u32[]{:S(2)}, u32[]{:S(2)}) collective-permute-start(bf16[512,256]{1,0:T(8,128)(2,1)S(1)} %get-tuple-element.129), channel_id=1, source_target_pairs={{0,1},{1,0},{2,3},{3,2},{4,5},{5,4},{6,7},{7,6},{8,9},{9,8},{10,11... | collective-permute-start | bytes 786440 | tf_op jit(solution)/shard_map/ppermute | solution.py:44
  61.4 14.6 %collective-permute-start.21 = (bf16[512,256]{1,0:T(8,128)(2,1)S(1)}, bf16[512,256]{1,0:T(8,128)(2,1)S(1)}, u32[]{:S(2)}, u32[]{:S(2)}) collective-permute-start(bf16[512,256]{1,0:T(8,128)(2,1)S(1)} %add_convert_fusion.12.near_ref), channel_id=1, source_target_pairs={{0,1},{1,0},{2,3},{3,2},{4,5},{5,4},{6,7},{7,6},{8,9},{9,8},{10,11... | collective-permute-start | bytes 786440 | tf_op jit(solution)/shard_map/ppermute | solution.py:44
  63.0 16.8 %collective-permute-start.19 = (bf16[512,256]{1,0:T(8,128)(2,1)S(1)}, bf16[512,256]{1,0:T(8,128)(2,1)S(1)}, u32[]{:S(2)}, u32[]{:S(2)}) collective-permute-start(bf16[512,256]{1,0:T(8,128)(2,1)S(1)} %add_convert_fusion.11), channel_id=1, source_target_pairs={{0,2},{1,3},{2,0},{3,1},{4,6},{5,7},{6,4},{7,5},{8,10},{9,11},{10,... | collective-permute-start | bytes 786440 | tf_op jit(solution)/shard_map/ppermute | solution.py:44
  68.4 13.2 %collective-permute-start.20 = (bf16[512,256]{1,0:T(8,128)(2,1)S(1)}, bf16[512,256]{1,0:T(8,128)(2,1)S(1)}, u32[]{:S(2)}, u32[]{:S(2)}) collective-permute-start(bf16[512,256]{1,0:T(8,128)(2,1)S(1)} %get-tuple-element.132), channel_id=1, source_target_pairs={{0,1},{1,0},{2,3},{3,2},{4,5},{5,4},{6,7},{7,6},{8,9},{9,8},{10,11... | collective-permute-start | bytes 786440 | tf_op jit(solution)/shard_map/ppermute | solution.py:44
  77.1 12.0 %collective-permute-start.24 = (bf16[768,256]{1,0:T(8,128)(2,1)S(1)}, bf16[768,256]{1,0:T(8,128)(2,1)S(1)}, u32[]{:S(2)}, u32[]{:S(2)}) collective-permute-start(bf16[768,256]{1,0:T(8,128)(2,1)S(1)} %get-tuple-element.140), channel_id=1, source_target_pairs={{0,24},{4,28},{8,16},{12,20},{16,8},{20,12},{24,0},{28,4},{1,25},{... | collective-permute-start | bytes 1179656 | tf_op jit(solution)/shard_map/ppermute | solution.py:34
  79.9 13.5 %collective-permute-start.38 = (bf16[512,256]{1,0:T(8,128)(2,1)S(1)}, bf16[512,256]{1,0:T(8,128)(2,1)S(1)}, u32[]{:S(2)}, u32[]{:S(2)}) collective-permute-start(bf16[512,256]{1,0:T(8,128)(2,1)S(1)} %add_convert_fusion.10.near_ref), channel_id=1, source_target_pairs={{0,1},{1,0},{2,3},{3,2},{4,5},{5,4},{6,7},{7,6},{8,9},{9,8},{10,11... | collective-permute-start | bytes 786440 | tf_op jit(solution)/shard_map/ppermute | solution.py:44
  80.0 12.9 %collective-permute-start.23 = (bf16[768,256]{1,0:T(8,128)(2,1)S(1)}, bf16[768,256]{1,0:T(8,128)(2,1)S(1)}, u32[]{:S(2)}, u32[]{:S(2)}) collective-permute-start(bf16[768,256]{1,0:T(8,128)(2,1)S(1)} %get-tuple-element.138), channel_id=1, source_target_pairs={{0,16},{4,20},{8,24},{12,28},{16,0},{20,4},{24,8},{28,12},{1,17},{... | collective-permute-start | bytes 1179656 | tf_op jit(solution)/shard_map/ppermute | solution.py:34
  80.7 12.6 %collective-permute-start.22 = (bf16[768,256]{1,0:T(8,128)(2,1)S(1)}, bf16[768,256]{1,0:T(8,128)(2,1)S(1)}, u32[]{:S(2)}, u32[]{:S(2)}) collective-permute-start(bf16[768,256]{1,0:T(8,128)(2,1)S(1)} %get-tuple-element.136), channel_id=1, source_target_pairs={{0,8},{4,12},{8,0},{12,4},{16,24},{20,28},{24,16},{28,20},{1,9},{5... | collective-permute-start | bytes 1179656 | tf_op jit(solution)/shard_map/ppermute | solution.py:34
  81.6 19.9 %collective-permute-start.25 = (bf16[768,256]{1,0:T(8,128)(2,1)S(1)}, bf16[768,256]{1,0:T(8,128)(2,1)S(1)}, u32[]{:S(2)}, u32[]{:S(2)}) collective-permute-start(bf16[768,256]{1,0:T(8,128)(2,1)S(1)} %get-tuple-element.135.refs_0_), channel_id=1, source_target_pairs={{0,4},{4,0},{8,12},{12,8},{16,20},{20,16},{24,28},{28,24},{1,5},{5... | collective-permute-start | bytes 1179656 | tf_op jit(solution)/shard_map/ppermute | solution.py:39
  89.1 10.1 %collective-permute-start.29 = (bf16[512,256]{1,0:T(8,128)(2,1)S(1)}, bf16[512,256]{1,0:T(8,128)(2,1)S(1)}, u32[]{:S(2)}, u32[]{:S(2)}) collective-permute-start(bf16[512,256]{1,0:T(8,128)(2,1)S(1)} %add_convert_fusion.9), channel_id=1, source_target_pairs={{0,2},{1,3},{2,0},{3,1},{4,6},{5,7},{6,4},{7,5},{8,10},{9,11},{10,... | collective-permute-start | bytes 786440 | tf_op jit(solution)/shard_map/ppermute | solution.py:44
  99.2 12.3 %collective-permute-start.41 = (bf16[768,256]{1,0:T(8,128)(2,1)S(1)}, bf16[768,256]{1,0:T(8,128)(2,1)S(1)}, u32[]{:S(2)}, u32[]{:S(2)}) collective-permute-start(bf16[768,256]{1,0:T(8,128)(2,1)S(1)} %get-tuple-element.161), channel_id=1, source_target_pairs={{0,24},{4,28},{8,16},{12,20},{16,8},{20,12},{24,0},{28,4},{1,25},{... | collective-permute-start | bytes 1179656 | tf_op jit(solution)/shard_map/ppermute | solution.py:34
  101.5 14.0 %collective-permute-start.40 = (bf16[768,256]{1,0:T(8,128)(2,1)S(1)}, bf16[768,256]{1,0:T(8,128)(2,1)S(1)}, u32[]{:S(2)}, u32[]{:S(2)}) collective-permute-start(bf16[768,256]{1,0:T(8,128)(2,1)S(1)} %get-tuple-element.159), channel_id=1, source_target_pairs={{0,16},{4,20},{8,24},{12,28},{16,0},{20,4},{24,8},{28,12},{1,17},{... | collective-permute-start | bytes 1179656 | tf_op jit(solution)/shard_map/ppermute | solution.py:34
  102.2 14.6 %collective-permute-start.39 = (bf16[768,256]{1,0:T(8,128)(2,1)S(1)}, bf16[768,256]{1,0:T(8,128)(2,1)S(1)}, u32[]{:S(2)}, u32[]{:S(2)}) collective-permute-start(bf16[768,256]{1,0:T(8,128)(2,1)S(1)} %get-tuple-element.157), channel_id=1, source_target_pairs={{0,8},{4,12},{8,0},{12,4},{16,24},{20,28},{24,16},{28,20},{1,9},{5... | collective-permute-start | bytes 1179656 | tf_op jit(solution)/shard_map/ppermute | solution.py:34
  111.4 9.7 %collective-permute-start.45 = (bf16[768,256]{1,0:T(8,128)(2,1)S(1)}, bf16[768,256]{1,0:T(8,128)(2,1)S(1)}, u32[]{:S(2)}, u32[]{:S(2)}) collective-permute-start(bf16[768,256]{1,0:T(8,128)(2,1)S(1)} %collective-permute-done.41.refs_3_), channel_id=1, source_target_pairs={{0,4},{4,0},{8,12},{12,8},{16,20},{20,16},{24,28},{28,24},{1,5},{5... | collective-permute-start | bytes 1179656 | tf_op jit(solution)/shard_map/ppermute | solution.py:39
  119.4 18.7 %collective-permute-start.34 = (bf16[768,256]{1,0:T(8,128)(2,1)}, bf16[768,256]{1,0:T(8,128)(2,1)S(1)}, u32[]{:S(2)}, u32[]{:S(2)}) collective-permute-start(bf16[768,256]{1,0:T(8,128)(2,1)} %get-tuple-element.148), channel_id=1, source_target_pairs={{0,24},{4,28},{8,16},{12,20},{16,8},{20,12},{24,0},{28,4},{1,25},{... | collective-permute-start | bytes 1179656 | tf_op jit(solution)/shard_map/ppermute | solution.py:34
  121.9 18.0 %collective-permute-start.33 = (bf16[768,256]{1,0:T(8,128)(2,1)}, bf16[768,256]{1,0:T(8,128)(2,1)S(1)}, u32[]{:S(2)}, u32[]{:S(2)}) collective-permute-start(bf16[768,256]{1,0:T(8,128)(2,1)} %get-tuple-element.147), channel_id=1, source_target_pairs={{0,16},{4,20},{8,24},{12,28},{16,0},{20,4},{24,8},{28,12},{1,17},{... | collective-permute-start | bytes 1179656 | tf_op jit(solution)/shard_map/ppermute | solution.py:34
  124.1 16.0 %collective-permute-start.32 = (bf16[768,256]{1,0:T(8,128)(2,1)}, bf16[768,256]{1,0:T(8,128)(2,1)S(1)}, u32[]{:S(2)}, u32[]{:S(2)}) collective-permute-start(bf16[768,256]{1,0:T(8,128)(2,1)} %get-tuple-element.146), channel_id=1, source_target_pairs={{0,8},{4,12},{8,0},{12,4},{16,24},{20,28},{24,16},{28,20},{1,9},{5... | collective-permute-start | bytes 1179656 | tf_op jit(solution)/shard_map/ppermute | solution.py:34
  141.2 14.5 %collective-permute-start.37 = (bf16[32,1536]{1,0:T(8,128)(2,1)S(1)}, bf16[32,1536]{1,0:T(8,128)(2,1)S(1)}, u32[]{:S(2)}, u32[]{:S(2)}) collective-permute-start(bf16[32,1536]{1,0:T(8,128)(2,1)S(1)} %get-tuple-element.152), channel_id=1, source_target_pairs={{0,24},{4,28},{8,16},{12,20},{16,8},{20,12},{24,0},{28,4},{1,25},{... | collective-permute-start | bytes 294920 | tf_op jit(solution)/shard_map/ppermute | solution.py:34
  143.2 12.6 %collective-permute-start.36 = (bf16[32,1536]{1,0:T(8,128)(2,1)S(1)}, bf16[32,1536]{1,0:T(8,128)(2,1)S(1)}, u32[]{:S(2)}, u32[]{:S(2)}) collective-permute-start(bf16[32,1536]{1,0:T(8,128)(2,1)S(1)} %get-tuple-element.151), channel_id=1, source_target_pairs={{0,16},{4,20},{8,24},{12,28},{16,0},{20,4},{24,8},{28,12},{1,17},{... | collective-permute-start | bytes 294920 | tf_op jit(solution)/shard_map/ppermute | solution.py:34
  144.5 11.3 %collective-permute-start.35 = (bf16[32,1536]{1,0:T(8,128)(2,1)S(1)}, bf16[32,1536]{1,0:T(8,128)(2,1)S(1)}, u32[]{:S(2)}, u32[]{:S(2)}) collective-permute-start(bf16[32,1536]{1,0:T(8,128)(2,1)S(1)} %get-tuple-element.150), channel_id=1, source_target_pairs={{0,8},{4,12},{8,0},{12,4},{16,24},{20,28},{24,16},{28,20},{1,9},{5... | collective-permute-start | bytes 294920 | tf_op jit(solution)/shard_map/ppermute | solution.py:34
  178.0 12.3 %collective-permute-start.67 = (bf16[96,2048]{1,0:T(8,128)(2,1)}, bf16[96,2048]{1,0:T(8,128)(2,1)S(1)}, u32[]{:S(2)}, u32[]{:S(2)}) collective-permute-start(bf16[96,2048]{1,0:T(8,128)(2,1)} %get-tuple-element.231), channel_id=1, source_target_pairs={{0,8},{4,12},{8,0},{12,4},{16,24},{20,28},{24,16},{28,20},{1,9},{5... | collective-permute-start | bytes 1179656 | tf_op jit(solution)/shard_map/ppermute | solution.py:34
  179.0 12.0 %collective-permute-start.68 = (bf16[96,2048]{1,0:T(8,128)(2,1)}, bf16[96,2048]{1,0:T(8,128)(2,1)S(1)}, u32[]{:S(2)}, u32[]{:S(2)}) collective-permute-start(bf16[96,2048]{1,0:T(8,128)(2,1)} %get-tuple-element.230), channel_id=1, source_target_pairs={{0,16},{4,20},{8,24},{12,28},{16,0},{20,4},{24,8},{28,12},{1,17},{... | collective-permute-start | bytes 1179656 | tf_op jit(solution)/shard_map/ppermute | solution.py:34
  179.7 17.9 %collective-permute-start.69 = (bf16[96,2048]{1,0:T(8,128)(2,1)S(1)}, bf16[96,2048]{1,0:T(8,128)(2,1)S(1)}, u32[]{:S(2)}, u32[]{:S(2)}) collective-permute-start(bf16[96,2048]{1,0:T(8,128)(2,1)S(1)} %get-tuple-element.229), channel_id=1, source_target_pairs={{0,24},{4,28},{8,16},{12,20},{16,8},{20,12},{24,0},{28,4},{1,25},{... | collective-permute-start | bytes 1179656 | tf_op jit(solution)/shard_map/ppermute | solution.py:34
  186.9 10.7 %collective-permute-start.61 = (bf16[96,2048]{1,0:T(8,128)(2,1)S(1)}, bf16[96,2048]{1,0:T(8,128)(2,1)S(1)}, u32[]{:S(2)}, u32[]{:S(2)}) collective-permute-start(bf16[96,2048]{1,0:T(8,128)(2,1)S(1)} %get-tuple-element.184), channel_id=1, source_target_pairs={{0,4},{4,0},{8,12},{12,8},{16,20},{20,16},{24,28},{28,24},{1,5},{5... | collective-permute-start | bytes 1179656 | tf_op jit(solution)/shard_map/ppermute | solution.py:39
  187.0 10.6 %collective-permute-start.62 = (bf16[96,2048]{1,0:T(8,128)(2,1)S(1)}, bf16[96,2048]{1,0:T(8,128)(2,1)S(1)}, u32[]{:S(2)}, u32[]{:S(2)}) collective-permute-start(bf16[96,2048]{1,0:T(8,128)(2,1)S(1)} %get-tuple-element.185), channel_id=1, source_target_pairs={{0,4},{4,0},{8,12},{12,8},{16,20},{20,16},{24,28},{28,24},{1,5},{5... | collective-permute-start | bytes 1179656 | tf_op jit(solution)/shard_map/ppermute | solution.py:39
  200.8 14.2 %collective-permute-start.76 = (bf16[96,2048]{1,0:T(8,128)(2,1)S(1)}, bf16[96,2048]{1,0:T(8,128)(2,1)S(1)}, u32[]{:S(2)}, u32[]{:S(2)}) collective-permute-start(bf16[96,2048]{1,0:T(8,128)(2,1)S(1)} %get-tuple-element.227), channel_id=1, source_target_pairs={{0,8},{4,12},{8,0},{12,4},{16,24},{20,28},{24,16},{28,20},{1,9},{5... | collective-permute-start | bytes 1179656 | tf_op jit(solution)/shard_map/ppermute | solution.py:34
  201.9 19.0 %collective-permute-start.77 = (bf16[96,2048]{1,0:T(8,128)(2,1)S(1)}, bf16[96,2048]{1,0:T(8,128)(2,1)S(1)}, u32[]{:S(2)}, u32[]{:S(2)}) collective-permute-start(bf16[96,2048]{1,0:T(8,128)(2,1)S(1)} %get-tuple-element.226), channel_id=1, source_target_pairs={{0,16},{4,20},{8,24},{12,28},{16,0},{20,4},{24,8},{28,12},{1,17},{... | collective-permute-start | bytes 1179656 | tf_op jit(solution)/shard_map/ppermute | solution.py:34
  203.2 17.7 %collective-permute-start.78 = (bf16[96,2048]{1,0:T(8,128)(2,1)S(1)}, bf16[96,2048]{1,0:T(8,128)(2,1)S(1)}, u32[]{:S(2)}, u32[]{:S(2)}) collective-permute-start(bf16[96,2048]{1,0:T(8,128)(2,1)S(1)} %get-tuple-element.225), channel_id=1, source_target_pairs={{0,24},{4,28},{8,16},{12,20},{16,8},{20,12},{24,0},{28,4},{1,25},{... | collective-permute-start | bytes 1179656 | tf_op jit(solution)/shard_map/ppermute | solution.py:34
  209.1 15.5 %collective-permute-start.66 = (bf16[32,1024]{1,0:T(8,128)(2,1)S(1)}, bf16[32,1024]{1,0:T(8,128)(2,1)S(1)}, u32[]{:S(2)}, u32[]{:S(2)}) collective-permute-start(bf16[32,1024]{1,0:T(8,128)(2,1)S(1)} %slice.244), channel_id=1, source_target_pairs={{0,2},{1,3},{2,0},{3,1},{4,6},{5,7},{6,4},{7,5},{8,10},{9,11},{10,... | collective-permute-start | bytes 196616 | tf_op jit(solution)/shard_map/ppermute | solution.py:44
  222.8 10.0 %collective-permute-start.79 = (bf16[64,2048]{1,0:T(8,128)(2,1)S(1)}, bf16[64,2048]{1,0:T(8,128)(2,1)S(1)}, u32[]{:S(2)}, u32[]{:S(2)}) collective-permute-start(bf16[64,2048]{1,0:T(8,128)(2,1)S(1)} %get-tuple-element.215), channel_id=1, source_target_pairs={{0,1},{1,0},{2,3},{3,2},{4,5},{5,4},{6,7},{7,6},{8,9},{9,8},{10,11... | collective-permute-start | bytes 786440 | tf_op jit(solution)/shard_map/ppermute | solution.py:44
  (82 other events, 538.7 us)

commit v4 on v3

--- a/solution.py
+++ b/solution.py
@@ -471,7 +471,7 @@
             joined = [joined[0]] + [swap_columns(joined[d], d) for d in range(1, columns)]
         sums = gate_up(i, both, sums)
     expert_hidden = after(sums, *joined)
-    tile = 512
+    tile = 1024
 
     def down(piece, *earlier):
         offset, out_width = piece

time: 252 us -> 250 us (level)
  waiting for transfers between devices: 100 us -> 107 us
  starting transfers between devices: 72.3 us -> 68.3 us
  Pallas kernels: 55.6 us -> 52 us
    ppermute x19, starting transfers between devices: 27.7 us -> 23.6 us  [swap_layers(): return lax.ppermute(array, 'mp', [(i, i ^ distance) for i in range(count)])]
    ppermute x30, waiting for transfers between devices: 52.3 us -> 55.1 us  [swap_columns(): lax.ppermute(array, 'seq', [(i, i ^ PAIR * distance) for i in range(count)])]
  transfers between devices with their start and end apart: 86 -> 86, of which waited for: 42 -> 42; matrix products, arithmetic and copies ran while one was open for 3% -> 3% of each run, Pallas kernels for 19% -> 18%
where the time goes in v4:
time: 250 us
  waiting for transfers between devices  107 us (43%)
  starting transfers between devices  68.3 us (27%)
  Pallas kernels  52 us (21%)
  local copies, waits for them, and re-layouts  14.8 us (6%)
  other arithmetic  7.5 us (3%)
    ppermute x30, waiting for transfers between devices, swap_columns(): lax.ppermute(array, 'seq', [(i, i ^ PAIR * distance) for i in range(count)])  55.1 us
    ppermute x19, waiting for transfers between devices, swap_layers(): return lax.ppermute(array, 'mp', [(i, i ^ distance) for i in range(count)])  43.9 us
    ppermute x30, starting transfers between devices, swap_columns(): lax.ppermute(array, 'seq', [(i, i ^ PAIR * distance) for i in range(count)])  37.2 us
    pallas_call x3, Pallas kernels, gate_up(): pl.pallas_call(functools.partial(expert_kernel, seq_count, blocks, first,...  24.6 us
    ppermute x19, starting transfers between devices, swap_layers(): return lax.ppermute(array, 'mp', [(i, i ^ distance) for i in range(count)])  23.6 us
    unnamed x59, local copies, waits for them, and re-layouts  12 us
    pallas_call x4, Pallas kernels, down(): pl.pallas_call(down_kernel, grid=(out_width // tile,), out_shape=(jax.Sha...  11.5 us
    ppermute x37, waiting for transfers between devices, swap_cores(): return lax.ppermute(array, 'seq', [(i, i ^ 1) for i in range(count)])  7.58 us
  transfers between devices with their start and end apart: 86, of which 42 were waited for; matrix products, arithmetic and copies ran while one was open for 3% of the time, Pallas kernels for 18%

profile of v4, /device:TPU:0, one launch (start us, length us, event | category | flops | bytes accessed | tf_op | source)
XLA Modules:
  0.0 250.0 jit_solution(602344938414398845)
XLA Ops:
  6.0 4.0 %collective-permute-start.4 = (bf16[960,128]{1,0:T(8,128)(2,1)S(1)}, bf16[960,128]{1,0:T(8,128)(2,1)S(1)}, u32[]{:S(2)}, u32[]{:S(2)}) collective-permute-start(bf16[960,128]{1,0:T(8,128)(2,1)S(1)} %get-tuple-element.123), channel_id=1, source_target_pairs={{0,24},{4,28},{8,16},{12,20},{16,8},{20,12},{24,0},{28,4},{1,25},{... | collective-permute-start | bytes 737288 | tf_op jit(solution)/shard_map/ppermute | solution.py:34
  12.7 2.7 %collective-permute-start = (bf16[16,32]{1,0:T(8,128)(2,1)S(1)}, bf16[16,32]{1,0:T(8,128)(2,1)S(1)}, u32[]{:S(2)}, u32[]{:S(2)}) collective-permute-start(bf16[16,32]{1,0:T(8,128)(2,1)S(1)} %pad.4), channel_id=1, source_target_pairs={{0,2},{1,3},{2,0},{3,1},{4,6},{5,7},{6,4},{7,5},{8,10},{9,11},{10,... | collective-permute-start | bytes 3080 | tf_op jit(solution)/shard_map/ppermute | solution.py:44
  29.2 3.2 %collective-permute-done.9.refs_1_ = bf16[144,512]{1,0:T(8,128)(2,1)S(1)} collective-permute-done((bf16[144,512]{1,0:T(8,128)(2,1)S(1)}, bf16[144,512]{1,0:T(8,128)(2,1)S(1)}, u32[]{:S(2)}, u32[]{:S(2)}) %collective-permute-start.9) | collective-permute-done | bytes 147488 | tf_op jit(solution)/shard_map/ppermute | solution.py:34
  32.9 2.7 %collective-permute-done.11.refs_3_ = bf16[144,512]{1,0:T(8,128)(2,1)S(1)} collective-permute-done((bf16[144,512]{1,0:T(8,128)(2,1)S(1)}, bf16[144,512]{1,0:T(8,128)(2,1)S(1)}, u32[]{:S(2)}, u32[]{:S(2)}) %collective-permute-start.11) | collective-permute-done | bytes 147488 | tf_op jit(solution)/shard_map/ppermute | solution.py:34
  40.2 6.8 %collective-permute-done.16 = bf16[512,256]{1,0:T(8,128)(2,1)S(1)} collective-permute-done((bf16[512,256]{1,0:T(8,128)(2,1)S(1)}, bf16[512,256]{1,0:T(8,128)(2,1)S(1)}, u32[]{:S(2)}, u32[]{:S(2)}) %collective-permute-start.16) | collective-permute-done | bytes 262176 | tf_op jit(solution)/shard_map/ppermute | solution.py:44
  47.1 2.3 collective-permute-start.17
  52.5 8.7 %collective-permute-done.17 = bf16[512,256]{1,0:T(8,128)(2,1)S(1)} collective-permute-done((bf16[512,256]{1,0:T(8,128)(2,1)S(1)}, bf16[512,256]{1,0:T(8,128)(2,1)S(1)}, u32[]{:S(2)}, u32[]{:S(2)}) %collective-permute-start.17) | collective-permute-done | bytes 262176 | tf_op jit(solution)/shard_map/ppermute | solution.py:44
  63.0 2.5 %collective-permute-start.19 = (bf16[512,256]{1,0:T(8,128)(2,1)S(1)}, bf16[512,256]{1,0:T(8,128)(2,1)S(1)}, u32[]{:S(2)}, u32[]{:S(2)}) collective-permute-start(bf16[512,256]{1,0:T(8,128)(2,1)S(1)} %add_convert_fusion.11), channel_id=1, source_target_pairs={{0,2},{1,3},{2,0},{3,1},{4,6},{5,7},{6,4},{7,5},{8,10},{9,11},{10,... | collective-permute-start | bytes 786440 | tf_op jit(solution)/shard_map/ppermute | solution.py:44
  69.1 6.9 %collective-permute-done.21.far_ref = bf16[512,256]{1,0:T(8,128)(2,1)S(1)} collective-permute-done((bf16[512,256]{1,0:T(8,128)(2,1)S(1)}, bf16[512,256]{1,0:T(8,128)(2,1)S(1)}, u32[]{:S(2)}, u32[]{:S(2)}) %collective-permute-start.21) | collective-permute-done | bytes 262176 | tf_op jit(solution)/shard_map/ppermute | solution.py:44
  77.1 2.7 %collective-permute-start.24 = (bf16[768,256]{1,0:T(8,128)(2,1)S(1)}, bf16[768,256]{1,0:T(8,128)(2,1)S(1)}, u32[]{:S(2)}, u32[]{:S(2)}) collective-permute-start(bf16[768,256]{1,0:T(8,128)(2,1)S(1)} %get-tuple-element.140), channel_id=1, source_target_pairs={{0,24},{4,28},{8,16},{12,20},{16,8},{20,12},{24,0},{28,4},{1,25},{... | collective-permute-start | bytes 1179656 | tf_op jit(solution)/shard_map/ppermute | solution.py:34
  81.7 7.4 %collective-permute-done.24.refs_3_ = bf16[768,256]{1,0:T(8,128)(2,1)S(1)} collective-permute-done((bf16[768,256]{1,0:T(8,128)(2,1)S(1)}, bf16[768,256]{1,0:T(8,128)(2,1)S(1)}, u32[]{:S(2)}, u32[]{:S(2)}) %collective-permute-start.24) | collective-permute-done | bytes 393248 | tf_op jit(solution)/shard_map/ppermute | solution.py:34
  90.1 2.8 %collective-permute-done.23.refs_2_ = bf16[768,256]{1,0:T(8,128)(2,1)S(1)} collective-permute-done((bf16[768,256]{1,0:T(8,128)(2,1)S(1)}, bf16[768,256]{1,0:T(8,128)(2,1)S(1)}, u32[]{:S(2)}, u32[]{:S(2)}) %collective-permute-start.23) | collective-permute-done | bytes 393248 | tf_op jit(solution)/shard_map/ppermute | solution.py:34
  94.9 4.3 %collective-permute-done.29 = bf16[512,256]{1,0:T(8,128)(2,1)S(1)} collective-permute-done((bf16[512,256]{1,0:T(8,128)(2,1)S(1)}, bf16[512,256]{1,0:T(8,128)(2,1)S(1)}, u32[]{:S(2)}, u32[]{:S(2)}) %collective-permute-start.29) | collective-permute-done | bytes 262176 | tf_op jit(solution)/shard_map/ppermute | solution.py:44
  99.2 2.4 collective-permute-start.41
  102.8 7.2 %gate_up.3 = (f32[768,1152]{1,0:T(8,128)S(1)}, f32[768,128]{1,0:T(8,128)S(1)}) custom-call(s32[8]{0:T(128)S(1)} %stack.86.place_ref, bf16[768,256]{1,0:T(8,128)(2,1)S(1)} %get-tuple-element.135.refs_0_, bf16[768,256]{1,0:T(8,128)(2,1)S(1)} %collective-permute-done.22.refs_1_, bf16[768,256]{1,0:T(8,128)(2,1)S(1)} %collective-permute-done.23.refs_2_, ...), custom_call_target="tpu_custom_call" | custom-call | bytes 29520000 | tf_op jit(solution)/shard_map/gate_up/pallas_call | solution.py:426
  111.4 4.1 %collective-permute-done.40.refs_2_ = bf16[768,256]{1,0:T(8,128)(2,1)S(1)} collective-permute-done((bf16[768,256]{1,0:T(8,128)(2,1)S(1)}, bf16[768,256]{1,0:T(8,128)(2,1)S(1)}, u32[]{:S(2)}, u32[]{:S(2)}) %collective-permute-start.40) | collective-permute-done | bytes 393248 | tf_op jit(solution)/shard_map/ppermute | solution.py:34
  117.3 2.0 pack.4
  127.7 8.6 %gate_up.4 = (f32[768,1152]{1,0:T(8,128)S(1)}, f32[768,128]{1,0:T(8,128)S(1)}) custom-call(s32[8]{0:T(128)S(1)} %stack.86.place_ref, bf16[768,256]{1,0:T(8,128)(2,1)S(1)} %get-tuple-element.156.refs_0_, bf16[768,256]{1,0:T(8,128)(2,1)S(1)} %collective-permute-done.39.refs_1_, bf16[768,256]{1,0:T(8,128)(2,1)S(1)} %collective-permute-done.40.refs_2_, ...), custom_call_target="tpu_custom_call" | custom-call | bytes 29520000 | tf_op jit(solution)/shard_map/gate_up/pallas_call | solution.py:426
  144.7 2.1 copy-done.3
  146.8 8.9 %gate_up.5.hidden_ref = bf16[768,576]{1,0:T(8,128)(2,1)S(1)} custom-call(s32[8]{0:T(128)S(1)} %stack.86.place_ref, bf16[768,256]{1,0:T(8,128)(2,1)S(1)} %get-tuple-element.166.refs_0_, bf16[768,256]{1,0:T(8,128)(2,1)S(1)} %collective-permute-done.32.refs_1_, bf16[768,256]{1,0:T(8,128)(2,1)S(1)} %collective-permute-done.33.refs_2_, ...), custom_call_target="tpu_custom_call" | custom-call | bytes 29520000 | tf_op jit(solution)/shard_map/gate_up/pallas_call | solution.py:426
  162.5 4.3 %down.5 = (bf16[384,2048]{1,0:T(8,128)(2,1)S(1)}, bf16[96,2048]{1,0:T(8,128)(2,1)S(1)}, bf16[96,2048]{1,0:T(8,128)(2,1)S(1)}, bf16[96,2048]{1,0:T(8,128)(2,1)S(1)}, bf16[96,2048]{1,0:T(8,128)(2,1)S(1)}) custom-call(bf16[768,576]{1,0:T(8,128)(2,1)S(1)} %gate_up.5.hidden_ref, bf16[576,6144]{1,0:T(8,128)(2,1)} %bitcast.34), custom_call_target="tpu_custom_call" | custom-call | bytes 19680000 | tf_op jit(solution)/shard_map/down/pallas_call | solution.py:478
  169.7 5.9 %collective-permute-done.56.refs_3_ = bf16[96,1024]{1,0:T(8,128)(2,1)S(1)} collective-permute-done((bf16[96,1024]{1,0:T(8,128)(2,1)S(1)}, bf16[96,1024]{1,0:T(8,128)(2,1)S(1)}, u32[]{:S(2)}, u32[]{:S(2)}) %collective-permute-start.56) | collective-permute-done | bytes 196640 | tf_op jit(solution)/shard_map/ppermute | solution.py:34
  180.8 4.4 %down.6 = (bf16[384,2048]{1,0:T(8,128)(2,1)S(1)}, bf16[96,2048]{1,0:T(8,128)(2,1)S(1)}, bf16[96,2048]{1,0:T(8,128)(2,1)S(1)}, bf16[96,2048]{1,0:T(8,128)(2,1)S(1)}, bf16[96,2048]{1,0:T(8,128)(2,1)S(1)}) custom-call(bf16[768,576]{1,0:T(8,128)(2,1)S(1)} %gate_up.5.hidden_ref, bf16[576,6144]{1,0:T(8,128)(2,1)} %bitcast.35), custom_call_target="tpu_custom_call" | custom-call | bytes 19680000 | tf_op jit(solution)/shard_map/down/pallas_call | solution.py:478
  185.8 3.6 %collective-permute-done.67.refs_1_ = bf16[96,2048]{1,0:T(8,128)(2,1)S(1)} collective-permute-done((bf16[96,2048]{1,0:T(8,128)(2,1)}, bf16[96,2048]{1,0:T(8,128)(2,1)S(1)}, u32[]{:S(2)}, u32[]{:S(2)}) %collective-permute-start.67) | collective-permute-done | bytes 393248 | tf_op jit(solution)/shard_map/ppermute | solution.py:34
  189.4 8.0 %collective-permute-done.68.refs_2_ = bf16[96,2048]{1,0:T(8,128)(2,1)S(1)} collective-permute-done((bf16[96,2048]{1,0:T(8,128)(2,1)}, bf16[96,2048]{1,0:T(8,128)(2,1)S(1)}, u32[]{:S(2)}, u32[]{:S(2)}) %collective-permute-start.68) | collective-permute-done | bytes 393248 | tf_op jit(solution)/shard_map/ppermute | solution.py:34
  200.8 3.1 %collective-permute-start.78 = (bf16[96,2048]{1,0:T(8,128)(2,1)S(1)}, bf16[96,2048]{1,0:T(8,128)(2,1)S(1)}, u32[]{:S(2)}, u32[]{:S(2)}) collective-permute-start(bf16[96,2048]{1,0:T(8,128)(2,1)S(1)} %get-tuple-element.225), channel_id=1, source_target_pairs={{0,24},{4,28},{8,16},{12,20},{16,8},{20,12},{24,0},{28,4},{1,25},{... | collective-permute-start | bytes 1179656 | tf_op jit(solution)/shard_map/ppermute | solution.py:34
  208.3 3.1 %collective-permute-start.66 = (bf16[32,1024]{1,0:T(8,128)(2,1)S(1)}, bf16[32,1024]{1,0:T(8,128)(2,1)S(1)}, u32[]{:S(2)}, u32[]{:S(2)}) collective-permute-start(bf16[32,1024]{1,0:T(8,128)(2,1)S(1)} %slice.244), channel_id=1, source_target_pairs={{0,2},{1,3},{2,0},{3,1},{4,6},{5,7},{6,4},{7,5},{8,10},{9,11},{10,... | collective-permute-start | bytes 196616 | tf_op jit(solution)/shard_map/ppermute | solution.py:44
  212.6 7.5 %collective-permute-done.77.refs_2_ = bf16[96,2048]{1,0:T(8,128)(2,1)S(1)} collective-permute-done((bf16[96,2048]{1,0:T(8,128)(2,1)S(1)}, bf16[96,2048]{1,0:T(8,128)(2,1)S(1)}, u32[]{:S(2)}, u32[]{:S(2)}) %collective-permute-start.77) | collective-permute-done | bytes 393248 | tf_op jit(solution)/shard_map/ppermute | solution.py:34
  223.5 2.7 %collective-permute-start.75 = (bf16[32,2048]{1,0:T(8,128)(2,1)S(1)}, bf16[32,2048]{1,0:T(8,128)(2,1)S(1)}, u32[]{:S(2)}, u32[]{:S(2)}) collective-permute-start(bf16[32,2048]{1,0:T(8,128)(2,1)S(1)} %slice.242), channel_id=1, source_target_pairs={{0,2},{1,3},{2,0},{3,1},{4,6},{5,7},{6,4},{7,5},{8,10},{9,11},{10,... | collective-permute-start | bytes 393224 | tf_op jit(solution)/shard_map/ppermute | solution.py:44
  231.7 2.9 %collective-permute-done.83.refs_3_ = bf16[96,1024]{1,0:T(8,128)(2,1)S(1)} collective-permute-done((bf16[96,1024]{1,0:T(8,128)(2,1)S(1)}, bf16[96,1024]{1,0:T(8,128)(2,1)S(1)}, u32[]{:S(2)}, u32[]{:S(2)}) %collective-permute-start.83) | collective-permute-done | bytes 196640 | tf_op jit(solution)/shard_map/ppermute | solution.py:34
  238.2 5.3 %collective-permute-done.84 = bf16[64,1024]{1,0:T(8,128)(2,1)S(1)} collective-permute-done((bf16[64,1024]{1,0:T(8,128)(2,1)S(1)}, bf16[64,1024]{1,0:T(8,128)(2,1)S(1)}, u32[]{:S(2)}, u32[]{:S(2)}) %collective-permute-start.84) | collective-permute-done | bytes 131104 | tf_op jit(solution)/shard_map/ppermute | solution.py:44
  243.6 3.9 %collective-permute-done.80 = bf16[32,2048]{1,0:T(8,128)(2,1)S(1)} collective-permute-done((bf16[32,2048]{1,0:T(8,128)(2,1)S(1)}, bf16[32,2048]{1,0:T(8,128)(2,1)S(1)}, u32[]{:S(2)}, u32[]{:S(2)}) %collective-permute-start.80) | collective-permute-done | bytes 131104 | tf_op jit(solution)/shard_map/ppermute | solution.py:44
  (276 shorter events, 102.2 us)
Async XLA Ops:
  6.0 15.0 %collective-permute-start.4 = (bf16[960,128]{1,0:T(8,128)(2,1)S(1)}, bf16[960,128]{1,0:T(8,128)(2,1)S(1)}, u32[]{:S(2)}, u32[]{:S(2)}) collective-permute-start(bf16[960,128]{1,0:T(8,128)(2,1)S(1)} %get-tuple-element.123), channel_id=1, source_target_pairs={{0,24},{4,28},{8,16},{12,20},{16,8},{20,12},{24,0},{28,4},{1,25},{... | collective-permute-start | bytes 737288 | tf_op jit(solution)/shard_map/ppermute | solution.py:34
  47.1 14.2 %collective-permute-start.17 = (bf16[512,256]{1,0:T(8,128)(2,1)S(1)}, bf16[512,256]{1,0:T(8,128)(2,1)S(1)}, u32[]{:S(2)}, u32[]{:S(2)}) collective-permute-start(bf16[512,256]{1,0:T(8,128)(2,1)S(1)} %add_convert_fusion.13), channel_id=1, source_target_pairs={{0,2},{1,3},{2,0},{3,1},{4,6},{5,7},{6,4},{7,5},{8,10},{9,11},{10,... | collective-permute-start | bytes 786440 | tf_op jit(solution)/shard_map/ppermute | solution.py:44
  50.9 12.0 %collective-permute-start.18 = (bf16[512,256]{1,0:T(8,128)(2,1)S(1)}, bf16[512,256]{1,0:T(8,128)(2,1)S(1)}, u32[]{:S(2)}, u32[]{:S(2)}) collective-permute-start(bf16[512,256]{1,0:T(8,128)(2,1)S(1)} %get-tuple-element.129), channel_id=1, source_target_pairs={{0,1},{1,0},{2,3},{3,2},{4,5},{5,4},{6,7},{7,6},{8,9},{9,8},{10,11... | collective-permute-start | bytes 786440 | tf_op jit(solution)/shard_map/ppermute | solution.py:44
  61.4 14.6 %collective-permute-start.21 = (bf16[512,256]{1,0:T(8,128)(2,1)S(1)}, bf16[512,256]{1,0:T(8,128)(2,1)S(1)}, u32[]{:S(2)}, u32[]{:S(2)}) collective-permute-start(bf16[512,256]{1,0:T(8,128)(2,1)S(1)} %add_convert_fusion.12.near_ref), channel_id=1, source_target_pairs={{0,1},{1,0},{2,3},{3,2},{4,5},{5,4},{6,7},{7,6},{8,9},{9,8},{10,11... | collective-permute-start | bytes 786440 | tf_op jit(solution)/shard_map/ppermute | solution.py:44
  63.0 16.8 %collective-permute-start.19 = (bf16[512,256]{1,0:T(8,128)(2,1)S(1)}, bf16[512,256]{1,0:T(8,128)(2,1)S(1)}, u32[]{:S(2)}, u32[]{:S(2)}) collective-permute-start(bf16[512,256]{1,0:T(8,128)(2,1)S(1)} %add_convert_fusion.11), channel_id=1, source_target_pairs={{0,2},{1,3},{2,0},{3,1},{4,6},{5,7},{6,4},{7,5},{8,10},{9,11},{10,... | collective-permute-start | bytes 786440 | tf_op jit(solution)/shard_map/ppermute | solution.py:44
  68.4 13.2 %collective-permute-start.20 = (bf16[512,256]{1,0:T(8,128)(2,1)S(1)}, bf16[512,256]{1,0:T(8,128)(2,1)S(1)}, u32[]{:S(2)}, u32[]{:S(2)}) collective-permute-start(bf16[512,256]{1,0:T(8,128)(2,1)S(1)} %get-tuple-element.132), channel_id=1, source_target_pairs={{0,1},{1,0},{2,3},{3,2},{4,5},{5,4},{6,7},{7,6},{8,9},{9,8},{10,11... | collective-permute-start | bytes 786440 | tf_op jit(solution)/shard_map/ppermute | solution.py:44
  77.1 12.0 %collective-permute-start.24 = (bf16[768,256]{1,0:T(8,128)(2,1)S(1)}, bf16[768,256]{1,0:T(8,128)(2,1)S(1)}, u32[]{:S(2)}, u32[]{:S(2)}) collective-permute-start(bf16[768,256]{1,0:T(8,128)(2,1)S(1)} %get-tuple-element.140), channel_id=1, source_target_pairs={{0,24},{4,28},{8,16},{12,20},{16,8},{20,12},{24,0},{28,4},{1,25},{... | collective-permute-start | bytes 1179656 | tf_op jit(solution)/shard_map/ppermute | solution.py:34
  79.9 13.5 %collective-permute-start.38 = (bf16[512,256]{1,0:T(8,128)(2,1)S(1)}, bf16[512,256]{1,0:T(8,128)(2,1)S(1)}, u32[]{:S(2)}, u32[]{:S(2)}) collective-permute-start(bf16[512,256]{1,0:T(8,128)(2,1)S(1)} %add_convert_fusion.10.near_ref), channel_id=1, source_target_pairs={{0,1},{1,0},{2,3},{3,2},{4,5},{5,4},{6,7},{7,6},{8,9},{9,8},{10,11... | collective-permute-start | bytes 786440 | tf_op jit(solution)/shard_map/ppermute | solution.py:44
  80.0 12.9 %collective-permute-start.23 = (bf16[768,256]{1,0:T(8,128)(2,1)S(1)}, bf16[768,256]{1,0:T(8,128)(2,1)S(1)}, u32[]{:S(2)}, u32[]{:S(2)}) collective-permute-start(bf16[768,256]{1,0:T(8,128)(2,1)S(1)} %get-tuple-element.138), channel_id=1, source_target_pairs={{0,16},{4,20},{8,24},{12,28},{16,0},{20,4},{24,8},{28,12},{1,17},{... | collective-permute-start | bytes 1179656 | tf_op jit(solution)/shard_map/ppermute | solution.py:34
  80.7 12.6 %collective-permute-start.22 = (bf16[768,256]{1,0:T(8,128)(2,1)S(1)}, bf16[768,256]{1,0:T(8,128)(2,1)S(1)}, u32[]{:S(2)}, u32[]{:S(2)}) collective-permute-start(bf16[768,256]{1,0:T(8,128)(2,1)S(1)} %get-tuple-element.136), channel_id=1, source_target_pairs={{0,8},{4,12},{8,0},{12,4},{16,24},{20,28},{24,16},{28,20},{1,9},{5... | collective-permute-start | bytes 1179656 | tf_op jit(solution)/shard_map/ppermute | solution.py:34
  81.6 19.9 %collective-permute-start.25 = (bf16[768,256]{1,0:T(8,128)(2,1)S(1)}, bf16[768,256]{1,0:T(8,128)(2,1)S(1)}, u32[]{:S(2)}, u32[]{:S(2)}) collective-permute-start(bf16[768,256]{1,0:T(8,128)(2,1)S(1)} %get-tuple-element.135.refs_0_), channel_id=1, source_target_pairs={{0,4},{4,0},{8,12},{12,8},{16,20},{20,16},{24,28},{28,24},{1,5},{5... | collective-permute-start | bytes 1179656 | tf_op jit(solution)/shard_map/ppermute | solution.py:39
  89.1 10.1 %collective-permute-start.29 = (bf16[512,256]{1,0:T(8,128)(2,1)S(1)}, bf16[512,256]{1,0:T(8,128)(2,1)S(1)}, u32[]{:S(2)}, u32[]{:S(2)}) collective-permute-start(bf16[512,256]{1,0:T(8,128)(2,1)S(1)} %add_convert_fusion.9), channel_id=1, source_target_pairs={{0,2},{1,3},{2,0},{3,1},{4,6},{5,7},{6,4},{7,5},{8,10},{9,11},{10,... | collective-permute-start | bytes 786440 | tf_op jit(solution)/shard_map/ppermute | solution.py:44
  99.2 12.3 %collective-permute-start.41 = (bf16[768,256]{1,0:T(8,128)(2,1)S(1)}, bf16[768,256]{1,0:T(8,128)(2,1)S(1)}, u32[]{:S(2)}, u32[]{:S(2)}) collective-permute-start(bf16[768,256]{1,0:T(8,128)(2,1)S(1)} %get-tuple-element.161), channel_id=1, source_target_pairs={{0,24},{4,28},{8,16},{12,20},{16,8},{20,12},{24,0},{28,4},{1,25},{... | collective-permute-start | bytes 1179656 | tf_op jit(solution)/shard_map/ppermute | solution.py:34
  101.5 14.0 %collective-permute-start.40 = (bf16[768,256]{1,0:T(8,128)(2,1)S(1)}, bf16[768,256]{1,0:T(8,128)(2,1)S(1)}, u32[]{:S(2)}, u32[]{:S(2)}) collective-permute-start(bf16[768,256]{1,0:T(8,128)(2,1)S(1)} %get-tuple-element.159), channel_id=1, source_target_pairs={{0,16},{4,20},{8,24},{12,28},{16,0},{20,4},{24,8},{28,12},{1,17},{... | collective-permute-start | bytes 1179656 | tf_op jit(solution)/shard_map/ppermute | solution.py:34
  102.2 14.6 %collective-permute-start.39 = (bf16[768,256]{1,0:T(8,128)(2,1)S(1)}, bf16[768,256]{1,0:T(8,128)(2,1)S(1)}, u32[]{:S(2)}, u32[]{:S(2)}) collective-permute-start(bf16[768,256]{1,0:T(8,128)(2,1)S(1)} %get-tuple-element.157), channel_id=1, source_target_pairs={{0,8},{4,12},{8,0},{12,4},{16,24},{20,28},{24,16},{28,20},{1,9},{5... | collective-permute-start | bytes 1179656 | tf_op jit(solution)/shard_map/ppermute | solution.py:34
  119.4 18.7 %collective-permute-start.34 = (bf16[768,256]{1,0:T(8,128)(2,1)}, bf16[768,256]{1,0:T(8,128)(2,1)S(1)}, u32[]{:S(2)}, u32[]{:S(2)}) collective-permute-start(bf16[768,256]{1,0:T(8,128)(2,1)} %get-tuple-element.148), channel_id=1, source_target_pairs={{0,24},{4,28},{8,16},{12,20},{16,8},{20,12},{24,0},{28,4},{1,25},{... | collective-permute-start | bytes 1179656 | tf_op jit(solution)/shard_map/ppermute | solution.py:34
  121.9 18.0 %collective-permute-start.33 = (bf16[768,256]{1,0:T(8,128)(2,1)}, bf16[768,256]{1,0:T(8,128)(2,1)S(1)}, u32[]{:S(2)}, u32[]{:S(2)}) collective-permute-start(bf16[768,256]{1,0:T(8,128)(2,1)} %get-tuple-element.147), channel_id=1, source_target_pairs={{0,16},{4,20},{8,24},{12,28},{16,0},{20,4},{24,8},{28,12},{1,17},{... | collective-permute-start | bytes 1179656 | tf_op jit(solution)/shard_map/ppermute | solution.py:34
  124.1 16.0 %collective-permute-start.32 = (bf16[768,256]{1,0:T(8,128)(2,1)}, bf16[768,256]{1,0:T(8,128)(2,1)S(1)}, u32[]{:S(2)}, u32[]{:S(2)}) collective-permute-start(bf16[768,256]{1,0:T(8,128)(2,1)} %get-tuple-element.146), channel_id=1, source_target_pairs={{0,8},{4,12},{8,0},{12,4},{16,24},{20,28},{24,16},{28,20},{1,9},{5... | collective-permute-start | bytes 1179656 | tf_op jit(solution)/shard_map/ppermute | solution.py:34
  141.2 14.5 %collective-permute-start.37 = (bf16[32,1536]{1,0:T(8,128)(2,1)S(1)}, bf16[32,1536]{1,0:T(8,128)(2,1)S(1)}, u32[]{:S(2)}, u32[]{:S(2)}) collective-permute-start(bf16[32,1536]{1,0:T(8,128)(2,1)S(1)} %get-tuple-element.152), channel_id=1, source_target_pairs={{0,24},{4,28},{8,16},{12,20},{16,8},{20,12},{24,0},{28,4},{1,25},{... | collective-permute-start | bytes 294920 | tf_op jit(solution)/shard_map/ppermute | solution.py:34
  143.2 12.6 %collective-permute-start.36 = (bf16[32,1536]{1,0:T(8,128)(2,1)S(1)}, bf16[32,1536]{1,0:T(8,128)(2,1)S(1)}, u32[]{:S(2)}, u32[]{:S(2)}) collective-permute-start(bf16[32,1536]{1,0:T(8,128)(2,1)S(1)} %get-tuple-element.151), channel_id=1, source_target_pairs={{0,16},{4,20},{8,24},{12,28},{16,0},{20,4},{24,8},{28,12},{1,17},{... | collective-permute-start | bytes 294920 | tf_op jit(solution)/shard_map/ppermute | solution.py:34
  144.5 11.3 %collective-permute-start.35 = (bf16[32,1536]{1,0:T(8,128)(2,1)S(1)}, bf16[32,1536]{1,0:T(8,128)(2,1)S(1)}, u32[]{:S(2)}, u32[]{:S(2)}) collective-permute-start(bf16[32,1536]{1,0:T(8,128)(2,1)S(1)} %get-tuple-element.150), channel_id=1, source_target_pairs={{0,8},{4,12},{8,0},{12,4},{16,24},{20,28},{24,16},{28,20},{1,9},{5... | collective-permute-start | bytes 294920 | tf_op jit(solution)/shard_map/ppermute | solution.py:34
  177.2 12.3 %collective-permute-start.67 = (bf16[96,2048]{1,0:T(8,128)(2,1)}, bf16[96,2048]{1,0:T(8,128)(2,1)S(1)}, u32[]{:S(2)}, u32[]{:S(2)}) collective-permute-start(bf16[96,2048]{1,0:T(8,128)(2,1)} %get-tuple-element.231), channel_id=1, source_target_pairs={{0,8},{4,12},{8,0},{12,4},{16,24},{20,28},{24,16},{28,20},{1,9},{5... | collective-permute-start | bytes 1179656 | tf_op jit(solution)/shard_map/ppermute | solution.py:34
  178.5 18.9 %collective-permute-start.68 = (bf16[96,2048]{1,0:T(8,128)(2,1)}, bf16[96,2048]{1,0:T(8,128)(2,1)S(1)}, u32[]{:S(2)}, u32[]{:S(2)}) collective-permute-start(bf16[96,2048]{1,0:T(8,128)(2,1)} %get-tuple-element.230), channel_id=1, source_target_pairs={{0,16},{4,20},{8,24},{12,28},{16,0},{20,4},{24,8},{28,12},{1,17},{... | collective-permute-start | bytes 1179656 | tf_op jit(solution)/shard_map/ppermute | solution.py:34
  179.3 18.2 %collective-permute-start.69 = (bf16[96,2048]{1,0:T(8,128)(2,1)S(1)}, bf16[96,2048]{1,0:T(8,128)(2,1)S(1)}, u32[]{:S(2)}, u32[]{:S(2)}) collective-permute-start(bf16[96,2048]{1,0:T(8,128)(2,1)S(1)} %get-tuple-element.229), channel_id=1, source_target_pairs={{0,24},{4,28},{8,16},{12,20},{16,8},{20,12},{24,0},{28,4},{1,25},{... | collective-permute-start | bytes 1179656 | tf_op jit(solution)/shard_map/ppermute | solution.py:34
  185.2 12.3 %collective-permute-start.61 = (bf16[96,2048]{1,0:T(8,128)(2,1)S(1)}, bf16[96,2048]{1,0:T(8,128)(2,1)S(1)}, u32[]{:S(2)}, u32[]{:S(2)}) collective-permute-start(bf16[96,2048]{1,0:T(8,128)(2,1)S(1)} %get-tuple-element.184), channel_id=1, source_target_pairs={{0,4},{4,0},{8,12},{12,8},{16,20},{20,16},{24,28},{28,24},{1,5},{5... | collective-permute-start | bytes 1179656 | tf_op jit(solution)/shard_map/ppermute | solution.py:39
  185.3 12.3 %collective-permute-start.62 = (bf16[96,2048]{1,0:T(8,128)(2,1)S(1)}, bf16[96,2048]{1,0:T(8,128)(2,1)S(1)}, u32[]{:S(2)}, u32[]{:S(2)}) collective-permute-start(bf16[96,2048]{1,0:T(8,128)(2,1)S(1)} %get-tuple-element.185), channel_id=1, source_target_pairs={{0,4},{4,0},{8,12},{12,8},{16,20},{20,16},{24,28},{28,24},{1,5},{5... | collective-permute-start | bytes 1179656 | tf_op jit(solution)/shard_map/ppermute | solution.py:39
  200.4 12.2 %collective-permute-start.76 = (bf16[96,2048]{1,0:T(8,128)(2,1)S(1)}, bf16[96,2048]{1,0:T(8,128)(2,1)S(1)}, u32[]{:S(2)}, u32[]{:S(2)}) collective-permute-start(bf16[96,2048]{1,0:T(8,128)(2,1)S(1)} %get-tuple-element.227), channel_id=1, source_target_pairs={{0,8},{4,12},{8,0},{12,4},{16,24},{20,28},{24,16},{28,20},{1,9},{5... | collective-permute-start | bytes 1179656 | tf_op jit(solution)/shard_map/ppermute | solution.py:34
  200.8 19.4 %collective-permute-start.77 = (bf16[96,2048]{1,0:T(8,128)(2,1)S(1)}, bf16[96,2048]{1,0:T(8,128)(2,1)S(1)}, u32[]{:S(2)}, u32[]{:S(2)}) collective-permute-start(bf16[96,2048]{1,0:T(8,128)(2,1)S(1)} %get-tuple-element.226), channel_id=1, source_target_pairs={{0,16},{4,20},{8,24},{12,28},{16,0},{20,4},{24,8},{28,12},{1,17},{... | collective-permute-start | bytes 1179656 | tf_op jit(solution)/shard_map/ppermute | solution.py:34
  200.8 19.3 %collective-permute-start.78 = (bf16[96,2048]{1,0:T(8,128)(2,1)S(1)}, bf16[96,2048]{1,0:T(8,128)(2,1)S(1)}, u32[]{:S(2)}, u32[]{:S(2)}) collective-permute-start(bf16[96,2048]{1,0:T(8,128)(2,1)S(1)} %get-tuple-element.225), channel_id=1, source_target_pairs={{0,24},{4,28},{8,16},{12,20},{16,8},{20,12},{24,0},{28,4},{1,25},{... | collective-permute-start | bytes 1179656 | tf_op jit(solution)/shard_map/ppermute | solution.py:34
  208.3 15.1 %collective-permute-start.66 = (bf16[32,1024]{1,0:T(8,128)(2,1)S(1)}, bf16[32,1024]{1,0:T(8,128)(2,1)S(1)}, u32[]{:S(2)}, u32[]{:S(2)}) collective-permute-start(bf16[32,1024]{1,0:T(8,128)(2,1)S(1)} %slice.244), channel_id=1, source_target_pairs={{0,2},{1,3},{2,0},{3,1},{4,6},{5,7},{6,4},{7,5},{8,10},{9,11},{10,... | collective-permute-start | bytes 196616 | tf_op jit(solution)/shard_map/ppermute | solution.py:44
  212.5 10.9 %collective-permute-start.74 = (bf16[64,2048]{1,0:T(8,128)(2,1)S(1)}, bf16[64,2048]{1,0:T(8,128)(2,1)S(1)}, u32[]{:S(2)}, u32[]{:S(2)}) collective-permute-start(bf16[64,2048]{1,0:T(8,128)(2,1)S(1)} %get-tuple-element.206), channel_id=1, source_target_pairs={{0,1},{1,0},{2,3},{3,2},{4,5},{5,4},{6,7},{7,6},{8,9},{9,8},{10,11... | collective-permute-start | bytes 786440 | tf_op jit(solution)/shard_map/ppermute | solution.py:44
  221.6 10.1 %collective-permute-start.79 = (bf16[64,2048]{1,0:T(8,128)(2,1)S(1)}, bf16[64,2048]{1,0:T(8,128)(2,1)S(1)}, u32[]{:S(2)}, u32[]{:S(2)}) collective-permute-start(bf16[64,2048]{1,0:T(8,128)(2,1)S(1)} %get-tuple-element.215), channel_id=1, source_target_pairs={{0,1},{1,0},{2,3},{3,2},{4,5},{5,4},{6,7},{7,6},{8,9},{9,8},{10,11... | collective-permute-start | bytes 786440 | tf_op jit(solution)/shard_map/ppermute | solution.py:44
  (82 other events, 551.2 us)

commit v5 on v4

--- a/solution.py
+++ b/solution.py
@@ -144,7 +144,7 @@
                 low_ref[d * slots : (d + 1) * slots, :] = (gain - high.astype(F32)).astype(BF16)
 
 
-def project_kernel(count, layers, tok, chunk, core_ref, *refs):
+def project_kernel(count, layers, tok, core_ref, *refs):
     row_refs, message_refs = refs[:count], refs[count : 2 * count]
     weight_ref, keep_ref, send_ref = refs[2 * count :]
     span = layers * tok
@@ -162,8 +162,7 @@
                 keep_ref[to : to + tok, :] = here.astype(F32)
             else:
                 for b in range(pieces):
-                    at = pl.multiple_of(core_ref[0] + (chunk * pieces + b) * tok, tok)
-                    own = message_refs[p][pl.ds(at, tok), :].astype(F32)
+                    own = message_refs[p][b * tok : (b + 1) * tok, :].astype(F32)
                     cols = slice(b * lanes, (b + 1) * lanes)
                     keep_ref[to : to + tok, cols] = here[:, cols].astype(F32) + own
 
@@ -372,17 +371,23 @@
     summed_rows = seq_count * half
     gate_view, up_view = gate_weight[0].T, up_weight[0].T
 
+    own_rows = width // size * tok
+
     def project(i, *earlier):
         keep, send = pl.pallas_call(
-            functools.partial(project_kernel, seq_count, layers, tok, i),
-            grid=(1,),
+            functools.partial(project_kernel, seq_count, layers, tok),
             out_shape=(
                 jax.ShapeDtypeStruct((summed_rows, width), F32),
                 jax.ShapeDtypeStruct((summed_rows, width), BF16),
             ),
-            in_specs=[smem] + [whole_block(a) for a in (*normed, *messages)]
-            + [pl.BlockSpec((heads * size, width), lambda n: (0, i))],
-            out_specs=(pl.BlockSpec((summed_rows, width), lambda n: (0, 0)),) * 2,
+            grid_spec=pltpu.PrefetchScalarGridSpec(
+                num_scalar_prefetch=1,
+                grid=(1,),
+                in_specs=[whole_block(a) for a in normed]
+                + [pl.BlockSpec((own_rows, size), lambda n, at: (at[0] // own_rows + i, 0))] * seq_count
+                + [pl.BlockSpec((heads * size, width), lambda n, at: (0, i))],
+                out_specs=(pl.BlockSpec((summed_rows, width), lambda n, at: (0, 0)),) * 2,
+            ),
             compiler_params=params(),
             cost_estimate=cost(1),
             name="project",
@@ -685,10 +690,12 @@
     return [(sum(parts[:i]) * tile, part * tile) for i, part in enumerate(parts)]
 
 
-def fits(mesh, tok, features, block, chunks):
+def fits(mesh, tok, features, block, chunks, heads):
     layers, seq_count = mesh.shape["mp"], mesh.shape["seq"]
     powers = seq_count & (seq_count - 1) == 0 and seq_count > PAIR
-    return powers and layers == 4 and tok % 16 == 0 and block % (128 * chunks) == 0 and features % (512 * 12) == 0
+    if block % (128 * chunks) or heads * (128 + EXTRA_ROWS) % (block // (128 * chunks) * tok):
+        return False
+    return powers and layers == 4 and tok % 16 == 0 and features % (512 * 12) == 0
 
 
 def solution(mesh):
@@ -710,7 +717,7 @@
     def per_device(*args):
         residual, out_weight = args[4], args[5]
         features, block = residual.shape[1], out_weight.shape[1]
-        if fits(mesh, residual.shape[0], features, block, chunks):
+        if fits(mesh, residual.shape[0], features, block, chunks, args[3].shape[0]):
             return tiled(*args, chunks=chunks, returns=cuts(features // 12, [2, 4, 4, 2]))
         return general(*args)
 

time: 250 us -> 250 us (level)
  no operation moved by 1% of the time
where the time goes in v5:
time: 250 us
  waiting for transfers between devices  107 us (43%)
  starting transfers between devices  68.3 us (27%)
  Pallas kernels  52 us (21%)
  local copies, waits for them, and re-layouts  14.8 us (6%)
  other arithmetic  7.5 us (3%)
    ppermute x30, waiting for transfers between devices, swap_columns(): lax.ppermute(array, 'seq', [(i, i ^ PAIR * distance) for i in range(count)])  55.1 us
    ppermute x19, waiting for transfers between devices, swap_layers(): return lax.ppermute(array, 'mp', [(i, i ^ distance) for i in range(count)])  43.9 us
    ppermute x30, starting transfers between devices, swap_columns(): lax.ppermute(array, 'seq', [(i, i ^ PAIR * distance) for i in range(count)])  37.2 us
    pallas_call x3, Pallas kernels, gate_up(): pl.pallas_call(functools.partial(expert_kernel, seq_count, blocks, first,...  24.6 us
    ppermute x19, starting transfers between devices, swap_layers(): return lax.ppermute(array, 'mp', [(i, i ^ distance) for i in range(count)])  23.6 us
    unnamed x59, local copies, waits for them, and re-layouts  12 us
    pallas_call x4, Pallas kernels, down(): pl.pallas_call(down_kernel, grid=(out_width // tile,), out_shape=(jax.Sha...  11.5 us
    ppermute x37, waiting for transfers between devices, swap_cores(): return lax.ppermute(array, 'seq', [(i, i ^ 1) for i in range(count)])  7.58 us
  transfers between devices with their start and end apart: 86, of which 42 were waited for; matrix products, arithmetic and copies ran while one was open for 3% of the time, Pallas kernels for 18%

profile of v5, /device:TPU:0, one launch (start us, length us, event | category | flops | bytes accessed | tf_op | source)
XLA Modules:
  0.0 250.0 jit_solution(7230842767763359980)
XLA Ops:
  6.0 4.0 %collective-permute-start.4 = (bf16[960,128]{1,0:T(8,128)(2,1)S(1)}, bf16[960,128]{1,0:T(8,128)(2,1)S(1)}, u32[]{:S(2)}, u32[]{:S(2)}) collective-permute-start(bf16[960,128]{1,0:T(8,128)(2,1)S(1)} %get-tuple-element.123), channel_id=1, source_target_pairs={{0,24},{4,28},{8,16},{12,20},{16,8},{20,12},{24,0},{28,4},{1,25},{... | collective-permute-start | bytes 737288 | tf_op jit(solution)/shard_map/ppermute | solution.py:34
  12.7 2.7 %collective-permute-start = (bf16[16,32]{1,0:T(8,128)(2,1)S(1)}, bf16[16,32]{1,0:T(8,128)(2,1)S(1)}, u32[]{:S(2)}, u32[]{:S(2)}) collective-permute-start(bf16[16,32]{1,0:T(8,128)(2,1)S(1)} %pad.4), channel_id=1, source_target_pairs={{0,2},{1,3},{2,0},{3,1},{4,6},{5,7},{6,4},{7,5},{8,10},{9,11},{10,... | collective-permute-start | bytes 3080 | tf_op jit(solution)/shard_map/ppermute | solution.py:44
  29.2 3.2 %collective-permute-done.9.refs_1_ = bf16[144,512]{1,0:T(8,128)(2,1)S(1)} collective-permute-done((bf16[144,512]{1,0:T(8,128)(2,1)S(1)}, bf16[144,512]{1,0:T(8,128)(2,1)S(1)}, u32[]{:S(2)}, u32[]{:S(2)}) %collective-permute-start.9) | collective-permute-done | bytes 147488 | tf_op jit(solution)/shard_map/ppermute | solution.py:34
  32.9 2.7 %collective-permute-done.11.refs_3_ = bf16[144,512]{1,0:T(8,128)(2,1)S(1)} collective-permute-done((bf16[144,512]{1,0:T(8,128)(2,1)S(1)}, bf16[144,512]{1,0:T(8,128)(2,1)S(1)}, u32[]{:S(2)}, u32[]{:S(2)}) %collective-permute-start.11) | collective-permute-done | bytes 147488 | tf_op jit(solution)/shard_map/ppermute | solution.py:34
  40.2 6.8 %collective-permute-done.16 = bf16[512,256]{1,0:T(8,128)(2,1)S(1)} collective-permute-done((bf16[512,256]{1,0:T(8,128)(2,1)S(1)}, bf16[512,256]{1,0:T(8,128)(2,1)S(1)}, u32[]{:S(2)}, u32[]{:S(2)}) %collective-permute-start.16) | collective-permute-done | bytes 262176 | tf_op jit(solution)/shard_map/ppermute | solution.py:44
  47.1 2.3 collective-permute-start.17
  52.5 8.7 %collective-permute-done.17 = bf16[512,256]{1,0:T(8,128)(2,1)S(1)} collective-permute-done((bf16[512,256]{1,0:T(8,128)(2,1)S(1)}, bf16[512,256]{1,0:T(8,128)(2,1)S(1)}, u32[]{:S(2)}, u32[]{:S(2)}) %collective-permute-start.17) | collective-permute-done | bytes 262176 | tf_op jit(solution)/shard_map/ppermute | solution.py:44
  63.0 2.5 %collective-permute-start.19 = (bf16[512,256]{1,0:T(8,128)(2,1)S(1)}, bf16[512,256]{1,0:T(8,128)(2,1)S(1)}, u32[]{:S(2)}, u32[]{:S(2)}) collective-permute-start(bf16[512,256]{1,0:T(8,128)(2,1)S(1)} %add_convert_fusion.11), channel_id=1, source_target_pairs={{0,2},{1,3},{2,0},{3,1},{4,6},{5,7},{6,4},{7,5},{8,10},{9,11},{10,... | collective-permute-start | bytes 786440 | tf_op jit(solution)/shard_map/ppermute | solution.py:44
  69.1 6.9 %collective-permute-done.21.far_ref = bf16[512,256]{1,0:T(8,128)(2,1)S(1)} collective-permute-done((bf16[512,256]{1,0:T(8,128)(2,1)S(1)}, bf16[512,256]{1,0:T(8,128)(2,1)S(1)}, u32[]{:S(2)}, u32[]{:S(2)}) %collective-permute-start.21) | collective-permute-done | bytes 262176 | tf_op jit(solution)/shard_map/ppermute | solution.py:44
  77.1 2.7 %collective-permute-start.24 = (bf16[768,256]{1,0:T(8,128)(2,1)S(1)}, bf16[768,256]{1,0:T(8,128)(2,1)S(1)}, u32[]{:S(2)}, u32[]{:S(2)}) collective-permute-start(bf16[768,256]{1,0:T(8,128)(2,1)S(1)} %get-tuple-element.140), channel_id=1, source_target_pairs={{0,24},{4,28},{8,16},{12,20},{16,8},{20,12},{24,0},{28,4},{1,25},{... | collective-permute-start | bytes 1179656 | tf_op jit(solution)/shard_map/ppermute | solution.py:34
  81.7 7.4 %collective-permute-done.24.refs_3_ = bf16[768,256]{1,0:T(8,128)(2,1)S(1)} collective-permute-done((bf16[768,256]{1,0:T(8,128)(2,1)S(1)}, bf16[768,256]{1,0:T(8,128)(2,1)S(1)}, u32[]{:S(2)}, u32[]{:S(2)}) %collective-permute-start.24) | collective-permute-done | bytes 393248 | tf_op jit(solution)/shard_map/ppermute | solution.py:34
  90.1 2.8 %collective-permute-done.23.refs_2_ = bf16[768,256]{1,0:T(8,128)(2,1)S(1)} collective-permute-done((bf16[768,256]{1,0:T(8,128)(2,1)S(1)}, bf16[768,256]{1,0:T(8,128)(2,1)S(1)}, u32[]{:S(2)}, u32[]{:S(2)}) %collective-permute-start.23) | collective-permute-done | bytes 393248 | tf_op jit(solution)/shard_map/ppermute | solution.py:34
  94.9 4.3 %collective-permute-done.29 = bf16[512,256]{1,0:T(8,128)(2,1)S(1)} collective-permute-done((bf16[512,256]{1,0:T(8,128)(2,1)S(1)}, bf16[512,256]{1,0:T(8,128)(2,1)S(1)}, u32[]{:S(2)}, u32[]{:S(2)}) %collective-permute-start.29) | collective-permute-done | bytes 262176 | tf_op jit(solution)/shard_map/ppermute | solution.py:44
  99.2 2.4 collective-permute-start.41
  102.8 7.2 %gate_up.3 = (f32[768,1152]{1,0:T(8,128)S(1)}, f32[768,128]{1,0:T(8,128)S(1)}) custom-call(s32[8]{0:T(128)S(1)} %stack.86.place_ref, bf16[768,256]{1,0:T(8,128)(2,1)S(1)} %get-tuple-element.135.refs_0_, bf16[768,256]{1,0:T(8,128)(2,1)S(1)} %collective-permute-done.22.refs_1_, bf16[768,256]{1,0:T(8,128)(2,1)S(1)} %collective-permute-done.23.refs_2_, ...), custom_call_target="tpu_custom_call" | custom-call | bytes 29520000 | tf_op jit(solution)/shard_map/gate_up/pallas_call | solution.py:431
  111.4 4.1 %collective-permute-done.40.refs_2_ = bf16[768,256]{1,0:T(8,128)(2,1)S(1)} collective-permute-done((bf16[768,256]{1,0:T(8,128)(2,1)S(1)}, bf16[768,256]{1,0:T(8,128)(2,1)S(1)}, u32[]{:S(2)}, u32[]{:S(2)}) %collective-permute-start.40) | collective-permute-done | bytes 393248 | tf_op jit(solution)/shard_map/ppermute | solution.py:34
  117.3 2.0 pack.4
  127.7 8.6 %gate_up.4 = (f32[768,1152]{1,0:T(8,128)S(1)}, f32[768,128]{1,0:T(8,128)S(1)}) custom-call(s32[8]{0:T(128)S(1)} %stack.86.place_ref, bf16[768,256]{1,0:T(8,128)(2,1)S(1)} %get-tuple-element.156.refs_0_, bf16[768,256]{1,0:T(8,128)(2,1)S(1)} %collective-permute-done.39.refs_1_, bf16[768,256]{1,0:T(8,128)(2,1)S(1)} %collective-permute-done.40.refs_2_, ...), custom_call_target="tpu_custom_call" | custom-call | bytes 29520000 | tf_op jit(solution)/shard_map/gate_up/pallas_call | solution.py:431
  144.7 2.1 copy-done.3
  146.8 8.9 %gate_up.5.hidden_ref = bf16[768,576]{1,0:T(8,128)(2,1)S(1)} custom-call(s32[8]{0:T(128)S(1)} %stack.86.place_ref, bf16[768,256]{1,0:T(8,128)(2,1)S(1)} %get-tuple-element.166.refs_0_, bf16[768,256]{1,0:T(8,128)(2,1)S(1)} %collective-permute-done.32.refs_1_, bf16[768,256]{1,0:T(8,128)(2,1)S(1)} %collective-permute-done.33.refs_2_, ...), custom_call_target="tpu_custom_call" | custom-call | bytes 29520000 | tf_op jit(solution)/shard_map/gate_up/pallas_call | solution.py:431
  162.5 4.3 %down.5 = (bf16[384,2048]{1,0:T(8,128)(2,1)S(1)}, bf16[96,2048]{1,0:T(8,128)(2,1)S(1)}, bf16[96,2048]{1,0:T(8,128)(2,1)S(1)}, bf16[96,2048]{1,0:T(8,128)(2,1)S(1)}, bf16[96,2048]{1,0:T(8,128)(2,1)S(1)}) custom-call(bf16[768,576]{1,0:T(8,128)(2,1)S(1)} %gate_up.5.hidden_ref, bf16[576,6144]{1,0:T(8,128)(2,1)} %bitcast.34), custom_call_target="tpu_custom_call" | custom-call | bytes 19680000 | tf_op jit(solution)/shard_map/down/pallas_call | solution.py:483
  169.7 5.9 %collective-permute-done.56.refs_3_ = bf16[96,1024]{1,0:T(8,128)(2,1)S(1)} collective-permute-done((bf16[96,1024]{1,0:T(8,128)(2,1)S(1)}, bf16[96,1024]{1,0:T(8,128)(2,1)S(1)}, u32[]{:S(2)}, u32[]{:S(2)}) %collective-permute-start.56) | collective-permute-done | bytes 196640 | tf_op jit(solution)/shard_map/ppermute | solution.py:34
  180.8 4.4 %down.6 = (bf16[384,2048]{1,0:T(8,128)(2,1)S(1)}, bf16[96,2048]{1,0:T(8,128)(2,1)S(1)}, bf16[96,2048]{1,0:T(8,128)(2,1)S(1)}, bf16[96,2048]{1,0:T(8,128)(2,1)S(1)}, bf16[96,2048]{1,0:T(8,128)(2,1)S(1)}) custom-call(bf16[768,576]{1,0:T(8,128)(2,1)S(1)} %gate_up.5.hidden_ref, bf16[576,6144]{1,0:T(8,128)(2,1)} %bitcast.35), custom_call_target="tpu_custom_call" | custom-call | bytes 19680000 | tf_op jit(solution)/shard_map/down/pallas_call | solution.py:483
  185.8 3.6 %collective-permute-done.67.refs_1_ = bf16[96,2048]{1,0:T(8,128)(2,1)S(1)} collective-permute-done((bf16[96,2048]{1,0:T(8,128)(2,1)}, bf16[96,2048]{1,0:T(8,128)(2,1)S(1)}, u32[]{:S(2)}, u32[]{:S(2)}) %collective-permute-start.67) | collective-permute-done | bytes 393248 | tf_op jit(solution)/shard_map/ppermute | solution.py:34
  189.4 8.0 %collective-permute-done.68.refs_2_ = bf16[96,2048]{1,0:T(8,128)(2,1)S(1)} collective-permute-done((bf16[96,2048]{1,0:T(8,128)(2,1)}, bf16[96,2048]{1,0:T(8,128)(2,1)S(1)}, u32[]{:S(2)}, u32[]{:S(2)}) %collective-permute-start.68) | collective-permute-done | bytes 393248 | tf_op jit(solution)/shard_map/ppermute | solution.py:34
  200.8 3.1 %collective-permute-start.78 = (bf16[96,2048]{1,0:T(8,128)(2,1)S(1)}, bf16[96,2048]{1,0:T(8,128)(2,1)S(1)}, u32[]{:S(2)}, u32[]{:S(2)}) collective-permute-start(bf16[96,2048]{1,0:T(8,128)(2,1)S(1)} %get-tuple-element.225), channel_id=1, source_target_pairs={{0,24},{4,28},{8,16},{12,20},{16,8},{20,12},{24,0},{28,4},{1,25},{... | collective-permute-start | bytes 1179656 | tf_op jit(solution)/shard_map/ppermute | solution.py:34
  208.3 3.1 %collective-permute-start.66 = (bf16[32,1024]{1,0:T(8,128)(2,1)S(1)}, bf16[32,1024]{1,0:T(8,128)(2,1)S(1)}, u32[]{:S(2)}, u32[]{:S(2)}) collective-permute-start(bf16[32,1024]{1,0:T(8,128)(2,1)S(1)} %slice.244), channel_id=1, source_target_pairs={{0,2},{1,3},{2,0},{3,1},{4,6},{5,7},{6,4},{7,5},{8,10},{9,11},{10,... | collective-permute-start | bytes 196616 | tf_op jit(solution)/shard_map/ppermute | solution.py:44
  212.6 7.5 %collective-permute-done.77.refs_2_ = bf16[96,2048]{1,0:T(8,128)(2,1)S(1)} collective-permute-done((bf16[96,2048]{1,0:T(8,128)(2,1)S(1)}, bf16[96,2048]{1,0:T(8,128)(2,1)S(1)}, u32[]{:S(2)}, u32[]{:S(2)}) %collective-permute-start.77) | collective-permute-done | bytes 393248 | tf_op jit(solution)/shard_map/ppermute | solution.py:34
  223.5 2.7 %collective-permute-start.75 = (bf16[32,2048]{1,0:T(8,128)(2,1)S(1)}, bf16[32,2048]{1,0:T(8,128)(2,1)S(1)}, u32[]{:S(2)}, u32[]{:S(2)}) collective-permute-start(bf16[32,2048]{1,0:T(8,128)(2,1)S(1)} %slice.242), channel_id=1, source_target_pairs={{0,2},{1,3},{2,0},{3,1},{4,6},{5,7},{6,4},{7,5},{8,10},{9,11},{10,... | collective-permute-start | bytes 393224 | tf_op jit(solution)/shard_map/ppermute | solution.py:44
  231.7 2.9 %collective-permute-done.83.refs_3_ = bf16[96,1024]{1,0:T(8,128)(2,1)S(1)} collective-permute-done((bf16[96,1024]{1,0:T(8,128)(2,1)S(1)}, bf16[96,1024]{1,0:T(8,128)(2,1)S(1)}, u32[]{:S(2)}, u32[]{:S(2)}) %collective-permute-start.83) | collective-permute-done | bytes 196640 | tf_op jit(solution)/shard_map/ppermute | solution.py:34
  238.2 5.3 %collective-permute-done.84 = bf16[64,1024]{1,0:T(8,128)(2,1)S(1)} collective-permute-done((bf16[64,1024]{1,0:T(8,128)(2,1)S(1)}, bf16[64,1024]{1,0:T(8,128)(2,1)S(1)}, u32[]{:S(2)}, u32[]{:S(2)}) %collective-permute-start.84) | collective-permute-done | bytes 131104 | tf_op jit(solution)/shard_map/ppermute | solution.py:44
  243.6 3.9 %collective-permute-done.80 = bf16[32,2048]{1,0:T(8,128)(2,1)S(1)} collective-permute-done((bf16[32,2048]{1,0:T(8,128)(2,1)S(1)}, bf16[32,2048]{1,0:T(8,128)(2,1)S(1)}, u32[]{:S(2)}, u32[]{:S(2)}) %collective-permute-start.80) | collective-permute-done | bytes 131104 | tf_op jit(solution)/shard_map/ppermute | solution.py:44
  (276 shorter events, 102.2 us)
Async XLA Ops:
  6.0 15.0 %collective-permute-start.4 = (bf16[960,128]{1,0:T(8,128)(2,1)S(1)}, bf16[960,128]{1,0:T(8,128)(2,1)S(1)}, u32[]{:S(2)}, u32[]{:S(2)}) collective-permute-start(bf16[960,128]{1,0:T(8,128)(2,1)S(1)} %get-tuple-element.123), channel_id=1, source_target_pairs={{0,24},{4,28},{8,16},{12,20},{16,8},{20,12},{24,0},{28,4},{1,25},{... | collective-permute-start | bytes 737288 | tf_op jit(solution)/shard_map/ppermute | solution.py:34
  47.1 14.2 %collective-permute-start.17 = (bf16[512,256]{1,0:T(8,128)(2,1)S(1)}, bf16[512,256]{1,0:T(8,128)(2,1)S(1)}, u32[]{:S(2)}, u32[]{:S(2)}) collective-permute-start(bf16[512,256]{1,0:T(8,128)(2,1)S(1)} %add_convert_fusion.13), channel_id=1, source_target_pairs={{0,2},{1,3},{2,0},{3,1},{4,6},{5,7},{6,4},{7,5},{8,10},{9,11},{10,... | collective-permute-start | bytes 786440 | tf_op jit(solution)/shard_map/ppermute | solution.py:44
  50.9 12.0 %collective-permute-start.18 = (bf16[512,256]{1,0:T(8,128)(2,1)S(1)}, bf16[512,256]{1,0:T(8,128)(2,1)S(1)}, u32[]{:S(2)}, u32[]{:S(2)}) collective-permute-start(bf16[512,256]{1,0:T(8,128)(2,1)S(1)} %get-tuple-element.129), channel_id=1, source_target_pairs={{0,1},{1,0},{2,3},{3,2},{4,5},{5,4},{6,7},{7,6},{8,9},{9,8},{10,11... | collective-permute-start | bytes 786440 | tf_op jit(solution)/shard_map/ppermute | solution.py:44
  61.4 14.6 %collective-permute-start.21 = (bf16[512,256]{1,0:T(8,128)(2,1)S(1)}, bf16[512,256]{1,0:T(8,128)(2,1)S(1)}, u32[]{:S(2)}, u32[]{:S(2)}) collective-permute-start(bf16[512,256]{1,0:T(8,128)(2,1)S(1)} %add_convert_fusion.12.near_ref), channel_id=1, source_target_pairs={{0,1},{1,0},{2,3},{3,2},{4,5},{5,4},{6,7},{7,6},{8,9},{9,8},{10,11... | collective-permute-start | bytes 786440 | tf_op jit(solution)/shard_map/ppermute | solution.py:44
  63.0 16.8 %collective-permute-start.19 = (bf16[512,256]{1,0:T(8,128)(2,1)S(1)}, bf16[512,256]{1,0:T(8,128)(2,1)S(1)}, u32[]{:S(2)}, u32[]{:S(2)}) collective-permute-start(bf16[512,256]{1,0:T(8,128)(2,1)S(1)} %add_convert_fusion.11), channel_id=1, source_target_pairs={{0,2},{1,3},{2,0},{3,1},{4,6},{5,7},{6,4},{7,5},{8,10},{9,11},{10,... | collective-permute-start | bytes 786440 | tf_op jit(solution)/shard_map/ppermute | solution.py:44
  68.4 13.2 %collective-permute-start.20 = (bf16[512,256]{1,0:T(8,128)(2,1)S(1)}, bf16[512,256]{1,0:T(8,128)(2,1)S(1)}, u32[]{:S(2)}, u32[]{:S(2)}) collective-permute-start(bf16[512,256]{1,0:T(8,128)(2,1)S(1)} %get-tuple-element.132), channel_id=1, source_target_pairs={{0,1},{1,0},{2,3},{3,2},{4,5},{5,4},{6,7},{7,6},{8,9},{9,8},{10,11... | collective-permute-start | bytes 786440 | tf_op jit(solution)/shard_map/ppermute | solution.py:44
  77.1 12.0 %collective-permute-start.24 = (bf16[768,256]{1,0:T(8,128)(2,1)S(1)}, bf16[768,256]{1,0:T(8,128)(2,1)S(1)}, u32[]{:S(2)}, u32[]{:S(2)}) collective-permute-start(bf16[768,256]{1,0:T(8,128)(2,1)S(1)} %get-tuple-element.140), channel_id=1, source_target_pairs={{0,24},{4,28},{8,16},{12,20},{16,8},{20,12},{24,0},{28,4},{1,25},{... | collective-permute-start | bytes 1179656 | tf_op jit(solution)/shard_map/ppermute | solution.py:34
  79.9 13.5 %collective-permute-start.38 = (bf16[512,256]{1,0:T(8,128)(2,1)S(1)}, bf16[512,256]{1,0:T(8,128)(2,1)S(1)}, u32[]{:S(2)}, u32[]{:S(2)}) collective-permute-start(bf16[512,256]{1,0:T(8,128)(2,1)S(1)} %add_convert_fusion.10.near_ref), channel_id=1, source_target_pairs={{0,1},{1,0},{2,3},{3,2},{4,5},{5,4},{6,7},{7,6},{8,9},{9,8},{10,11... | collective-permute-start | bytes 786440 | tf_op jit(solution)/shard_map/ppermute | solution.py:44
  80.0 12.9 %collective-permute-start.23 = (bf16[768,256]{1,0:T(8,128)(2,1)S(1)}, bf16[768,256]{1,0:T(8,128)(2,1)S(1)}, u32[]{:S(2)}, u32[]{:S(2)}) collective-permute-start(bf16[768,256]{1,0:T(8,128)(2,1)S(1)} %get-tuple-element.138), channel_id=1, source_target_pairs={{0,16},{4,20},{8,24},{12,28},{16,0},{20,4},{24,8},{28,12},{1,17},{... | collective-permute-start | bytes 1179656 | tf_op jit(solution)/shard_map/ppermute | solution.py:34
  80.7 12.6 %collective-permute-start.22 = (bf16[768,256]{1,0:T(8,128)(2,1)S(1)}, bf16[768,256]{1,0:T(8,128)(2,1)S(1)}, u32[]{:S(2)}, u32[]{:S(2)}) collective-permute-start(bf16[768,256]{1,0:T(8,128)(2,1)S(1)} %get-tuple-element.136), channel_id=1, source_target_pairs={{0,8},{4,12},{8,0},{12,4},{16,24},{20,28},{24,16},{28,20},{1,9},{5... | collective-permute-start | bytes 1179656 | tf_op jit(solution)/shard_map/ppermute | solution.py:34
  81.6 19.9 %collective-permute-start.25 = (bf16[768,256]{1,0:T(8,128)(2,1)S(1)}, bf16[768,256]{1,0:T(8,128)(2,1)S(1)}, u32[]{:S(2)}, u32[]{:S(2)}) collective-permute-start(bf16[768,256]{1,0:T(8,128)(2,1)S(1)} %get-tuple-element.135.refs_0_), channel_id=1, source_target_pairs={{0,4},{4,0},{8,12},{12,8},{16,20},{20,16},{24,28},{28,24},{1,5},{5... | collective-permute-start | bytes 1179656 | tf_op jit(solution)/shard_map/ppermute | solution.py:39
  89.1 10.1 %collective-permute-start.29 = (bf16[512,256]{1,0:T(8,128)(2,1)S(1)}, bf16[512,256]{1,0:T(8,128)(2,1)S(1)}, u32[]{:S(2)}, u32[]{:S(2)}) collective-permute-start(bf16[512,256]{1,0:T(8,128)(2,1)S(1)} %add_convert_fusion.9), channel_id=1, source_target_pairs={{0,2},{1,3},{2,0},{3,1},{4,6},{5,7},{6,4},{7,5},{8,10},{9,11},{10,... | collective-permute-start | bytes 786440 | tf_op jit(solution)/shard_map/ppermute | solution.py:44
  99.2 12.3 %collective-permute-start.41 = (bf16[768,256]{1,0:T(8,128)(2,1)S(1)}, bf16[768,256]{1,0:T(8,128)(2,1)S(1)}, u32[]{:S(2)}, u32[]{:S(2)}) collective-permute-start(bf16[768,256]{1,0:T(8,128)(2,1)S(1)} %get-tuple-element.161), channel_id=1, source_target_pairs={{0,24},{4,28},{8,16},{12,20},{16,8},{20,12},{24,0},{28,4},{1,25},{... | collective-permute-start | bytes 1179656 | tf_op jit(solution)/shard_map/ppermute | solution.py:34
  101.5 14.0 %collective-permute-start.40 = (bf16[768,256]{1,0:T(8,128)(2,1)S(1)}, bf16[768,256]{1,0:T(8,128)(2,1)S(1)}, u32[]{:S(2)}, u32[]{:S(2)}) collective-permute-start(bf16[768,256]{1,0:T(8,128)(2,1)S(1)} %get-tuple-element.159), channel_id=1, source_target_pairs={{0,16},{4,20},{8,24},{12,28},{16,0},{20,4},{24,8},{28,12},{1,17},{... | collective-permute-start | bytes 1179656 | tf_op jit(solution)/shard_map/ppermute | solution.py:34
  102.2 14.6 %collective-permute-start.39 = (bf16[768,256]{1,0:T(8,128)(2,1)S(1)}, bf16[768,256]{1,0:T(8,128)(2,1)S(1)}, u32[]{:S(2)}, u32[]{:S(2)}) collective-permute-start(bf16[768,256]{1,0:T(8,128)(2,1)S(1)} %get-tuple-element.157), channel_id=1, source_target_pairs={{0,8},{4,12},{8,0},{12,4},{16,24},{20,28},{24,16},{28,20},{1,9},{5... | collective-permute-start | bytes 1179656 | tf_op jit(solution)/shard_map/ppermute | solution.py:34
  119.4 18.7 %collective-permute-start.34 = (bf16[768,256]{1,0:T(8,128)(2,1)}, bf16[768,256]{1,0:T(8,128)(2,1)S(1)}, u32[]{:S(2)}, u32[]{:S(2)}) collective-permute-start(bf16[768,256]{1,0:T(8,128)(2,1)} %get-tuple-element.148), channel_id=1, source_target_pairs={{0,24},{4,28},{8,16},{12,20},{16,8},{20,12},{24,0},{28,4},{1,25},{... | collective-permute-start | bytes 1179656 | tf_op jit(solution)/shard_map/ppermute | solution.py:34
  121.9 18.0 %collective-permute-start.33 = (bf16[768,256]{1,0:T(8,128)(2,1)}, bf16[768,256]{1,0:T(8,128)(2,1)S(1)}, u32[]{:S(2)}, u32[]{:S(2)}) collective-permute-start(bf16[768,256]{1,0:T(8,128)(2,1)} %get-tuple-element.147), channel_id=1, source_target_pairs={{0,16},{4,20},{8,24},{12,28},{16,0},{20,4},{24,8},{28,12},{1,17},{... | collective-permute-start | bytes 1179656 | tf_op jit(solution)/shard_map/ppermute | solution.py:34
  124.1 16.0 %collective-permute-start.32 = (bf16[768,256]{1,0:T(8,128)(2,1)}, bf16[768,256]{1,0:T(8,128)(2,1)S(1)}, u32[]{:S(2)}, u32[]{:S(2)}) collective-permute-start(bf16[768,256]{1,0:T(8,128)(2,1)} %get-tuple-element.146), channel_id=1, source_target_pairs={{0,8},{4,12},{8,0},{12,4},{16,24},{20,28},{24,16},{28,20},{1,9},{5... | collective-permute-start | bytes 1179656 | tf_op jit(solution)/shard_map/ppermute | solution.py:34
  141.2 14.5 %collective-permute-start.37 = (bf16[32,1536]{1,0:T(8,128)(2,1)S(1)}, bf16[32,1536]{1,0:T(8,128)(2,1)S(1)}, u32[]{:S(2)}, u32[]{:S(2)}) collective-permute-start(bf16[32,1536]{1,0:T(8,128)(2,1)S(1)} %get-tuple-element.152), channel_id=1, source_target_pairs={{0,24},{4,28},{8,16},{12,20},{16,8},{20,12},{24,0},{28,4},{1,25},{... | collective-permute-start | bytes 294920 | tf_op jit(solution)/shard_map/ppermute | solution.py:34
  143.2 12.6 %collective-permute-start.36 = (bf16[32,1536]{1,0:T(8,128)(2,1)S(1)}, bf16[32,1536]{1,0:T(8,128)(2,1)S(1)}, u32[]{:S(2)}, u32[]{:S(2)}) collective-permute-start(bf16[32,1536]{1,0:T(8,128)(2,1)S(1)} %get-tuple-element.151), channel_id=1, source_target_pairs={{0,16},{4,20},{8,24},{12,28},{16,0},{20,4},{24,8},{28,12},{1,17},{... | collective-permute-start | bytes 294920 | tf_op jit(solution)/shard_map/ppermute | solution.py:34
  144.5 11.3 %collective-permute-start.35 = (bf16[32,1536]{1,0:T(8,128)(2,1)S(1)}, bf16[32,1536]{1,0:T(8,128)(2,1)S(1)}, u32[]{:S(2)}, u32[]{:S(2)}) collective-permute-start(bf16[32,1536]{1,0:T(8,128)(2,1)S(1)} %get-tuple-element.150), channel_id=1, source_target_pairs={{0,8},{4,12},{8,0},{12,4},{16,24},{20,28},{24,16},{28,20},{1,9},{5... | collective-permute-start | bytes 294920 | tf_op jit(solution)/shard_map/ppermute | solution.py:34
  177.2 12.3 %collective-permute-start.67 = (bf16[96,2048]{1,0:T(8,128)(2,1)}, bf16[96,2048]{1,0:T(8,128)(2,1)S(1)}, u32[]{:S(2)}, u32[]{:S(2)}) collective-permute-start(bf16[96,2048]{1,0:T(8,128)(2,1)} %get-tuple-element.231), channel_id=1, source_target_pairs={{0,8},{4,12},{8,0},{12,4},{16,24},{20,28},{24,16},{28,20},{1,9},{5... | collective-permute-start | bytes 1179656 | tf_op jit(solution)/shard_map/ppermute | solution.py:34
  178.5 18.9 %collective-permute-start.68 = (bf16[96,2048]{1,0:T(8,128)(2,1)}, bf16[96,2048]{1,0:T(8,128)(2,1)S(1)}, u32[]{:S(2)}, u32[]{:S(2)}) collective-permute-start(bf16[96,2048]{1,0:T(8,128)(2,1)} %get-tuple-element.230), channel_id=1, source_target_pairs={{0,16},{4,20},{8,24},{12,28},{16,0},{20,4},{24,8},{28,12},{1,17},{... | collective-permute-start | bytes 1179656 | tf_op jit(solution)/shard_map/ppermute | solution.py:34
  179.3 18.2 %collective-permute-start.69 = (bf16[96,2048]{1,0:T(8,128)(2,1)S(1)}, bf16[96,2048]{1,0:T(8,128)(2,1)S(1)}, u32[]{:S(2)}, u32[]{:S(2)}) collective-permute-start(bf16[96,2048]{1,0:T(8,128)(2,1)S(1)} %get-tuple-element.229), channel_id=1, source_target_pairs={{0,24},{4,28},{8,16},{12,20},{16,8},{20,12},{24,0},{28,4},{1,25},{... | collective-permute-start | bytes 1179656 | tf_op jit(solution)/shard_map/ppermute | solution.py:34
  185.2 12.3 %collective-permute-start.61 = (bf16[96,2048]{1,0:T(8,128)(2,1)S(1)}, bf16[96,2048]{1,0:T(8,128)(2,1)S(1)}, u32[]{:S(2)}, u32[]{:S(2)}) collective-permute-start(bf16[96,2048]{1,0:T(8,128)(2,1)S(1)} %get-tuple-element.184), channel_id=1, source_target_pairs={{0,4},{4,0},{8,12},{12,8},{16,20},{20,16},{24,28},{28,24},{1,5},{5... | collective-permute-start | bytes 1179656 | tf_op jit(solution)/shard_map/ppermute | solution.py:39
  185.3 12.3 %collective-permute-start.62 = (bf16[96,2048]{1,0:T(8,128)(2,1)S(1)}, bf16[96,2048]{1,0:T(8,128)(2,1)S(1)}, u32[]{:S(2)}, u32[]{:S(2)}) collective-permute-start(bf16[96,2048]{1,0:T(8,128)(2,1)S(1)} %get-tuple-element.185), channel_id=1, source_target_pairs={{0,4},{4,0},{8,12},{12,8},{16,20},{20,16},{24,28},{28,24},{1,5},{5... | collective-permute-start | bytes 1179656 | tf_op jit(solution)/shard_map/ppermute | solution.py:39
  200.4 12.2 %collective-permute-start.76 = (bf16[96,2048]{1,0:T(8,128)(2,1)S(1)}, bf16[96,2048]{1,0:T(8,128)(2,1)S(1)}, u32[]{:S(2)}, u32[]{:S(2)}) collective-permute-start(bf16[96,2048]{1,0:T(8,128)(2,1)S(1)} %get-tuple-element.227), channel_id=1, source_target_pairs={{0,8},{4,12},{8,0},{12,4},{16,24},{20,28},{24,16},{28,20},{1,9},{5... | collective-permute-start | bytes 1179656 | tf_op jit(solution)/shard_map/ppermute | solution.py:34
  200.8 19.4 %collective-permute-start.77 = (bf16[96,2048]{1,0:T(8,128)(2,1)S(1)}, bf16[96,2048]{1,0:T(8,128)(2,1)S(1)}, u32[]{:S(2)}, u32[]{:S(2)}) collective-permute-start(bf16[96,2048]{1,0:T(8,128)(2,1)S(1)} %get-tuple-element.226), channel_id=1, source_target_pairs={{0,16},{4,20},{8,24},{12,28},{16,0},{20,4},{24,8},{28,12},{1,17},{... | collective-permute-start | bytes 1179656 | tf_op jit(solution)/shard_map/ppermute | solution.py:34
  200.8 19.3 %collective-permute-start.78 = (bf16[96,2048]{1,0:T(8,128)(2,1)S(1)}, bf16[96,2048]{1,0:T(8,128)(2,1)S(1)}, u32[]{:S(2)}, u32[]{:S(2)}) collective-permute-start(bf16[96,2048]{1,0:T(8,128)(2,1)S(1)} %get-tuple-element.225), channel_id=1, source_target_pairs={{0,24},{4,28},{8,16},{12,20},{16,8},{20,12},{24,0},{28,4},{1,25},{... | collective-permute-start | bytes 1179656 | tf_op jit(solution)/shard_map/ppermute | solution.py:34
  208.3 15.1 %collective-permute-start.66 = (bf16[32,1024]{1,0:T(8,128)(2,1)S(1)}, bf16[32,1024]{1,0:T(8,128)(2,1)S(1)}, u32[]{:S(2)}, u32[]{:S(2)}) collective-permute-start(bf16[32,1024]{1,0:T(8,128)(2,1)S(1)} %slice.244), channel_id=1, source_target_pairs={{0,2},{1,3},{2,0},{3,1},{4,6},{5,7},{6,4},{7,5},{8,10},{9,11},{10,... | collective-permute-start | bytes 196616 | tf_op jit(solution)/shard_map/ppermute | solution.py:44
  212.5 10.9 %collective-permute-start.74 = (bf16[64,2048]{1,0:T(8,128)(2,1)S(1)}, bf16[64,2048]{1,0:T(8,128)(2,1)S(1)}, u32[]{:S(2)}, u32[]{:S(2)}) collective-permute-start(bf16[64,2048]{1,0:T(8,128)(2,1)S(1)} %get-tuple-element.206), channel_id=1, source_target_pairs={{0,1},{1,0},{2,3},{3,2},{4,5},{5,4},{6,7},{7,6},{8,9},{9,8},{10,11... | collective-permute-start | bytes 786440 | tf_op jit(solution)/shard_map/ppermute | solution.py:44
  221.6 10.1 %collective-permute-start.79 = (bf16[64,2048]{1,0:T(8,128)(2,1)S(1)}, bf16[64,2048]{1,0:T(8,128)(2,1)S(1)}, u32[]{:S(2)}, u32[]{:S(2)}) collective-permute-start(bf16[64,2048]{1,0:T(8,128)(2,1)S(1)} %get-tuple-element.215), channel_id=1, source_target_pairs={{0,1},{1,0},{2,3},{3,2},{4,5},{5,4},{6,7},{7,6},{8,9},{9,8},{10,11... | collective-permute-start | bytes 786440 | tf_op jit(solution)/shard_map/ppermute | solution.py:44
  (82 other events, 551.2 us)
